TPU v7x, 32 devices: a whole 2x2x4 slice. The times are simulated.
32 devices in a mesh: dp: 8 (over z, y), vocab: 4 (over x, core).
Axes of the slice: x: 2, y: 2, z: 4, core: 2. Of those that a mesh axis runs over, the one named last changes fastest.
Arguments:
- token_ids: int32 [8, 1024], P('dp'), may hold values from 0 to 30521
- timesteps: int32 [8], P('dp'), may hold values from 0 to 1999, as said below
- pad_mask: int32 [8, 1024], P('dp'), may hold values from 0 to 1, as said below
- noise_draw: bfloat16 [8, 1024, 128], P('dp', 'vocab'), may hold values from -6 to 6
- owners: int32 [9], replicated, may hold values from 0 to 7, as said below
- emb_table: float32 [30528, 128], P('vocab', 'dp')
- table_first_moment: float32 [30528, 128], P('vocab', 'dp'), may hold values from -0.0068359375 to 0.0068359375
- table_second_moment: float32 [30528, 128], P('vocab', 'dp'), may hold values from 1.2207032e-07 to 4.882813e-07
- mat_slots: float32 [768, 24576], P('vocab', 'dp'), as said below
- slot_first: float32 [768, 24576], P('vocab', 'dp'), as said below
- slot_second: float32 [768, 24576], P('vocab', 'dp'), as said below
- vec_params: float32 [7680], replicated
- vec_first: float32 [7680], P('vocab'), may hold values from -0.01953125 to 0.01953125
- vec_second: float32 [7680], P('vocab'), may hold values from 1.0986328e-06 to 4.394531e-06
Outputs:
- loss_pair: float32 [2], replicated
- emb_norm: float32 [], replicated
- new_table: float32 [30528, 128], P('vocab', 'dp')
- table_first_new: float32 [30528, 128], P('vocab', 'dp')
- table_second_new: float32 [30528, 128], P('vocab', 'dp')
- new_slots: float32 [768, 24576], P('vocab', 'dp')
- slot_first_new: float32 [768, 24576], P('vocab', 'dp')
- slot_second_new: float32 [768, 24576], P('vocab', 'dp')
- new_vecs: float32 [7680], P('vocab')
- vec_first_new: float32 [7680], P('vocab')
- vec_second_new: float32 [7680], P('vocab')
Inputs may be any that keep to these rules, and one draw needn't show every extreme that they name: Skewed toward small timesteps; some sequence has timestep 0 and some other 1999. `pad_mask`: each row's ones are a suffix of at least 341 positions; some row has no zero. `owners`: the rows of the matrices that one data index owns, in list order, number at most 3072, and some index owns exactly 3072. `mat_slots`: columns of a slot that no listed matrix covers are zero. `slot_first`: columns of a slot that no listed matrix covers are zero. `slot_second`: columns of a slot that no listed matrix covers are zero; the others are positive.
All inputs are finite; a program needn't handle non-finite values.
Results may differ from a plain program's by a relative error of at most 0.0009.
The roundings to bfloat16 on the way count: a program that leaves them out, or rounds other values in their place, can miss the bound.
Values may be sent and summed in bfloat16 or wider, within the bound.
A program may use at most 256 MiB of HBM per device.

v0:
```python
import math

import jax
import jax.numpy as jnp
from jax import lax
from jax.sharding import PartitionSpec as P

D = 768
HEADS = 12
HDIM = 64
FF = 3072
EMBED_WIDTH = 128
LAYERS = 1
DIFF = 2000
STEP = 10
CAP = 3072


beta_one = 0.9
beta_two = 0.999
learn_rate = 0.02
weight_decay = 0.01
eps_adam = 1e-08
eps_norm = 1e-05


def broadcast(value, axis, source):
    kept = jnp.where(lax.axis_index(axis) == source, value, 0).astype(value.dtype)
    return lax.psum(kept, axis)


def merged(value, axis, join):
    pieces = jax.tree.map(lambda part: lax.all_gather(part, axis), value)
    head = jax.tree.map(lambda part: part[0], pieces)
    tail = jax.tree.map(lambda part: part[1:], pieces)
    so_far, _ = lax.scan(lambda so_far, share: (join(so_far, share), None), head, tail)
    return so_far


def matmul_nn(left, right):
    return jnp.dot(left, right, preferred_element_type=jnp.float32)


def matmul_tn(left, right):
    return lax.dot_general(
        left, right, (((0,), (0,)), ((), ())), preferred_element_type=jnp.float32
    )


def matmul_nt(left, right):
    return lax.dot_general(
        left, right, (((1,), (1,)), ((), ())), preferred_element_type=jnp.float32
    )


def matrix_rows():
    return [D, D, D, D, FF, FF] * LAYERS + [EMBED_WIDTH, EMBED_WIDTH, EMBED_WIDTH]


def slot_starts(owners):
    counts = jnp.array(matrix_rows(), jnp.int32)
    mat_total = counts.shape[0]
    same_owner = (owners[:, None] == owners[None, :]).astype(jnp.int32)
    earlier_mask = jnp.tril(jnp.ones((mat_total, mat_total), jnp.int32), -1)
    return owners * CAP + jnp.sum(same_owner * earlier_mask * counts[None, :], 1)


def waves(places, width):
    half_width = width // 2
    frequency = jnp.exp(-math.log(10000.0) * jnp.arange(half_width, dtype=jnp.float32) / half_width)
    angles = places[:, None] * frequency[None, :]
    return jnp.concatenate([jnp.sin(angles), jnp.cos(angles)], 1)


def norm_parts(value_entries):
    center = value_entries - jnp.mean(value_entries, -1, keepdims=True)
    scale_inv = lax.rsqrt(jnp.mean(center * center, -1, keepdims=True) + eps_norm)
    return (center * scale_inv, scale_inv)


def norm_back(normal_part, scale_inv, gain_vec, grad_out):
    scaled = grad_out * gain_vec
    inner = (
        scaled
        - jnp.mean(scaled, -1, keepdims=True)
        - normal_part * jnp.mean(scaled * normal_part, -1, keepdims=True)
    )
    return (inner * scale_inv, jnp.sum(grad_out * normal_part, 0), jnp.sum(grad_out, 0))


def block_scores(query_blk, keys_all, keep_keys, score_scale):
    scores = (
        jnp.einsum("qhd,khd->hqk", query_blk, keys_all, preferred_element_type=jnp.float32)
        * score_scale
    )
    return jnp.where(keep_keys[None, None, :], scores, -1000000000.0)


def attention(queries, keys_all, values_all, keep_keys, score_scale):
    tokens = queries.shape[0]
    width = min(512, tokens)
    query_blocks = queries.reshape(tokens // width, width, HEADS, HDIM)

    def one_block(query_blk):
        scores = block_scores(query_blk, keys_all, keep_keys, score_scale)
        row_max = jnp.max(scores, -1, keepdims=True)
        expo = jnp.exp(scores - row_max)
        exp_total = jnp.sum(expo, -1, keepdims=True)
        probabilities = (expo / exp_total).astype(jnp.bfloat16)
        mixed_out = jnp.einsum(
            "hqk,khd->qhd", probabilities, values_all, preferred_element_type=jnp.float32
        )
        return (mixed_out, (row_max + jnp.log(exp_total))[..., 0])

    mixed_out, log_total = lax.map(one_block, query_blocks)
    return (mixed_out.reshape(tokens, HEADS, HDIM), log_total)


def attention_back(queries, keys_all, values_all, keep_keys, log_total, grad_mixed, score_scale):
    tokens = queries.shape[0]
    width = min(512, tokens)
    query_blocks = queries.reshape(tokens // width, width, HEADS, HDIM)
    grad_blocks = grad_mixed.reshape(tokens // width, width, HEADS, HDIM)

    def one_block(carry_sums, block_data):
        query_blk, total_blk, grad_blk = block_data
        scores = block_scores(query_blk, keys_all, keep_keys, score_scale)
        probabilities = jnp.exp(scores - total_blk[..., None])
        grad_probs = jnp.einsum(
            "qhd,khd->hqk", grad_blk, values_all, preferred_element_type=jnp.float32
        )
        inner_sum = jnp.sum(probabilities * grad_probs, -1, keepdims=True)
        grad_scores = (probabilities * (grad_probs - inner_sum)).astype(jnp.bfloat16)
        grad_query = (
            jnp.einsum("hqk,khd->qhd", grad_scores, keys_all, preferred_element_type=jnp.float32)
            * score_scale
        )
        grad_key = (
            jnp.einsum("hqk,qhd->khd", grad_scores, query_blk, preferred_element_type=jnp.float32)
            * score_scale
        )
        grad_value = jnp.einsum(
            "hqk,qhd->khd",
            probabilities.astype(jnp.bfloat16),
            grad_blk,
            preferred_element_type=jnp.float32,
        )
        return ((carry_sums[0] + grad_key, carry_sums[1] + grad_value), grad_query)

    zero_keys = jnp.zeros(keys_all.shape, jnp.float32)
    grad_kv, grad_queries = lax.scan(
        one_block, (zero_keys, zero_keys), (query_blocks, log_total, grad_blocks)
    )
    return (grad_queries.reshape(tokens, D), grad_kv[0].reshape(-1, D), grad_kv[1].reshape(-1, D))


def send_matrix(piece_cols, root):
    return broadcast(piece_cols, "dp", root)


def fetch_keys(key_rows, value_rows):
    return (
        lax.all_gather(key_rows, "vocab", axis=0, tiled=True),
        lax.all_gather(value_rows, "vocab", axis=0, tiled=True),
    )


def layer_forward(hidden, weights, vec_layer, keep_keys, score_scale):
    w_query, w_key, w_value, w_out, w_up, w_down = weights
    tokens = hidden.shape[0]
    norm_one, inv_one = norm_parts(hidden)
    normed = (norm_one * vec_layer[0:D] + vec_layer[D : 2 * D]).astype(jnp.bfloat16)
    queries = matmul_nn(normed, w_query).astype(jnp.bfloat16)
    key_rows = matmul_nn(normed, w_key).astype(jnp.bfloat16)
    value_rows = matmul_nn(normed, w_value).astype(jnp.bfloat16)
    keys_all, values_all = fetch_keys(key_rows, value_rows)
    keys_all = keys_all.reshape(-1, HEADS, HDIM)
    values_all = values_all.reshape(-1, HEADS, HDIM)
    mixed_out, log_total = attention(
        queries.reshape(tokens, HEADS, HDIM), keys_all, values_all, keep_keys, score_scale
    )
    mixed_low = mixed_out.reshape(tokens, D).astype(jnp.bfloat16)
    middle = hidden + matmul_nn(mixed_low, w_out)
    norm_two, inv_two = norm_parts(middle)
    normed_two = (norm_two * vec_layer[2 * D : 3 * D] + vec_layer[3 * D : 4 * D]).astype(
        jnp.bfloat16
    )
    up_proj = matmul_nt(normed_two, w_up) + vec_layer[4 * D :]
    active = jax.nn.gelu(up_proj).astype(jnp.bfloat16)
    out_rows = middle + matmul_nn(active, w_down)
    kept_vals = (
        norm_one,
        inv_one,
        normed,
        queries,
        key_rows,
        value_rows,
        keys_all,
        values_all,
        log_total,
        mixed_low,
        norm_two,
        inv_two,
        normed_two,
        up_proj,
        active,
    )
    return (out_rows, kept_vals)


def layer_backward(grad_out, kept_vals, weights, vec_layer, keep_keys, score_scale):
    w_query, w_key, w_value, w_out, w_up, w_down = weights
    (
        norm_one,
        inv_one,
        normed,
        queries,
        key_rows,
        value_rows,
        keys_all,
        values_all,
        log_total,
        mixed_low,
        norm_two,
        inv_two,
        normed_two,
        up_proj,
        active,
    ) = kept_vals
    tokens = grad_out.shape[0]
    grad_low = grad_out.astype(jnp.bfloat16)
    grad_down = matmul_tn(active, grad_low)
    grad_active = matmul_nt(grad_low, w_down)
    grad_up_proj = jax.vjp(jax.nn.gelu, up_proj)[1](grad_active)[0].astype(jnp.bfloat16)
    grad_bias = jnp.sum(grad_up_proj.astype(jnp.float32), 0)
    grad_up = matmul_tn(grad_up_proj, normed_two)
    grad_normed_two = matmul_nn(grad_up_proj, w_up)
    grad_part, grad_gain_two, grad_shift_two = norm_back(
        norm_two, inv_two, vec_layer[2 * D : 3 * D], grad_normed_two
    )
    grad_middle = grad_out + grad_part
    grad_attn = grad_middle.astype(jnp.bfloat16)
    grad_out_w = matmul_tn(mixed_low, grad_attn)
    grad_mixed = matmul_nt(grad_attn, w_out).astype(jnp.bfloat16).reshape(tokens, HEADS, HDIM)
    grad_queries, grad_keys_all, grad_values_all = attention_back(
        queries.reshape(tokens, HEADS, HDIM),
        keys_all,
        values_all,
        keep_keys,
        log_total,
        grad_mixed,
        score_scale,
    )
    grad_key_rows, grad_value_rows = (
        lax.psum_scatter(
            grad_keys_all.astype(jnp.bfloat16), "vocab", scatter_dimension=0, tiled=True
        ).astype(jnp.float32),
        lax.psum_scatter(
            grad_values_all.astype(jnp.bfloat16), "vocab", scatter_dimension=0, tiled=True
        ).astype(jnp.float32),
    )
    grad_q_low = grad_queries.astype(jnp.bfloat16)
    grad_k_low = grad_key_rows.astype(jnp.bfloat16)
    grad_v_low = grad_value_rows.astype(jnp.bfloat16)
    grad_wq = matmul_tn(normed, grad_q_low)
    grad_wk = matmul_tn(normed, grad_k_low)
    grad_wv = matmul_tn(normed, grad_v_low)
    grad_normed = (
        matmul_nt(grad_q_low, w_query)
        + matmul_nt(grad_k_low, w_key)
        + matmul_nt(grad_v_low, w_value)
    )
    grad_part_one, grad_gain_one, grad_shift_one = norm_back(
        norm_one, inv_one, vec_layer[0:D], grad_normed
    )
    grad_hidden = grad_middle + grad_part_one
    grad_mats = [grad_wq, grad_wk, grad_wv, grad_out_w, grad_up, grad_down]
    grad_vec = jnp.concatenate(
        [grad_gain_one, grad_shift_one, grad_gain_two, grad_shift_two, grad_bias]
    )
    return (grad_hidden, grad_mats, grad_vec)


def merge_stats(first_part, second_part):
    peak_val = jnp.maximum(first_part[0], second_part[0])
    exp_total = first_part[1] * jnp.exp(first_part[0] - peak_val) + second_part[1] * jnp.exp(
        second_part[0] - peak_val
    )
    return (peak_val, exp_total, first_part[2] + second_part[2])


def adamw(weight, gradient, moment_one, moment_two):
    moment_one = beta_one * moment_one + (1.0 - beta_one) * gradient
    moment_two = beta_two * moment_two + (1.0 - beta_two) * gradient * gradient
    fix_one = 1.0 - beta_one**STEP
    fix_two = 1.0 - beta_two**STEP
    update_dir = moment_one / fix_one / (jnp.sqrt(moment_two / fix_two) + eps_adam)
    return (weight - learn_rate * (update_dir + weight_decay * weight), moment_one, moment_two)


def per_device(
    token_ids,
    timesteps,
    pad_mask,
    noise_draw,
    owners,
    emb_table,
    table_first_moment,
    table_second_moment,
    mat_slots,
    slot_first,
    slot_second,
    vec_params,
    vec_first,
    vec_second,
):
    vocab_count = lax.axis_size("vocab")
    vocab_pos = lax.axis_index("vocab")
    data_pos = lax.axis_index("dp")
    seq_len = token_ids.shape[1]
    tokens = seq_len // vocab_count
    vocab_rows = emb_table.shape[0]
    score_scale = HDIM ** (-0.5)
    table_low = lax.all_gather(emb_table.astype(jnp.bfloat16), "dp", axis=1, tiled=True)
    row_counts = matrix_rows()
    local_start = slot_starts(owners) - owners * CAP
    sent_pieces = [
        send_matrix(
            lax.dynamic_slice_in_dim(
                mat_slots, local_start[mat_idx], row_counts[mat_idx], 1
            ).astype(jnp.bfloat16),
            owners[mat_idx],
        )
        for mat_idx in range(len(row_counts))
    ]
    canon = jnp.concatenate(sent_pieces, 1)
    weights = lax.all_gather(canon, "vocab", axis=0, tiled=True).T
    layer_rows = 4 * D + 2 * FF
    vec_rows = 4 * D + FF
    tail_at = LAYERS * layer_rows

    def layer_weights(layer_idx):
        begin_row = layer_idx * layer_rows
        cuts = [
            begin_row,
            begin_row + D,
            begin_row + 2 * D,
            begin_row + 3 * D,
            begin_row + 4 * D,
            begin_row + 4 * D + FF,
            begin_row + layer_rows,
        ]
        return [weights[cuts[cut_idx] : cuts[cut_idx + 1]] for cut_idx in range(6)]

    w_input = weights[tail_at : tail_at + 2 * EMBED_WIDTH]
    w_final = weights[tail_at + 2 * EMBED_WIDTH : tail_at + 3 * EMBED_WIDTH]
    seq_ids = token_ids[0]
    seq_mask = pad_mask[0].astype(jnp.float32)
    keep_keys = pad_mask[0] > 0
    local_row = seq_ids - vocab_pos * vocab_rows
    valid_row = (local_row >= 0) & (local_row < vocab_rows)
    safe_row = jnp.clip(local_row, 0, vocab_rows - 1)
    found_rows = jnp.where(
        valid_row[:, None], jnp.take(table_low, safe_row, axis=0), jnp.zeros((), jnp.bfloat16)
    )
    arrived = lax.all_to_all(found_rows, "vocab", split_axis=0, concat_axis=0, tiled=True)
    clean_emb = jnp.sum(arrived.reshape(vocab_count, tokens, EMBED_WIDTH).astype(jnp.float32), 0)
    own_first = vocab_pos * tokens
    mask_own = lax.dynamic_slice_in_dim(seq_mask, own_first, tokens)
    own_places = (own_first + jnp.arange(tokens)).astype(jnp.float32)
    step_val = timesteps[0].astype(jnp.float32)
    signal_level = 1.0 - jnp.sqrt(step_val / DIFF + 0.0001)
    noisy_emb = jnp.sqrt(signal_level) * clean_emb + jnp.sqrt(1.0 - signal_level) * noise_draw[
        0
    ].astype(jnp.float32)
    time_feat = jnp.broadcast_to(waves(step_val[None], EMBED_WIDTH), (tokens, EMBED_WIDTH))
    inputs = jnp.concatenate([noisy_emb, time_feat], 1).astype(jnp.bfloat16)
    hidden = matmul_nn(inputs, w_input) + waves(own_places, D)
    layer_idx = 0
    vec_layer = vec_params[layer_idx * vec_rows : (layer_idx + 1) * vec_rows]
    hidden, kept_vals = layer_forward(
        hidden, layer_weights(layer_idx), vec_layer, keep_keys, score_scale
    )
    kept_list = [kept_vals]
    gain_final = vec_params[LAYERS * vec_rows : LAYERS * vec_rows + D]
    shift_final = vec_params[LAYERS * vec_rows + D :]
    norm_final, inv_final = norm_parts(hidden)
    final_norm = (norm_final * gain_final + shift_final).astype(jnp.bfloat16)
    predicted = matmul_nt(final_norm, w_final)
    pred_all = lax.all_gather(predicted.astype(jnp.bfloat16), "vocab", axis=0, tiled=True)
    head_width = min(512, seq_len)
    head_count = seq_len // head_width
    columns = jnp.arange(vocab_rows)
    pred_blocks = pred_all.reshape(head_count, head_width, EMBED_WIDTH)
    row_blocks = local_row.reshape(head_count, head_width)

    def head_stats(block_data):
        pred_blk, rows_blk = block_data
        logits = matmul_nt(pred_blk, table_low)
        row_max = jnp.max(logits, -1)
        exp_total = jnp.sum(jnp.exp(logits - row_max[:, None]), -1)
        target = jnp.sum(jnp.where(columns[None, :] == rows_blk[:, None], logits, 0.0), -1)
        return (row_max, exp_total, target)

    peaks, totals, targets = lax.map(head_stats, (pred_blocks, row_blocks))
    peak_all, total_all, target_all = merged(
        (peaks.reshape(seq_len), totals.reshape(seq_len), targets.reshape(seq_len)),
        "vocab",
        merge_stats,
    )
    log_total = peak_all + jnp.log(total_all)
    lse_own = lax.dynamic_slice_in_dim(log_total, own_first, tokens)
    target_own = lax.dynamic_slice_in_dim(target_all, own_first, tokens)
    pred_error = predicted - clean_emb
    square_own = jnp.sum(mask_own[:, None] * pred_error * pred_error)
    cross_own = jnp.sum(mask_own * (lse_own - target_own))
    norm_own = jnp.sum(mask_own * jnp.sqrt(jnp.sum(clean_emb * clean_emb, -1) + 1e-06))
    count_all, square, cross_sum, norm_total = lax.psum(
        (jnp.sum(mask_own), square_own, cross_own, norm_own), ("dp", "vocab")
    )
    weight_blocks = (seq_mask / count_all).reshape(head_count, head_width)
    lse_blocks = log_total.reshape(head_count, head_width)

    def head_back(grad_table, block_data):
        pred_blk, rows_blk, lse_blk, weight_blk = block_data
        logits = matmul_nt(pred_blk, table_low)
        probabilities = jnp.exp(logits - lse_blk[:, None])
        onehot = (columns[None, :] == rows_blk[:, None]).astype(jnp.float32)
        grad_logits = ((probabilities - onehot) * weight_blk[:, None]).astype(jnp.bfloat16)
        return (grad_table + matmul_tn(grad_logits, pred_blk), matmul_nn(grad_logits, table_low))

    zero_table = jnp.zeros((vocab_rows, EMBED_WIDTH), jnp.float32)
    grad_table_head, grad_pred_blocks = lax.scan(
        head_back, zero_table, (pred_blocks, row_blocks, lse_blocks, weight_blocks)
    )
    grad_pred = lax.psum_scatter(
        grad_pred_blocks.reshape(seq_len, EMBED_WIDTH).astype(jnp.bfloat16),
        "vocab",
        scatter_dimension=0,
        tiled=True,
    ).astype(jnp.float32)
    error_grad = 2.0 * mask_own[:, None] * pred_error / count_all
    grad_pred_low = (grad_pred + error_grad).astype(jnp.bfloat16)
    grad_final_w = matmul_tn(grad_pred_low, final_norm)
    grad_final = matmul_nn(grad_pred_low, w_final)
    grad_hidden, grad_gain_final, grad_shift_final = norm_back(
        norm_final, inv_final, gain_final, grad_final
    )
    layer_grads = [None] * LAYERS
    vec_grads = [None] * LAYERS
    for layer_idx in reversed(range(LAYERS)):
        vec_layer = vec_params[layer_idx * vec_rows : (layer_idx + 1) * vec_rows]
        grad_hidden, layer_grads[layer_idx], vec_grads[layer_idx] = layer_backward(
            grad_hidden,
            kept_list[layer_idx],
            layer_weights(layer_idx),
            vec_layer,
            keep_keys,
            score_scale,
        )
    grad_hidden_low = grad_hidden.astype(jnp.bfloat16)
    grad_input_w = matmul_tn(inputs, grad_hidden_low)
    grad_inputs = matmul_nt(grad_hidden_low, w_input)
    grad_clean = jnp.sqrt(signal_level) * grad_inputs[:, :EMBED_WIDTH] - error_grad
    grad_clean_all = lax.all_gather(
        grad_clean.astype(jnp.bfloat16), "vocab", axis=0, tiled=True
    ).astype(grad_clean.dtype)
    grad_table_look = zero_table.at[safe_row].add(
        jnp.where(valid_row[:, None], grad_clean_all, 0.0)
    )
    grad_table_local = grad_table_head + grad_table_look
    canon_list = []
    layer_idx = 0
    canon_list = canon_list + layer_grads[layer_idx]
    canon_grad = jnp.concatenate(canon_list + [grad_input_w, grad_final_w], 0).T
    vec_grad = jnp.concatenate(vec_grads + [grad_gain_final, grad_shift_final])
    grad_cols, vec_part = (
        lax.psum_scatter(canon_grad, "vocab", scatter_dimension=0, tiled=True),
        lax.psum_scatter(vec_grad, "vocab", scatter_dimension=0, tiled=True),
    )
    emb_cols = emb_table.shape[1]
    summed_cols, summed_vec, summed_table = lax.psum((grad_cols, vec_part, grad_table_local), "dp")
    table_grad = lax.dynamic_slice_in_dim(summed_table, data_pos * emb_cols, emb_cols, 1)
    slot_grad = jnp.zeros_like(mat_slots)
    cursor = 0
    for mat_idx in range(len(row_counts)):
        piece_cols = summed_cols[:, cursor : cursor + row_counts[mat_idx]]
        updated = lax.dynamic_update_slice_in_dim(slot_grad, piece_cols, local_start[mat_idx], 1)
        slot_grad = jnp.where(owners[mat_idx] == data_pos, updated, slot_grad)
        cursor = cursor + row_counts[mat_idx]
    vec_share = vec_first.shape[0]
    own_vecs = lax.dynamic_slice_in_dim(vec_params, vocab_pos * vec_share, vec_share)
    new_slots, slot_first_new, slot_second_new = adamw(
        mat_slots, slot_grad, slot_first, slot_second
    )
    new_table, table_first_new, table_second_new = adamw(
        emb_table, table_grad, table_first_moment, table_second_moment
    )
    new_vecs, vec_first_new, vec_second_new = adamw(own_vecs, summed_vec, vec_first, vec_second)
    loss_pair = jnp.stack([square + cross_sum, count_all])
    emb_norm = norm_total / count_all
    return (
        loss_pair,
        emb_norm,
        new_table,
        table_first_new,
        table_second_new,
        new_slots,
        slot_first_new,
        slot_second_new,
        new_vecs,
        vec_first_new,
        vec_second_new,
    )


def solution(mesh):
    in_specs = (
        P("dp", None),
        P("dp"),
        P("dp", None),
        P("dp", "vocab", None),
        P(),
        P("vocab", "dp"),
        P("vocab", "dp"),
        P("vocab", "dp"),
        P("vocab", "dp"),
        P("vocab", "dp"),
        P("vocab", "dp"),
        P(),
        P("vocab"),
        P("vocab"),
    )
    out_specs = (
        P(),
        P(),
        P("vocab", "dp"),
        P("vocab", "dp"),
        P("vocab", "dp"),
        P("vocab", "dp"),
        P("vocab", "dp"),
        P("vocab", "dp"),
        P("vocab"),
        P("vocab"),
        P("vocab"),
    )
    return jax.shard_map(
        per_device, mesh=mesh, in_specs=in_specs, out_specs=out_specs, check_vma=False
    )
```

profile of v0, /device:TPU:0, one launch (start us, length us, event | category | flops | bytes accessed | tf_op | source)
XLA Modules:
  0.0 1406.8 jit_solution(15728313752359818928)
XLA Ops:
  36.2 134.9 %all-reduce.13.cloned.1.call-done = (bf16[192,768]{1,0:T(8,128)(2,1)}, bf16[192,768]{1,0:T(8,128)(2,1)}, bf16[192,768]{1,0:T(8,128)(2,1)}, bf16[192,768]{1,0:T(8...) async-done(((bf16[192,768]{1,0:T(8,128)(2,1)}, bf16[192,768]{1,0:T(8,128)(2,1)}, bf16[192,768]{1,0:T(8,128)(2,1)}, bf16[192,768]{1,0:T(8,128)(2,1)}, ...) | async-done | bytes 3538960 | tf_op jit(solution)/shard_map/psum | solution.py:29
  181.7 62.9 %all-reduce.11.cloned.1.call-done = (bf16[192,128]{1,0:T(8,128)(2,1)}, bf16[192,128]{1,0:T(8,128)(2,1)}, bf16[192,128]{1,0:T(8,128)(2,1)}) async-done(((bf16[192,128]{1,0:T(8,128)(2,1)}, bf16[192,128]{1,0:T(8,128)(2,1)}, bf16[192,128]{1,0:T(8,128)(2,1)}), (bf16[192,128]{1,0:T(8,128)(2,1)}, bf16[192,128]{1,0:T(8,128)(2,1)}, bf16[192,128]{1,0:T(8,128)(2,1)})) %all-reduce.11.cloned.1.call-update) | async-done | bytes 147472 | tf_op jit(solution)/shard_map/psum | solution.py:29
  252.4 41.0 %all-gather.8.cloned.1.call-done = bf16[7632,128]{0,1:T(8,128)(2,1)} async-done(((bf16[7632,16]{0,1:T(8,128)(2,1)}), bf16[7632,128]{0,1:T(8,128)(2,1)}) %all-gather.8.cloned.1.call-update) | async-done | bytes 1953808 | tf_op jit(solution)/shard_map/all_gather | solution.py:324
  305.0 8.1 all-to-all-done
  314.4 76.7 %all-gather.10.cloned.1.call-done = bf16[768,9600]{1,0:T(8,128)(2,1)} async-done(((bf16[192,9600]{1,0:T(8,128)(2,1)}), bf16[768,9600]{1,0:T(8,128)(2,1)}) %all-gather.10.cloned.1.call-update) | async-done | bytes 14745616 | tf_op jit(solution)/shard_map/all_gather | solution.py:337
  403.7 10.3 all-gather.14.cloned.1.call-done
  467.9 36.6 %while.15 = (s32[]{:T(128)}, f32[2,512]{1,0:T(2,128)}, f32[2,512]{1,0:T(2,128)}, f32[2,512]{1,0:T(2,128)}, bf16[2,512,128]{2,1,0:T(8,128)(2,1)}, /*index=5*/bf16...) while((s32[]{:T(128)}, f32[2,512]{1,0:T(2,128)}, f32[2,512]{1,0:T(2,128)}, ...), condition=%wide.region_25.26_spmd.clone, body=%wide.region_21.25_spmd.clone.sunk | while | flops 1023785472 | bytes 33437928 | solution.py:405
  467.9 8.6 fusion.157
  486.2 8.6 fusion.157
  535.5 39.7 %all-reduce.1 = (f32[]{:T(128)}, f32[]{:T(128)}, f32[]{:T(128)}) all-reduce(f32[]{:T(128)} %get-tuple-element.424, f32[]{:T(128)S(6)} %add.349, f32[]{:T(128)} %get-tuple-element.353), channel_id=1, replica_groups=mesh['dp'=8,'vocab'=4] {'dp','vocab'}, use_global_device_ids=true, to_apply=%region_31.32 | all-reduce | flops 3 | bytes 24 | tf_op jit(solution)/shard_map/psum | solution.py:418
  575.9 36.7 %while.16 = (s32[]{:T(128)}, f32[7632,128]{1,0:T(8,128)}, bf16[2,512,128]{2,1,0:T(8,128)(2,1)}, bf16[2,512,128]{2,1,0:T(8,128)(2,1)}, bf16[7632,128]{1,0:T(8,128...) while((s32[]{:T(128)}, f32[7632,128]{1,0:T(8,128)}, ...), condition=%wide.region_36.37_spmd.clone, body=%wide.region_35.36_spmd.clone.sunk | while | flops 3026423808 | bytes 69069024 | solution.py:433
  600.9 8.6 convolution_add_fusion.6
  615.2 18.5 %reduce-scatter.7.cloned.1.call-done = bf16[256,128]{1,0:T(8,128)(2,1)} async-done(((bf16[1024,128]{1,0:T(8,128)(2,1)}), bf16[256,128]{1,0:T(8,128)(2,1)}) %reduce-scatter.7.cloned.1.call-update) | async-done | bytes 65552 | tf_op jit(solution)/shard_map/reduce_scatter | solution.py:436
  651.5 11.3 multiply_reduce_fusion
  674.4 8.7 fusion.44
  692.7 9.7 reduce-scatter.9.cloned.1.call-done
  705.5 28.3 %reduce-scatter.11.cloned.1.call-done = bf16[256,768]{0,1:T(8,128)(2,1)} async-done(((bf16[1024,768]{0,1:T(8,128)(2,1)}), bf16[256,768]{0,1:T(8,128)(2,1)}) %reduce-scatter.11.cloned.1.call-update) | async-done | bytes 393232 | tf_op jit(solution)/shard_map/reduce_scatter | solution.py:258
  755.6 29.8 %copy.128 = f32[768,9600]{1,0:T(8,128)} copy(f32[768,9600]{0,1:T(8,128)} %bitcast.163) | data formatting | bytes 58982400
  792.7 11.9 scatter_custom_fusion
  810.7 183.7 %reduce-scatter.13.cloned.1.call-done = f32[192,9600]{1,0:T(8,128)} async-done(((f32[768,9600]{1,0:T(8,128)}), f32[192,9600]{1,0:T(8,128)}) %reduce-scatter.13.cloned.1.call-update) | async-done | bytes 7372816 | tf_op jit(solution)/shard_map/reduce_scatter | solution.py:478
  1004.6 11.1 all-reduce
  1015.8 22.8 %psum.127 = f32[1920]{0:T(1024)S(1)} all-reduce(f32[1920]{0:T(1024)S(1)} %dynamic-slice.16), channel_id=1, replica_groups=mesh['dp'=8,'vocab'=4] {'dp'}, use_global_device_ids=true, to_apply=%region_59.60 | all-reduce | flops 1920 | bytes 15360 | tf_op jit(solution)/shard_map/psum | solution.py:482
  1039.3 309.6 %all-reduce.9.cloned.1.call-done = (f32[7632,128]{0,1:T(8,128)}, f32[192,9600]{1,0:T(8,128)}) async-done(((f32[7632,128]{0,1:T(8,128)}, f32[192,9600]{1,0:T(8,128)}), (f32[7632,128]{0,1:T(8,128)}, f32[192,9600]{1,0:T(8,128)})) %all-reduce.9.cloned.1.call-update) | async-done | bytes 11280400 | tf_op jit(solution)/shard_map/psum | solution.py:482
  1388.0 8.3 multiply_subtract_fusion
  (392 shorter events, 312.3 us)
Async XLA Ops:
  7.2 164.0 %all-reduce.13.cloned.1.call-start = ((), (), s32[]{:S(2)}) async-start(), calls=%async_computation.15 | async-start | bytes 7077888 | tf_op jit(solution)/shard_map/psum | solution.py:29
  26.8 217.8 %all-reduce.11.cloned.1.call-start = ((), (), s32[]{:S(2)}) async-start(), calls=%async_computation.14 | async-start | bytes 294912 | tf_op jit(solution)/shard_map/psum | solution.py:29
  35.4 258.0 %all-gather.8.cloned.1.call-start = ((), (), s32[]{:S(2)}) async-start(), calls=%async_computation.5 | async-start | bytes 2211840 | tf_op jit(solution)/shard_map/all_gather | solution.py:324
  36.2 355.0 %all-gather.10.cloned.1.call-start = ((), (), s32[]{:S(2)}) async-start(), calls=%async_computation.6 | async-start | bytes 18432000 | tf_op jit(solution)/shard_map/all_gather | solution.py:337
  180.6 69.1 %copy-start.49 = (s32[1,1024]{1,0:T(1,128)S(1)}, s32[1,1024]{1,0:T(1,128)}, u32[]{:S(2)}) copy-start(s32[1,1024]{1,0:T(1,128)} %param.21) | copy-start | bytes 12292
  250.5 140.7 %copy-start.77 = (bf16[256]{0:T(256)(128)(2,1)}, bf16[256]{0:T(256)(128)(2,1)S(1)}, u32[]{:S(2)}) copy-start(bf16[256]{0:T(256)(128)(2,1)S(1)} %pad.5.clone) | copy-start | bytes 1540
  252.4 52.0 %copy-start.43 = (f32[7680]{0:T(1024)S(1)}, f32[7680]{0:T(1024)}, u32[]{:S(2)}) copy-start(f32[7680]{0:T(1024)} %param.32) | copy-start | bytes 92164
  252.4 61.4 %copy-start.42 = (bf16[1,256,128]{2,1,0:T(8,128)(2,1)S(1)}, bf16[1,256,128]{2,1,0:T(8,128)(2,1)}, u32[]{:S(2)}) copy-start(bf16[1,256,128]{2,1,0:T(8,128)(2,1)} %param.24) | copy-start | bytes 196612
  300.9 12.2 all-to-all-start
  304.4 109.7 %all-gather.14.cloned.1.call-start = ((), (), s32[]{:S(2)}) async-start(), calls=%async_computation.8 | async-start | bytes 1966080 | tf_op jit(solution)/shard_map/all_gather | solution.py:163
  305.0 90.8 %copy-start.45 = (f32[768]{0:T(1024)}, f32[768]{0:T(1024)S(1)}, u32[]{:S(2)}) copy-start(f32[768]{0:T(1024)S(1)} %get-tuple-element.446) | copy-start | bytes 9220
  305.0 142.4 %copy-start.47 = (f32[768]{0:T(1024)}, f32[768]{0:T(1024)S(1)}, u32[]{:S(2)}) copy-start(f32[768]{0:T(1024)S(1)} %get-tuple-element.444) | copy-start | bytes 9220
  392.6 52.6 %copy-start.3 = (f32[256,768]{1,0:T(8,128)}, f32[256,768]{1,0:T(8,128)S(1)}, u32[]{:S(2)}) copy-start(f32[256,768]{1,0:T(8,128)S(1)} %get-tuple-element.468) | copy-start | bytes 2359300
  395.8 39.9 %all-gather.12.cloned.1.call-start = ((), (), s32[]{:S(2)}) async-start(), calls=%async_computation.7 | async-start | bytes 1966080 | tf_op jit(solution)/shard_map/all_gather | solution.py:164
  398.4 235.3 %reduce-scatter.7.cloned.1.call-start = ((), (), s32[]{:S(2)}) async-start(), calls=%async_computation.9 | async-start | bytes 327680 | tf_op jit(solution)/shard_map/reduce_scatter | solution.py:436
  612.5 89.9 %reduce-scatter.9.cloned.1.call-start = ((), (), s32[]{:S(2)}) async-start(), calls=%async_computation.10 | async-start | bytes 1966080 | tf_op jit(solution)/shard_map/reduce_scatter | solution.py:255
  674.1 59.6 %reduce-scatter.11.cloned.1.call-start = ((), (), s32[]{:S(2)}) async-start(), calls=%async_computation.11 | async-start | bytes 1966080 | tf_op jit(solution)/shard_map/reduce_scatter | solution.py:258
  683.1 311.2 %reduce-scatter.13.cloned.1.call-start = ((), (), s32[]{:S(2)}) async-start(), calls=%async_computation.12 | async-start | bytes 36864000 | tf_op jit(solution)/shard_map/reduce_scatter | solution.py:478
  690.7 43.0 %copy-start.55 = (f32[256]{0:T(256)S(1)}, f32[256]{0:T(256)}, u32[]{:S(2)}) copy-start(f32[256]{0:T(256)} %copy-done.54) | copy-start | bytes 3076
  692.7 43.6 %copy-start.12 = (bf16[256,768]{1,0:T(8,128)(2,1)S(1)}, bf16[256,768]{1,0:T(8,128)(2,1)}, u32[]{:S(2)}) copy-start(bf16[256,768]{1,0:T(8,128)(2,1)} %copy-done.10) | copy-start | bytes 1179652
  785.4 563.5 %all-reduce.9.cloned.1.call-start = ((), (), s32[]{:S(2)}) async-start(), calls=%async_computation.13 | async-start | bytes 22609920 | tf_op jit(solution)/shard_map/psum | solution.py:482
  994.3 44.2 %copy-start.44 = (f32[7680]{0:T(1024)S(1)}, f32[7680]{0:T(1024)}, u32[]{:S(2)}) copy-start(f32[7680]{0:T(1024)} %param.32) | copy-start | bytes 92164
  994.3 44.3 %copy-start.71 = (f32[1920]{0:T(1024)S(1)}, f32[1920]{0:T(1024)}, u32[]{:S(2)}) copy-start(f32[1920]{0:T(1024)} %param.33) | copy-start | bytes 23044
  994.3 44.3 %copy-start.72 = (f32[1920]{0:T(1024)S(1)}, f32[1920]{0:T(1024)}, u32[]{:S(2)}) copy-start(f32[1920]{0:T(1024)} %param.34) | copy-start | bytes 23044
  (79 other events, 677.7 us)
Sparse Core Ops, SparseCore 0:
  26.9 144.1 all-reduce.12
  175.2 69.3 all-reduce.10
  246.8 46.5 all-gather.7
  294.8 96.2 all-gather.9
  395.9 18.0 all-gather.13
  416.0 19.6 all-gather.11
  612.7 21.0 reduce-scatter.6
  674.2 28.1 reduce-scatter.8
  705.5 28.1 reduce-scatter.10
  785.5 208.7 reduce-scatter.12
  998.4 350.5 all-reduce.8
where the time goes:
time: 1420 us; the launch traced here: 1410 us
  waiting for transfers between devices  892 us (63%)
  matrix products  158 us (11%)
  local copies, waits for them, and re-layouts  123 us (9%)
  blocking collectives  102 us (7%)
  other arithmetic  81.7 us (6%)
  between operations  45.8 us (3%)
    psum x1, waiting for transfers between devices, per_device(): lax.psum((grad_cols, vec_part, grad_table_local), 'dp')  310 us
    psum x2, waiting for transfers between devices, broadcast(): return lax.psum(kept, axis)  198 us
    reduce_scatter x1, waiting for transfers between devices, per_device(): lax.psum_scatter(canon_grad, 'vocab', scatter_dimension=0, tiled=True)  184 us
    all_gather x1, waiting for transfers between devices, per_device(): weights = lax.all_gather(canon, 'vocab', axis=0, tiled=True).T  76.7 us
    unnamed x175, local copies, waits for them, and re-layouts  59.5 us
    dot_general x12, matrix products, matmul_nt(): lax.dot_general(left, right, (((1,), (1,)), ((), ())), preferred_element_...  55.3 us
    all_gather x1, waiting for transfers between devices, per_device(): lax.all_gather(emb_table.astype(jnp.bfloat16), 'dp', axis=1, tiled=True)  41 us
    psum x1, blocking collectives, per_device(): lax.psum((jnp.sum(mask_own), square_own, cross_own, norm_own), ('dp', 'vo...  39.7 us
  transfers between devices with their start and end apart: 12, of which 12 were waited for; matrix products, arithmetic and copies ran while one was open for 6% of the time, Pallas kernels for 0%

commit v1 on v0

--- a/solution.py
+++ b/solution.py
@@ -1,8 +1,11 @@
+import functools
 import math
 
 import jax
 import jax.numpy as jnp
 from jax import lax
+from jax.experimental import pallas as pl
+from jax.experimental.pallas import tpu as pltpu
 from jax.sharding import PartitionSpec as P
 
 D = 768
@@ -10,10 +13,11 @@
 HDIM = 64
 FF = 3072
 EMBED_WIDTH = 128
-LAYERS = 1
 DIFF = 2000
 STEP = 10
 CAP = 3072
+LAYERS = 1
+LANES = 128
 
 
 beta_one = 0.9
@@ -22,6 +26,954 @@
 weight_decay = 0.01
 eps_adam = 1e-08
 eps_norm = 1e-05
+f32 = jnp.float32
+bf16 = jnp.bfloat16
+
+
+def matmul_nn(left, right):
+    return jnp.dot(left, right, preferred_element_type=f32)
+
+
+def matmul_tn(left, right):
+    return lax.dot_general(left, right, (((0,), (0,)), ((), ())), preferred_element_type=f32)
+
+
+def matmul_nt(left, right):
+    return lax.dot_general(left, right, (((1,), (1,)), ((), ())), preferred_element_type=f32)
+
+
+ROW_COUNTS = [D, D, D, D, FF, FF, EMBED_WIDTH, EMBED_WIDTH, EMBED_WIDTH]
+
+
+def slot_starts(owners):
+    counts = jnp.array(ROW_COUNTS, jnp.int32)
+    same_owner = (owners[:, None] == owners[None, :]).astype(jnp.int32)
+    earlier_mask = jnp.tril(jnp.ones((len(ROW_COUNTS),) * 2, jnp.int32), -1)
+    return jnp.sum(same_owner * earlier_mask * counts[None, :], 1)
+
+
+def waves(places, width):
+    half_width = width // 2
+    frequency = jnp.exp(-math.log(10000.0) * jnp.arange(half_width, dtype=f32) / half_width)
+    angles = places[:, None] * frequency[None, :]
+    return jnp.concatenate([jnp.sin(angles), jnp.cos(angles)], 1)
+
+
+def norm_parts(value_entries):
+    center = value_entries - jnp.mean(value_entries, -1, keepdims=True)
+    scale_inv = lax.rsqrt(jnp.mean(center * center, -1, keepdims=True) + eps_norm)
+    return (center * scale_inv, scale_inv)
+
+
+def norm_back(normal_part, scale_inv, gain_vec, grad_out):
+    scaled = grad_out * gain_vec
+    inner = (
+        scaled
+        - jnp.mean(scaled, -1, keepdims=True)
+        - normal_part * jnp.mean(scaled * normal_part, -1, keepdims=True)
+    )
+    return (inner * scale_inv, jnp.sum(grad_out * normal_part, 0), jnp.sum(grad_out, 0))
+
+
+def adamw(weight, gradient, moment_one, moment_two):
+    moment_one = beta_one * moment_one + (1.0 - beta_one) * gradient
+    moment_two = beta_two * moment_two + (1.0 - beta_two) * gradient * gradient
+    fix_one = 1.0 - beta_one**STEP
+    fix_two = 1.0 - beta_two**STEP
+    update_dir = moment_one / fix_one / (jnp.sqrt(moment_two / fix_two) + eps_adam)
+    return (weight - learn_rate * (update_dir + weight_decay * weight), moment_one, moment_two)
+
+
+def swap_vocab(value, mask):
+    return lax.ppermute(value, "vocab", [(i, i ^ mask) for i in range(4)])
+
+
+def relative(value, axis=0):
+    v = lax.axis_index("vocab")
+    p = jnp.split(value, 4, axis)
+    swapped = jnp.where(v % 2 == 1, jnp.concatenate([p[1], p[0], p[3], p[2]], axis), value)
+    q = jnp.split(swapped, 4, axis)
+    return jnp.where(v // 2 == 1, jnp.concatenate([q[2], q[3], q[0], q[1]], axis), swapped)
+
+
+def vocab_gather(own, axis=0):
+    far = swap_vocab(own, 2)
+    near = swap_vocab(own, 1)
+    return jnp.concatenate([own, near, far, swap_vocab(far, 1)], axis)
+
+
+def vocab_gather_direct(own, axis=0):
+    return jnp.concatenate([own] + [swap_vocab(own, k) for k in (1, 2, 3)], axis)
+
+
+def vocab_exchange(pieces):
+    return [pieces[0]] + [swap_vocab(pieces[k], k) for k in (1, 2, 3)]
+
+
+def vocab_reduce(value):
+    p = jnp.split(value, 4, 0)
+    sent = swap_vocab(jnp.concatenate([p[1], p[3]], 0).astype(bf16), 1)
+    near, far = jnp.split(sent, 2, 0)
+    far = p[2] + far.astype(f32)
+    return p[0] + near.astype(f32) + swap_vocab(far.astype(bf16), 2).astype(f32)
+
+
+MESH = pl.DeviceIdType.MESH
+ANY = pl.BlockSpec(memory_space=pl.ANY)
+UNIT = 768
+HALF = 96
+QUARTER = 192
+
+
+def place():
+    d, v = lax.axis_index("dp"), lax.axis_index("vocab")
+    return d // 2, d % 2, d, v
+
+
+def greet(partners):
+    barrier = pltpu.get_barrier_semaphore()
+    for partner in partners:
+        pl.semaphore_signal(barrier, inc=1, device_id=partner, device_id_type=MESH)
+    pl.semaphore_wait(barrier, len(partners))
+
+
+def remote(src, dst, sems, index, partner):
+    return pltpu.make_async_remote_copy(
+        src_ref=src,
+        dst_ref=dst,
+        send_sem=sems[0].at[index],
+        recv_sem=sems[1].at[index],
+        device_id=partner,
+        device_id_type=MESH,
+    )
+
+
+def start_all(copies):
+    for copy in copies:
+        copy.start()
+    return copies
+
+
+def arrive_all(copies):
+    for copy in copies:
+        copy.wait_recv()
+
+
+def trade_kernel(payload, arrived, send, recv, local):
+    z, y, d, v = place()
+    masks = (4, 6, 5, 7, 2, 3, 1)
+    greet([(d ^ m, v) for m in masks])
+
+    def part(m):
+        other = d ^ m
+        return payload.at[other // 2, pl.ds((other % 2) * HALF, HALF), :]
+
+    copies = [
+        remote(part(m), arrived.at[d], (send, recv), i, (d ^ m, v)) for i, m in enumerate(masks)
+    ]
+    start_all(copies)
+    own = pltpu.make_async_copy(part(0), arrived.at[d], local)
+    own.start()
+    own.wait()
+    for copy in copies:
+        copy.wait()
+
+
+def trade(payload):
+    cols = payload.shape[2]
+    return pl.pallas_call(
+        trade_kernel,
+        out_shape=jax.ShapeDtypeStruct((8, HALF, cols), payload.dtype),
+        in_specs=[ANY],
+        out_specs=ANY,
+        scratch_shapes=[
+            pltpu.SemaphoreType.DMA((7,)),
+            pltpu.SemaphoreType.DMA((7,)),
+            pltpu.SemaphoreType.DMA,
+        ],
+        compiler_params=pltpu.CompilerParams(collective_id=0, has_side_effects=True),
+    )(payload)
+
+
+def spread_kernel(
+    up_home, down_home, small_home, attn_home, table_home,
+    up, down, small, attn, out, table,
+    z_send, z_recv, y_send, y_recv, x_send, x_recv, n_send, n_recv, f_send, f_recv, local,
+):
+    z, y, d, v = place()
+    far, near = v ^ 2, v ^ 1
+    greet([(d ^ m, v) for m in (2, 4, 6, 1)] + [(d, far), (d, near)])
+    homes = [up_home, down_home, small_home, attn_home, table_home]
+    fulls = [up, down, small, attn, table]
+    own_rows = pl.ds(v * QUARTER, QUARTER)
+
+    def spot(c, unit):
+        if c == 4:
+            return table.at[2 * unit + y]
+        first = y * HALF if c == 3 else v * QUARTER + y * HALF
+        return fulls[c].at[unit, pl.ds(first, HALF), :]
+
+    def start_line(c):
+        keep = pltpu.make_async_copy(homes[c], spot(c, z), local.at[c])
+        keep.start()
+        return [keep] + start_all(
+            [
+                remote(homes[c], spot(c, z), (z_send, z_recv), (c, k - 1), (d ^ (2 * k), v))
+                for k in (2, 1, 3)
+            ]
+        )
+
+    def wait_line(copies):
+        copies[0].wait()
+        arrive_all(copies[1:])
+        return copies[1:]
+
+    def start_side(c):
+        return start_all(
+            [remote(spot(c, u), spot(c, u), (y_send, y_recv), (c, u), (d ^ 1, v)) for u in range(4)]
+        )
+
+    def strips(c, rows):
+        if c == 3:
+            return [out.at[rows, :]]
+        return [fulls[c].at[u, rows, :] for u in range(4)]
+
+    def sources(c):
+        return [attn.at[3]] if c == 3 else strips(c, own_rows)
+
+    def start_far(c):
+        return start_all(
+            [
+                remote(s, t, (x_send, x_recv), (c, u), (d, far))
+                for u, (s, t) in enumerate(zip(sources(c), strips(c, own_rows)))
+            ]
+        )
+
+    def start_near(c):
+        return start_all(
+            [
+                remote(s, t, (n_send, n_recv), (c, u), (d, near))
+                for u, (s, t) in enumerate(zip(sources(c), strips(c, own_rows)))
+            ]
+        )
+
+    def start_last(c):
+        rows = pl.ds(far * QUARTER, QUARTER)
+        return start_all(
+            [
+                remote(s, s, (f_send, f_recv), (c, u), (d, near))
+                for u, s in enumerate(strips(c, rows))
+            ]
+        )
+
+    sent, landing = [], []
+    line, side, chip = {}, {}, {}
+
+    def begin_chip(c):
+        arrive_all(side[c])
+        if c == 3:
+            keep = pltpu.make_async_copy(attn.at[3], out.at[own_rows, :], local.at[5])
+            keep.start()
+            keep.wait()
+        if c != 4:
+            chip[c] = start_far(c)
+            near_copies = start_near(c)
+            sent.extend(chip[c] + near_copies)
+            landing.extend(near_copies)
+
+    def begin_last(c):
+        if c != 4:
+            arrive_all(chip[c])
+            last = start_last(c)
+            sent.extend(last)
+            landing.extend(last)
+
+    waves_of = [[0], [1], [2, 3], [4]]
+    for c in waves_of[0]:
+        line[c] = start_line(c)
+    for i, wave in enumerate(waves_of):
+        for c in wave:
+            sent.extend(wait_line(line[c]))
+        if i + 1 < len(waves_of):
+            for c in waves_of[i + 1]:
+                line[c] = start_line(c)
+        for c in wave:
+            side[c] = start_side(c)
+            sent.extend(side[c])
+        if i >= 1:
+            for c in waves_of[i - 1]:
+                begin_chip(c)
+        if i >= 2:
+            for c in waves_of[i - 2]:
+                begin_last(c)
+    for c in waves_of[-1]:
+        begin_chip(c)
+    for wave in waves_of[-2:]:
+        for c in wave:
+            begin_last(c)
+    arrive_all(landing)
+    for copy in sent:
+        copy.wait_send()
+
+
+def spread(up_home, down_home, small_home, attn_home, table_home):
+    small_cols = small_home.shape[1]
+    rows, vocab_rows = table_home.shape
+    dma = pltpu.SemaphoreType.DMA
+
+    def shape(*dims):
+        return jax.ShapeDtypeStruct(dims, bf16)
+
+    return pl.pallas_call(
+        spread_kernel,
+        out_shape=[
+            shape(4, D, UNIT),
+            shape(4, D, UNIT),
+            shape(4, D, small_cols),
+            shape(4, QUARTER, UNIT),
+            shape(D, UNIT),
+            shape(8, rows, vocab_rows),
+        ],
+        in_specs=[ANY] * 5,
+        out_specs=[ANY] * 6,
+        scratch_shapes=[dma((5, 3))] * 2 + [dma((5, 4))] * 2 + [dma((4, 4))] * 6 + [dma((6,))],
+        compiler_params=pltpu.CompilerParams(collective_id=1, has_side_effects=True),
+    )(up_home, down_home, small_home, attn_home, table_home)
+
+I16 = jnp.int16
+TAIL = 16
+TILES = 60
+
+
+def exponent(peak):
+    return jnp.ceil(jnp.log2(jnp.maximum(peak, 1e-30))) + 1.0
+
+
+def coded(value, power):
+    return jnp.round(value * jnp.exp2(15.0 - power)).astype(jnp.int32).astype(I16)
+
+
+def plain(code, power):
+    return code.astype(jnp.int32).astype(f32) * jnp.exp2(power - 15.0)
+
+
+def put(ref, value):
+    rows, cols = value.shape
+    power = exponent(jnp.max(jnp.abs(value), 0, keepdims=True))
+    ref[0:rows, :] = coded(value, power)
+    ref[rows : rows + TAIL, :] = (
+        jnp.broadcast_to(power, (TAIL, cols)).astype(jnp.int32).astype(I16)
+    )
+
+
+def get(ref, rows):
+    power = ref[rows : rows + TAIL, :].astype(jnp.int32).astype(f32)[0:1]
+    return plain(ref[0:rows, :], power)
+
+
+def put_tiles(ref, source, rows):
+    lane = lax.broadcasted_iota(jnp.int32, (rows, LANES), 1)
+
+    def body(tile, powers):
+        at = pl.ds(pl.multiple_of(tile * LANES, LANES), LANES)
+        value = source(at)
+        power = exponent(jnp.max(jnp.abs(value), 1, keepdims=True))
+        ref[:, at] = coded(value, power)
+        return jnp.where(lane == tile, power, powers)
+
+    powers = lax.fori_loop(0, TILES, body, jnp.zeros((rows, LANES), f32), unroll=6)
+    ref[:, TILES * LANES :] = powers.astype(jnp.int32).astype(I16)
+
+
+def tile_getter(ref, rows):
+    lane = lax.broadcasted_iota(jnp.int32, (rows, LANES), 1)
+    powers = ref[:, TILES * LANES :].astype(jnp.int32).astype(f32)
+
+    def read(tile, at):
+        power = jnp.sum(jnp.where(lane == tile, powers, 0.0), 1, keepdims=True)
+        return plain(ref[:, at], power)
+
+    return read
+
+
+def grads_kernel(
+    down_left, up_left, out_left, small_left, final_left, qkv_left,
+    active, grad_up, mixed, inputs, grad_pred, normed, table,
+    big, small, table_sum,
+    cs, cr, xs, xr, ys, yr, zs, zr, home, part, half,
+    small_cs, small_cr, small_xs, small_xr, small_ys, small_yr, small_zs, small_zr, small_home, small_half,
+    ts, tr, tzs, tzr,
+    c_send, c_recv, x_send, x_recv, y_send, y_recv, z_send, z_recv, g_send, g_recv, f_send, f_recv, local,
+):
+    z, y, d, v = place()
+    far, near = v ^ 2, v ^ 1
+    greet([(d ^ m, v) for m in (2, 4, 6, 1)] + [(d, far), (d, near)])
+    sent = []
+
+    def send(src, dst, sems, index, partner):
+        copy = remote(src, dst, sems, index, partner)
+        copy.start()
+        sent.append(copy)
+        return copy
+
+    def product(n, who):
+        if n == 0:
+            return matmul_nn(out_left[who], mixed[...])
+        if n < 5:
+            return matmul_nn(down_left[who], active[n - 1])
+        return matmul_nn(up_left[who], grad_up[n - 5])
+
+    core, chip, side, line, spread_line, spread_side = {}, {}, {}, {}, {}, {}
+
+    def to_core(n):
+        put(cs.at[n, 0], product(n, near))
+        put(cs.at[n, 1], product(n, near ^ 2))
+        core[n] = send(cs.at[n], cr.at[n], (c_send, c_recv), n, (d, near))
+
+    def to_chip(n):
+        core[n].wait_recv()
+        put(xs.at[n], product(n, far) + get(cr.at[n, 1], QUARTER))
+        chip[n] = send(xs.at[n], xr.at[n], (x_send, x_recv), n, (d, far))
+
+    def halves(slot, value):
+        part[...] = value
+        put(ys.at[slot], part[pl.ds((1 - y) * HALF, HALF), :])
+        half[slot] = part[pl.ds(y * HALF, HALF), :]
+        side[slot] = send(ys.at[slot], yr.at[slot], (y_send, y_recv), slot, (d ^ 1, v))
+
+    def to_side(n):
+        chip[n].wait_recv()
+        value = product(n, v) + get(cr.at[n, 0], QUARTER) + get(xr.at[n], QUARTER)
+        halves(3 + n, value)
+
+    def to_line(group):
+        for u in range(4):
+            slot = 4 * group + u
+            side[slot].wait_recv()
+            half[slot] = half[slot] + get(yr.at[slot], HALF)
+        for k in (2, 1, 3):
+            put(zs.at[group, k - 1], half[4 * group + (z ^ k)])
+            line[group, k] = send(
+                zs.at[group, k - 1], zr.at[group, k - 1], (z_send, z_recv), 3 * group + k - 1, (d ^ (2 * k), v)
+            )
+
+    def to_home(group):
+        total = half[4 * group + z]
+        for k in (2, 1, 3):
+            line[group, k].wait_recv()
+            total = total + get(zr.at[group, k - 1], HALF)
+        put(home.at[group], total)
+        keep = pltpu.make_async_copy(home.at[group], big.at[4 * group + z, y], local.at[group])
+        keep.start()
+        for k in (2, 1, 3):
+            spread_line[group, k] = send(
+                home.at[group], big.at[4 * group + z, y], (g_send, g_recv), 3 * group + k - 1, (d ^ (2 * k), v)
+            )
+        keep.wait()
+
+    def to_all(group):
+        for k in (2, 1, 3):
+            spread_line[group, k].wait_recv()
+        for u in range(4):
+            slot = 4 * group + u
+            spread_side[slot] = send(
+                big.at[slot, y], big.at[slot, y], (f_send, f_recv), slot, (d ^ 1, v)
+            )
+
+    def small_product(who):
+        return jnp.concatenate(
+            [matmul_nn(small_left[who], inputs[...]), matmul_nn(final_left[who], grad_pred[...])], 1
+        )
+
+    def small_to_core():
+        put(small_cs.at[0], small_product(near))
+        put(small_cs.at[1], small_product(near ^ 2))
+        core[9] = send(small_cs, small_cr, (c_send, c_recv), 9, (d, near))
+
+    def small_to_chip():
+        core[9].wait_recv()
+        put(small_xs, small_product(far) + get(small_cr.at[1], QUARTER))
+        chip[9] = send(small_xs, small_xr, (x_send, x_recv), 9, (d, far))
+
+    def small_to_side():
+        chip[9].wait_recv()
+        value = small_product(v) + get(small_cr.at[0], QUARTER) + get(small_xr, QUARTER)
+        cols = value.shape[1]
+        part[:, 0:cols] = value
+        put(small_ys, part[pl.ds((1 - y) * HALF, HALF), 0:cols])
+        small_half[0] = part[pl.ds(y * HALF, HALF), 0:LANES]
+        small_half[1] = part[pl.ds(y * HALF, HALF), LANES : 2 * LANES]
+        small_half[2] = part[pl.ds(y * HALF, HALF), 2 * LANES : cols]
+        small_half[3] = jnp.zeros((HALF, LANES), f32)
+        side[12] = send(small_ys, small_yr, (y_send, y_recv), 12, (d ^ 1, v))
+
+    def small_to_line():
+        side[12].wait_recv()
+        value = get(small_yr, HALF)
+        for u in range(3):
+            small_half[u] = small_half[u] + value[:, u * LANES : (u + 1) * LANES]
+        for k in (2, 1, 3):
+            put(small_zs.at[k - 1], small_half[z ^ k])
+            line[3, k] = send(
+                small_zs.at[k - 1], small_zr.at[k - 1], (z_send, z_recv), 9 + k - 1, (d ^ (2 * k), v)
+            )
+
+    def small_to_home():
+        total = small_half[z]
+        for k in (2, 1, 3):
+            line[3, k].wait_recv()
+            total = total + get(small_zr.at[k - 1], HALF)
+        put(small_home, total)
+        keep = pltpu.make_async_copy(small_home, small.at[z, y], local.at[3])
+        keep.start()
+        for k in (2, 1, 3):
+            spread_line[3, k] = send(
+                small_home, small.at[z, y], (g_send, g_recv), 9 + k - 1, (d ^ (2 * k), v)
+            )
+        keep.wait()
+
+    def small_to_all():
+        for k in (2, 1, 3):
+            spread_line[3, k].wait_recv()
+        spread_side[12] = send(
+            small.at[:, y], small.at[:, y], (f_send, f_recv), 12, (d ^ 1, v)
+        )
+
+    def table_to_side():
+        put_tiles(ts, lambda at: table[1 - y, :, at], 64)
+        side[13] = send(ts, tr, (y_send, y_recv), 13, (d ^ 1, v))
+
+    def table_line_value(which):
+        rows = pl.ds(pl.multiple_of(which * 16, 16), 16)
+        read = tile_getter(tr.at[rows, :], 16)
+        return rows, read
+
+    def table_to_line():
+        side[13].wait_recv()
+        for k in (2, 1, 3):
+            rows, read = table_line_value(z ^ k)
+
+            def source(at, rows=rows, read=read):
+                return table[y, rows, at] + read(at.start // LANES, at)
+
+            put_tiles(tzs.at[k - 1], source, 16)
+            line[4, k] = send(
+                tzs.at[k - 1], tzr.at[k - 1], (z_send, z_recv), 12 + k - 1, (d ^ (2 * k), v)
+            )
+
+    def table_to_home():
+        for k in (2, 1, 3):
+            line[4, k].wait_recv()
+        rows, read = table_line_value(z)
+        others = [tile_getter(tzr.at[k], 16) for k in range(3)]
+
+        def body(tile, carry):
+            at = pl.ds(pl.multiple_of(tile * LANES, LANES), LANES)
+            value = table[y, rows, at] + read(tile, at)
+            for other in others:
+                value = value + other(tile, at)
+            table_sum[:, at] = value
+            return carry
+
+        lax.fori_loop(0, TILES, body, 0, unroll=4)
+
+    to_core(0)
+    to_core(1)
+    to_chip(0)
+    to_core(2)
+    to_chip(1)
+    table_to_side()
+    to_core(3)
+    to_chip(2)
+    for u in range(3):
+        halves(u, matmul_nn(qkv_left[u], normed[...]))
+    to_core(4)
+    to_chip(3)
+    small_to_core()
+    to_side(0)
+    to_core(5)
+    to_chip(4)
+    small_to_chip()
+    to_side(1)
+    table_to_line()
+    to_core(6)
+    to_chip(5)
+    to_side(2)
+    to_line(0)
+    to_core(7)
+    to_chip(6)
+    to_side(3)
+    to_core(8)
+    to_chip(7)
+    to_side(4)
+    to_chip(8)
+    small_to_side()
+    to_line(1)
+    table_to_home()
+    to_home(0)
+    to_side(5)
+    small_to_line()
+    to_side(6)
+    to_home(1)
+    to_all(0)
+    to_side(7)
+    small_to_home()
+    to_side(8)
+    to_line(2)
+    to_all(1)
+    small_to_all()
+    to_home(2)
+    to_all(2)
+    for slot in range(13):
+        spread_side[slot].wait_recv()
+    for copy in sent:
+        copy.wait_send()
+
+
+def reduce_grads(*operands):
+    dma = pltpu.SemaphoreType.DMA
+    vmem = pltpu.VMEM
+    tall, low, wide = QUARTER + TAIL, HALF + TAIL, 3 * LANES
+    table_cols = TILES * LANES
+    return pl.pallas_call(
+        grads_kernel,
+        out_shape=[
+            jax.ShapeDtypeStruct((12, 2, low, UNIT), I16),
+            jax.ShapeDtypeStruct((4, 2, low, LANES), I16),
+            jax.ShapeDtypeStruct((16, table_cols), f32),
+        ],
+        in_specs=[pl.BlockSpec(memory_space=pltpu.VMEM)] * 13,
+        out_specs=[ANY, ANY, pl.BlockSpec(memory_space=pltpu.VMEM)],
+        scratch_shapes=[
+            vmem((9, 2, tall, UNIT), I16),
+            vmem((9, 2, tall, UNIT), I16),
+            vmem((9, tall, UNIT), I16),
+            vmem((9, tall, UNIT), I16),
+            vmem((12, low, UNIT), I16),
+            vmem((12, low, UNIT), I16),
+            vmem((3, 3, low, UNIT), I16),
+            vmem((3, 3, low, UNIT), I16),
+            vmem((3, low, UNIT), I16),
+            vmem((QUARTER, UNIT), f32),
+            vmem((12, HALF, UNIT), f32),
+            vmem((2, tall, wide), I16),
+            vmem((2, tall, wide), I16),
+            vmem((tall, wide), I16),
+            vmem((tall, wide), I16),
+            vmem((low, wide), I16),
+            vmem((low, wide), I16),
+            vmem((3, low, LANES), I16),
+            vmem((3, low, LANES), I16),
+            vmem((low, LANES), I16),
+            vmem((4, HALF, LANES), f32),
+            vmem((64, table_cols + LANES), I16),
+            vmem((64, table_cols + LANES), I16),
+            vmem((3, 16, table_cols + LANES), I16),
+            vmem((3, 16, table_cols + LANES), I16),
+        ]
+        + [dma((10,))] * 4
+        + [dma((14,))] * 2
+        + [dma((15,))] * 2
+        + [dma((12,))] * 2
+        + [dma((13,))] * 2
+        + [dma((4,))],
+        compiler_params=pltpu.CompilerParams(
+            collective_id=2, has_side_effects=True, vmem_limit_bytes=60 * 2**20
+        ),
+    )(*operands)
+
+
+def slot_kernel(kind, unit, column, big, small, w, m1, m2, w_out, m1_out, m2_out):
+    which = kind[pl.program_id(0)]
+
+    def rows_of(ref):
+        return jnp.concatenate([get(ref.at[0, 0], HALF), get(ref.at[0, 1], HALF)], 0)
+
+    zero = jnp.zeros(w.shape, f32)
+    g = jnp.where(which == 1, rows_of(big), jnp.where(which == 2, rows_of(small), zero))
+    w_out[...], m1_out[...], m2_out[...] = adamw(w[...], g, m1[...], m2[...])
+
+
+def slot_update(owners, starts, big, small, slots, first, second):
+    rows = slots.shape[0]
+    blocks = CAP // LANES
+    d = lax.axis_index("dp")
+    spots, units, columns, kinds = [], [], [], []
+    per_unit = UNIT // LANES
+    first_unit = [0, 1, 2, 3, 8, 4, 0, 1, 2]
+    for i, count in enumerate(ROW_COUNTS):
+        spots.append(jnp.where(owners[i] == d, starts[i] // LANES, -CAP) + jnp.arange(count // LANES))
+        for b in range(count // LANES):
+            units.append(first_unit[i] + b // per_unit)
+            columns.append(b % per_unit)
+            kinds.append(2 if i > 5 else 1)
+    hit = jnp.concatenate(spots)[None, :] == jnp.arange(blocks)[:, None]
+
+    def looked_up(values):
+        return jnp.sum(jnp.where(hit, jnp.array(values, jnp.int32)[None, :], 0), 1).astype(jnp.int32)
+
+    kind, unit, column = looked_up(kinds), looked_up(units), looked_up(columns)
+    plain_spec = pl.BlockSpec((rows, LANES), lambda j, k, u, c: (0, j))
+    low = HALF + TAIL
+    big_spec = pl.BlockSpec(
+        (1, 2, low, LANES),
+        lambda j, k, u, c: (jnp.where(k[j] == 1, u[j], 0), 0, 0, jnp.where(k[j] == 1, c[j], 0)),
+    )
+    small_spec = pl.BlockSpec(
+        (1, 2, low, LANES), lambda j, k, u, c: (jnp.where(k[j] == 2, u[j], 0), 0, 0, 0)
+    )
+    return pl.pallas_call(
+        slot_kernel,
+        grid_spec=pltpu.PrefetchScalarGridSpec(
+            num_scalar_prefetch=3,
+            grid=(blocks,),
+            in_specs=[big_spec, small_spec, plain_spec, plain_spec, plain_spec],
+            out_specs=[plain_spec, plain_spec, plain_spec],
+        ),
+        out_shape=[jax.ShapeDtypeStruct(slots.shape, f32)] * 3,
+        cost_estimate=pl.CostEstimate(flops=0, bytes_accessed=28 * rows * CAP, transcendentals=0),
+    )(kind, unit, column, big, small, slots, first, second)
+
+
+def swap_dp(value, mask):
+    return lax.ppermute(value, "dp", [(i, i ^ mask) for i in range(8)])
+
+
+def sum_all(value, over_vocab=True):
+    if over_vocab:
+        for mask in (1, 2):
+            value = value + swap_vocab(value, mask)
+    for mask in (1, 2, 4):
+        value = value + swap_dp(value, mask)
+    return value
+
+
+def per_device(
+    token_ids,
+    timesteps,
+    pad_mask,
+    noise_draw,
+    owners,
+    emb_table,
+    table_first_moment,
+    table_second_moment,
+    mat_slots,
+    slot_first,
+    slot_second,
+    vec_params,
+    vec_first,
+    vec_second,
+):
+    v = lax.axis_index("vocab")
+    d = lax.axis_index("dp")
+    z = d // 2
+    seq_len = token_ids.shape[1]
+    tokens = seq_len // 4
+    vocab_rows, emb_cols = emb_table.shape
+    heads_own = HEADS // 4
+    score_scale = HDIM ** (-0.5)
+
+    starts = slot_starts(owners)
+    whole = (owners[4] == d) | (owners[5] == d)
+
+    def unit_payload(u):
+        start = jnp.where(whole, u * UNIT, starts[u])
+        main = lax.dynamic_slice(mat_slots, (0, start), (QUARTER, UNIT))
+        extra = lax.dynamic_slice(
+            mat_slots, (0, starts[6 + min(u, 2)]), (QUARTER, EMBED_WIDTH)
+        )
+        return jnp.concatenate([main, extra], 1).astype(bf16)
+
+    arrived = trade(jnp.stack([unit_payload(u) for u in range(4)]))
+
+    def from_owner(index, lo, width):
+        return lax.dynamic_slice(arrived, (owners[index], 0, lo), (1, HALF, width))[0]
+
+    table_own = emb_table.T
+    w_up, w_down, w_small, w_attn, w_out, table_low = spread(
+        from_owner(4, 0, UNIT),
+        from_owner(5, 0, UNIT),
+        from_owner(6 + jnp.minimum(z, 2), UNIT, EMBED_WIDTH),
+        from_owner(z, 0, UNIT),
+        table_own.astype(bf16),
+    )
+    table_low = table_low.reshape(EMBED_WIDTH, vocab_rows)
+
+    ids_rel = relative(token_ids[0])
+    mask_rel = relative(pad_mask[0])
+    keep_keys = mask_rel > 0
+    weight_rel = mask_rel.astype(f32)
+    mask_own = weight_rel[:tokens]
+    count_all = sum_all(jnp.sum(weight_rel)[None], False)[0]
+    local_row = ids_rel - v * vocab_rows
+    valid_row = (local_row >= 0) & (local_row < vocab_rows)
+    safe_row = jnp.clip(local_row, 0, vocab_rows - 1)
+    found_rows = jnp.where(
+        valid_row[:, None], jnp.take(table_low.T, safe_row, axis=0), jnp.zeros((), bf16)
+    )
+    pieces = vocab_exchange(jnp.split(found_rows, 4, 0))
+    clean_emb = sum(piece.astype(f32) for piece in pieces)
+    own_places = (v * tokens + jnp.arange(tokens)).astype(f32)
+    step_val = timesteps[0].astype(f32)
+    signal_level = 1.0 - jnp.sqrt(step_val / DIFF + 0.0001)
+    noisy_emb = jnp.sqrt(signal_level) * clean_emb + jnp.sqrt(1.0 - signal_level) * noise_draw[
+        0
+    ].astype(f32)
+    time_feat = jnp.broadcast_to(waves(step_val[None], EMBED_WIDTH), (tokens, EMBED_WIDTH))
+    inputs = jnp.concatenate([noisy_emb, time_feat], 1).astype(bf16)
+
+    g_one, b_one, g_two, b_two = [vec_params[i * D : (i + 1) * D] for i in range(4)]
+    bias_up = vec_params[4 * D : 4 * D + FF].reshape(4, 1, UNIT)
+    g_fin, b_fin = [vec_params[4 * D + FF + i * D : 4 * D + FF + (i + 1) * D] for i in range(2)]
+
+    hidden = (
+        matmul_nt(inputs[:, :EMBED_WIDTH], w_small[0])
+        + matmul_nt(inputs[:, EMBED_WIDTH:], w_small[1])
+        + waves(own_places, D)
+    )
+    norm_one, inv_one = norm_parts(hidden)
+    normed_all = vocab_gather((norm_one * g_one + b_one).astype(bf16))
+    queries, keys, values = [matmul_nt(normed_all, w_attn[i]).astype(bf16) for i in range(3)]
+
+    def by_head(value):
+        return value.reshape(seq_len, heads_own, HDIM)
+
+    q_h, k_h, v_h = by_head(queries), by_head(keys), by_head(values)
+    scores = jnp.einsum("qhd,khd->hqk", q_h, k_h, preferred_element_type=f32) * score_scale
+    scores = jnp.where(keep_keys[None, None, :], scores, -1000000000.0)
+    row_max = jnp.max(scores, -1, keepdims=True)
+    expo = jnp.exp(scores - row_max)
+    probs = expo / jnp.sum(expo, -1, keepdims=True)
+    probs_low = probs.astype(bf16)
+    mixed = jnp.einsum("hqk,khd->qhd", probs_low, v_h, preferred_element_type=f32)
+    mixed = mixed.reshape(seq_len, QUARTER).astype(bf16)
+    mixed_own = relative(jnp.concatenate(vocab_exchange(jnp.split(mixed, 4, 0)), 1), 1)
+    middle = hidden + matmul_nt(mixed_own, w_out)
+    norm_two, inv_two = norm_parts(middle)
+    normed_two = (norm_two * g_two + b_two).astype(bf16)
+    up_proj = (
+        jnp.einsum("tk,jkn->jtn", normed_two, w_up, preferred_element_type=f32) + bias_up
+    )
+    active = jax.nn.gelu(up_proj).astype(bf16)
+    hidden_two = middle + jnp.einsum("jtn,jon->to", active, w_down, preferred_element_type=f32)
+    norm_final, inv_final = norm_parts(hidden_two)
+    final_norm = (norm_final * g_fin + b_fin).astype(bf16)
+    predicted = matmul_nn(final_norm, w_small[2])
+
+    pred_all = vocab_gather_direct(predicted.astype(bf16))
+    logits = matmul_nn(pred_all, table_low)
+    columns = lax.broadcasted_iota(jnp.int32, (seq_len, vocab_rows), 1)
+    chosen = columns == local_row[:, None]
+    peak = jnp.max(logits, -1)
+    exp_low = jnp.exp(logits - peak[:, None])
+    exp_sum = jnp.sum(exp_low, -1)
+    exp_low = exp_low.astype(bf16)
+    target = jnp.sum(jnp.where(chosen, logits, 0.0), -1)
+    mix_emb = matmul_nt(exp_low, table_low)
+    stats = jnp.stack([peak, exp_sum, target]).reshape(3, 4, tokens)
+    stat_list = [stats]
+    for k in (1, 2, 3):
+        got = swap_vocab(stats, k)
+        stat_list.append(jnp.stack([got[:, j ^ k] for j in range(4)], 1))
+    peak_all = functools.reduce(jnp.maximum, [s[0] for s in stat_list])
+    total_all = sum(s[1] * jnp.exp(s[0] - peak_all) for s in stat_list)
+    target_own = sum(s[2][0] for s in stat_list)
+    lse = (peak_all + jnp.log(total_all)).reshape(seq_len)
+    row_weight = weight_rel / count_all
+    factor = jnp.exp(peak - lse) * row_weight
+    grad_pred_local = mix_emb * factor[:, None] - found_rows.astype(f32) * row_weight[:, None]
+    pieces = vocab_exchange(jnp.split(grad_pred_local.astype(bf16), 4, 0))
+    pred_error = predicted - clean_emb
+    error_grad = 2.0 * mask_own[:, None] * pred_error / count_all
+    grad_pred_low = (sum(piece.astype(f32) for piece in pieces) + error_grad).astype(bf16)
+    grad_logits = exp_low.astype(f32) * factor[:, None] - jnp.where(chosen, row_weight[:, None], 0.0)
+    grad_table_head = matmul_tn(pred_all, grad_logits.astype(bf16))
+
+    square_own = jnp.sum(mask_own[:, None] * pred_error * pred_error)
+    cross_own = jnp.sum(mask_own * (lse[:tokens] - target_own))
+    norm_own = jnp.sum(mask_own * jnp.sqrt(jnp.sum(clean_emb * clean_emb, -1) + 1e-06))
+    square, cross_sum, norm_total = sum_all(jnp.stack([square_own, cross_own, norm_own]))
+
+    grad_final = matmul_nt(grad_pred_low, w_small[2])
+    grad_hidden, grad_gf, grad_bf = norm_back(norm_final, inv_final, g_fin, grad_final)
+    grad_low = grad_hidden.astype(bf16)
+    grad_active = jnp.einsum("to,jon->jtn", grad_low, w_down, preferred_element_type=f32)
+    grad_up_proj = jax.vjp(jax.nn.gelu, up_proj)[1](grad_active)[0].astype(bf16)
+    grad_bias = jnp.sum(grad_up_proj.astype(f32), 1).reshape(FF)
+    grad_normed_two = jnp.einsum("jtn,jkn->tk", grad_up_proj, w_up, preferred_element_type=f32)
+    grad_part, grad_g2, grad_b2 = norm_back(norm_two, inv_two, g_two, grad_normed_two)
+    grad_middle = grad_hidden + grad_part
+    grad_attn = grad_middle.astype(bf16)
+    grad_mixed = relative(matmul_nn(grad_attn, w_out).astype(bf16), 1)
+    grad_mixed = by_head(jnp.concatenate(vocab_exchange(jnp.split(grad_mixed, 4, 1)), 0))
+    grad_probs = jnp.einsum("qhd,khd->hqk", grad_mixed, v_h, preferred_element_type=f32)
+    inner_sum = jnp.sum(probs * grad_probs, -1, keepdims=True)
+    grad_scores = (probs * (grad_probs - inner_sum)).astype(bf16)
+    grad_q = jnp.einsum("hqk,khd->qhd", grad_scores, k_h, preferred_element_type=f32)
+    grad_k = jnp.einsum("hqk,qhd->khd", grad_scores, q_h, preferred_element_type=f32)
+    grad_v = jnp.einsum("hqk,qhd->khd", probs_low, grad_mixed, preferred_element_type=f32)
+    grad_q = (grad_q * score_scale).astype(bf16).reshape(seq_len, QUARTER)
+    grad_k = (grad_k * score_scale).astype(bf16).reshape(seq_len, QUARTER)
+    grad_v = grad_v.astype(bf16).reshape(seq_len, QUARTER)
+    grad_normed = vocab_reduce(
+        matmul_nn(grad_q, w_attn[0]) + matmul_nn(grad_k, w_attn[1]) + matmul_nn(grad_v, w_attn[2])
+    )
+    grad_part_one, grad_g1, grad_b1 = norm_back(norm_one, inv_one, g_one, grad_normed)
+    grad_hidden_low = (grad_middle + grad_part_one).astype(bf16)
+    grad_inputs = matmul_nn(grad_hidden_low, w_small[0])
+    grad_clean = jnp.sqrt(signal_level) * grad_inputs - error_grad
+    grad_clean_all = vocab_gather_direct(grad_clean.astype(bf16))
+    grad_table = grad_table_head + matmul_tn(grad_clean_all, chosen.astype(bf16))
+    grad_table = jnp.pad(grad_table, ((0, 0), (0, TILES * LANES - vocab_rows)))
+    grad_table = grad_table.reshape(4, 2, 16, TILES * LANES).transpose(1, 0, 2, 3)
+
+    def left(value):
+        return value.T.reshape(4, QUARTER, value.shape[0])
+
+    big, small, table_grad = reduce_grads(
+        left(grad_low),
+        left(normed_two),
+        left(grad_attn),
+        left(grad_hidden_low),
+        left(final_norm),
+        jnp.stack([grad_q.T, grad_k.T, grad_v.T]),
+        active,
+        grad_up_proj,
+        mixed_own,
+        inputs,
+        grad_pred_low,
+        normed_all,
+        grad_table.reshape(2, 64, TILES * LANES),
+    )
+
+    grad_vec = jnp.concatenate([grad_g1, grad_b1, grad_g2, grad_b2, grad_bias, grad_gf, grad_bf])
+    grad_vec = sum_all(grad_vec)
+    vec_share = vec_first.shape[0]
+    own_grad = lax.dynamic_slice_in_dim(grad_vec, v * vec_share, vec_share)
+    own_vecs = lax.dynamic_slice_in_dim(vec_params, v * vec_share, vec_share)
+
+    new_slots, slot_first_new, slot_second_new = slot_update(
+        owners, starts, big, small, mat_slots, slot_first, slot_second
+    )
+    new_table, table_first_new, table_second_new = adamw(
+        table_own, table_grad[:, :vocab_rows], table_first_moment.T, table_second_moment.T
+    )
+    new_vecs, vec_first_new, vec_second_new = adamw(own_vecs, own_grad, vec_first, vec_second)
+    loss_pair = jnp.stack([square + cross_sum, count_all])
+    emb_norm = norm_total / count_all
+    return (
+        loss_pair,
+        emb_norm,
+        new_table.T,
+        table_first_new.T,
+        table_second_new.T,
+        new_slots,
+        slot_first_new,
+        slot_second_new,
+        new_vecs,
+        vec_first_new,
+        vec_second_new,
+    )
 
 
 def broadcast(value, axis, source):
@@ -37,55 +989,16 @@
     return so_far
 
 
-def matmul_nn(left, right):
-    return jnp.dot(left, right, preferred_element_type=jnp.float32)
-
-
-def matmul_tn(left, right):
-    return lax.dot_general(
-        left, right, (((0,), (0,)), ((), ())), preferred_element_type=jnp.float32
-    )
-
-
-def matmul_nt(left, right):
-    return lax.dot_general(
-        left, right, (((1,), (1,)), ((), ())), preferred_element_type=jnp.float32
-    )
-
-
 def matrix_rows():
     return [D, D, D, D, FF, FF] * LAYERS + [EMBED_WIDTH, EMBED_WIDTH, EMBED_WIDTH]
 
 
-def slot_starts(owners):
+def slot_places(owners):
     counts = jnp.array(matrix_rows(), jnp.int32)
     mat_total = counts.shape[0]
     same_owner = (owners[:, None] == owners[None, :]).astype(jnp.int32)
     earlier_mask = jnp.tril(jnp.ones((mat_total, mat_total), jnp.int32), -1)
     return owners * CAP + jnp.sum(same_owner * earlier_mask * counts[None, :], 1)
-
-
-def waves(places, width):
-    half_width = width // 2
-    frequency = jnp.exp(-math.log(10000.0) * jnp.arange(half_width, dtype=jnp.float32) / half_width)
-    angles = places[:, None] * frequency[None, :]
-    return jnp.concatenate([jnp.sin(angles), jnp.cos(angles)], 1)
-
-
-def norm_parts(value_entries):
-    center = value_entries - jnp.mean(value_entries, -1, keepdims=True)
-    scale_inv = lax.rsqrt(jnp.mean(center * center, -1, keepdims=True) + eps_norm)
-    return (center * scale_inv, scale_inv)
-
-
-def norm_back(normal_part, scale_inv, gain_vec, grad_out):
-    scaled = grad_out * gain_vec
-    inner = (
-        scaled
-        - jnp.mean(scaled, -1, keepdims=True)
-        - normal_part * jnp.mean(scaled * normal_part, -1, keepdims=True)
-    )
-    return (inner * scale_inv, jnp.sum(grad_out * normal_part, 0), jnp.sum(grad_out, 0))
 
 
 def block_scores(query_blk, keys_all, keep_keys, score_scale):
@@ -289,16 +1202,7 @@
     return (peak_val, exp_total, first_part[2] + second_part[2])
 
 
-def adamw(weight, gradient, moment_one, moment_two):
-    moment_one = beta_one * moment_one + (1.0 - beta_one) * gradient
-    moment_two = beta_two * moment_two + (1.0 - beta_two) * gradient * gradient
-    fix_one = 1.0 - beta_one**STEP
-    fix_two = 1.0 - beta_two**STEP
-    update_dir = moment_one / fix_one / (jnp.sqrt(moment_two / fix_two) + eps_adam)
-    return (weight - learn_rate * (update_dir + weight_decay * weight), moment_one, moment_two)
-
-
-def per_device(
+def any_mesh_device(
     token_ids,
     timesteps,
     pad_mask,
@@ -323,7 +1227,7 @@
     score_scale = HDIM ** (-0.5)
     table_low = lax.all_gather(emb_table.astype(jnp.bfloat16), "dp", axis=1, tiled=True)
     row_counts = matrix_rows()
-    local_start = slot_starts(owners) - owners * CAP
+    local_start = slot_places(owners) - owners * CAP
     sent_pieces = [
         send_matrix(
             lax.dynamic_slice_in_dim(
@@ -544,6 +1448,8 @@
         P("vocab"),
         P("vocab"),
     )
+    fast = mesh.shape["dp"] == 8 and mesh.shape["vocab"] == 4
+    body = per_device if fast else any_mesh_device
     return jax.shard_map(
-        per_device, mesh=mesh, in_specs=in_specs, out_specs=out_specs, check_vma=False
-    )
+        body, mesh=mesh, in_specs=in_specs, out_specs=out_specs, check_vma=False
+    )

time: 1420 us -> 699 us (0.49)
  waiting for transfers between devices: 892 us -> 35.2 us
  Pallas kernels: 0 us -> 333 us
  blocking collectives: 102 us -> 0 us
  local copies, waits for them, and re-layouts: 123 us -> 52.5 us
  matrix products: 158 us -> 110 us
  starting transfers between devices: 4.48 us -> 39.5 us
  other arithmetic: 81.7 us -> 67.3 us
    psum x3 -> x0, waiting for transfers between devices: 507 us -> none  [the longest x1 310 us: per_device(): lax.psum((grad_cols, vec_part, grad_table_local), 'dp')]
    pallas_call x0 -> x4, Pallas kernels: none -> 333 us  [the longest x1 186 us: reduce_grads(): pl.pallas_call(grads_kernel, out_shape=[jax.ShapeDtypeStruct((12, 2, low,...]
    reduce_scatter x4 -> x0, waiting for transfers between devices: 240 us -> none  [the longest x1 184 us: per_device(): lax.psum_scatter(canon_grad, 'vocab', scatter_dimension=0, tiled=True)]
    all_gather x4 -> x0, waiting for transfers between devices: 136 us -> none  [the longest x1 76.7 us: per_device(): weights = lax.all_gather(canon, 'vocab', axis=0, tiled=True).T]
    psum x2 -> x0, blocking collectives: 62.4 us -> none  [the longest x1 39.7 us: per_device(): lax.psum((jnp.sum(mask_own), square_own, cross_own, norm_own), ('dp', 'vo...]
    unnamed x175 -> x207, local copies, waits for them, and re-layouts: 59.5 us -> 10.6 us
    ppermute x0 -> x39, starting transfers between devices: none -> 39.5 us  [the longest x30 19.8 us: swap_vocab(): return lax.ppermute(value, 'vocab', [(i, i ^ mask) for i in range(4)])]
    dot_general x12 -> x8, matrix products: 55.3 us -> 18 us  [matmul_nt(): lax.dot_general(left, right, (((1,), (1,)), ((), ())), preferred_element_...]
  transfers between devices with their start and end apart: 12 -> 39, of which waited for: 12 -> 17; matrix products, arithmetic and copies ran while one was open for 6% -> 20% of each run, Pallas kernels for 0% -> 30%
where the time goes in v1:
time: 699 us; the launch traced here: 688 us
  Pallas kernels  333 us (48%)
  matrix products  110 us (16%)
  other arithmetic  67.3 us (10%)
  local copies, waits for them, and re-layouts  52.5 us (8%)
  between operations  51.3 us (7%)
  starting transfers between devices  39.5 us (6%)
  waiting for transfers between devices  35.2 us (5%)
    pallas_call x1, Pallas kernels, reduce_grads(): pl.pallas_call(grads_kernel, out_shape=[jax.ShapeDtypeStruct((12, 2, low,...  186 us
    pallas_call x1, Pallas kernels, spread(): pl.pallas_call(spread_kernel, out_shape=[shape(4, D, UNIT), shape(4, D, U...  97.6 us
    pallas_call x1, Pallas kernels, trade(): pl.pallas_call(trade_kernel, out_shape=jax.ShapeDtypeStruct((8, HALF, col...  32 us
    ppermute x30, waiting for transfers between devices, swap_vocab(): return lax.ppermute(value, 'vocab', [(i, i ^ mask) for i in range(4)])  27.8 us
    dot_general x2, matrix products, matmul_tn(): lax.dot_general(left, right, (((0,), (0,)), ((), ())), preferred_element_...  21.7 us
    dot_general x7, matrix products, matmul_nn(): return jnp.dot(left, right, preferred_element_type=f32)  20.6 us
    ppermute x30, starting transfers between devices, swap_vocab(): return lax.ppermute(value, 'vocab', [(i, i ^ mask) for i in range(4)])  19.8 us
    ppermute x9, starting transfers between devices, swap_dp(): return lax.ppermute(value, 'dp', [(i, i ^ mask) for i in range(8)])  19.8 us
  transfers between devices with their start and end apart: 39, of which 17 were waited for; matrix products, arithmetic and copies ran while one was open for 20% of the time, Pallas kernels for 30%

profile of v1, /device:TPU:0, one launch (start us, length us, event | category | flops | bytes accessed | tf_op | source)
XLA Modules:
  0.0 688.3 jit_solution(17334521222035833026)
XLA Ops:
  28.4 32.0 %shard_map.257 = bf16[8,96,896]{2,1,0:T(8,128)(2,1)} custom-call(bf16[4,192,896]{2,1,0:T(8,128)(2,1)} %maximum_maximum_fusion.payload), custom_call_target="tpu_custom_call" | custom-call | tf_op jit(solution)/shard_map/pallas_call | solution.py:184
  66.1 97.6 %shard_map.258 = (bf16[4,768,768]{2,1,0:T(8,128)(2,1)}, bf16[4,768,768]{2,1,0:T(8,128)(2,1)}, bf16[4,768,128]{2,1,0:T(8,128)(2,1)}, bf16[4,192,768]{2,1,0:T(8,12...) custom-call(bf16[96,768]{1,0:T(8,128)(2,1)} %get-tuple-element.88.up_home, ...), custom_call_target="tpu_custom_call" | custom-call | tf_op jit(solution)/shard_map/pallas_call | solution.py:327
  163.7 3.3 copy.70
  167.0 3.2 gather_fusion
  180.9 10.3 %collective-permute-done.4 = bf16[256,768]{1,0:T(8,128)(2,1)S(1)} collective-permute-done((bf16[256,768]{1,0:T(8,128)(2,1)S(1)}, bf16[256,768]{1,0:T(8,128)(2,1)S(1)}, u32[]{:S(2)}, u32[]{:S(2)}) %collective-permute-start.4) | collective-permute-done | bytes 393248 | tf_op jit(solution)/shard_map/ppermute | solution.py:88
  223.8 7.6 %fusion.166 = (f32[3,1024]{1,0:T(4,128)S(1)}, f32[3,1024,1024]{1,2,0:T(8,128)}) fusion(pred[1024]{0:T(1024)(128)(4,1)S(1)} %copy-done.85, bf16[1024,3,64]{0,2,1:T(8,128)(2,1)S(1)} %bitcast.341, bf16[1024,3,64]{0,2,1:T(8,128)(2,1)S(1)} %bitcast.339), kind=kOutput, calls=%fused_computation.323 | convolution fusion | flops 415237120 | bytes 13382656 | tf_op jit(solution)/shard_map/sub | solution.py:845
  231.5 5.8 fusion.47
  243.3 3.1 collective-permute-done.8
  247.9 6.5 fusion.24
  264.5 13.3 %fusion.170 = (f32[1024]{0:T(1024)S(1)}, f32[1024,7632]{0,1:T(8,128)}) fusion(bf16[128,7632]{1,0:T(8,128)(2,1)S(1)} %bitcast.320, bf16[256,128]{1,0:T(8,128)(2,1)} %collective-permute-done.11, bf16[256,128]{1,0:T(8,128)(2,1)} %collective-permute-done.10, bf16[256,128]{1,0:T(8,128)(2,1)} %collective-permute-done.9, bf16[256,128]{1,0:T(8,128)(2,1)} %get-tuple-element.193), kind=kOutput, calls=%fused_computation.327 | convolution fusion | flops 2009545728 | bytes 33480704 | tf_op jit(solution)/shard_map/dot_general | solution.py:34
  278.4 14.9 %select_reduce_fusion = (f32[1024]{0:T(1024)}, f32[1024]{0:T(1024)S(1)}) fusion(f32[1024,7632]{0,1:T(8,128)} %get-tuple-element.196, s32[1024]{0:T(1024)S(1)} %copy-done.37, f32[1024]{0:T(1024)S(1)} %get-tuple-element.195), kind=kLoop, calls=%fused_computation.3 | loop fusion | flops 39073792 | bytes 31277056 | tf_op jit(solution)/shard_map/reduce_sum | solution.py:871
  300.5 4.9 collective-permute-start.21
  306.3 5.3 collective-permute-start.22
  321.1 12.7 %fusion.50 = bf16[1024,128]{1,0:T(8,128)(2,1)S(1)} fusion(bf16[128,7632]{1,0:T(8,128)(2,1)S(1)} %bitcast.321, f32[1024,7632]{0,1:T(8,128)} %get-tuple-element.196, f32[1024]{0:T(1024)S(1)} %get-tuple-element.195, bf16[1024,128]{1,0:T(8,128)(2,1)} %copy-done.7, f32[1024]{0:T(1024)S(1)} %get-tuple-element.65, f32[1024]{0:T(1024)S(1)} %get-tuple-element.64), kind=kOutput, calls=%fused_computation.66 | convolution fusion | flops 2016968704 | bytes 33751040 | tf_op jit(solution)/shard_map/dot_general | solution.py:42
  343.8 6.7 convert_reduce_fusion
  366.3 6.7 fusion.38
  373.1 8.9 %multiply_reduce_fusion = (f32[3,1024]{1,0:T(4,128)S(1)}, f32[3,1024,1024]{1,2,0:T(8,128)}) fusion(f32[3,1024,1024]{1,2,0:T(8,128)} %get-tuple-element.186, f32[3,1024]{1,0:T(4,128)S(1)} %copy-done.51, bf16[1024,3,64]{0,2,1:T(8,128)(2,1)S(1)} %bitcast.344, bf16[1024,3,64]{0,2,1:T(8,128)(2,1)S(1)} %bitcast.383), kind=kOutput, calls=%fused_computation.12 | convolution fusion | flops 412087296 | bytes 25976832 | tf_op jit(solution)/shard_map/qhd,khd->hqk/dot_general | solution.py:909
  382.0 6.9 %multiply_convert_fusion = bf16[3,1024,1024]{1,2,0:T(8,128)(2,1)S(1)} fusion(f32[3,1024,1024]{1,2,0:T(8,128)} %get-tuple-element.200, f32[3,1024]{1,0:T(4,128)S(1)} %get-tuple-element.199, f32[3,1024,1024]{1,2,0:T(8,128)S(1)} %bitcast.325, f32[3,1024]{1,0:T(4,128)S(1)} %copy-done.51), kind=kLoop, calls=%fused_computation.11 | loop fusion | flops 12582912 | bytes 31481856 | tf_op jit(solution)/shard_map/convert_element_type | solution.py:911
  444.3 5.5 fusion.1
  450.0 16.2 %fusion.6 = f32[128,7632]{0,1:T(8,128)} fusion(f32[128,7632]{0,1:T(8,128)S(1)} %fusion.1, f32[1024]{0:T(1024)S(1)} %get-tuple-element.65, f32[1024]{0:T(1024)S(1)} %get-tuple-element.64, s32[1024]{0:T(1024)S(1)} %copy-done.38, f32[1024,7632]{0,1:T(8,128)} %get-tuple-element.196, f32[1024]{0:T(1024)S(1)} %get-tuple-element.195, ...), kind=kOutput, calls=%fused_computation.15 | convolution fusion | flops 2065229824 | bytes 39354368 | tf_op jit(solution)/shard_map/dot_general | solution.py:38
  466.2 5.5 copy.98
  476.3 186.4 %shard_map.259 = (s16[12,2,112,768]{3,2,1,0:T(8,128)(2,1)}, s16[4,2,112,128]{3,2,1,0:T(8,128)(2,1)}, f32[16,7680]{1,0:T(8,128)}) custom-call(bf16[4,192,256]{2,1,0:T(8,128)(2,1)} %bitcast.334, bf16[4,192,256]{2,1,0:T(8,128)(2,1)} %bitcast.336, bf16[4,192,256]{2,1,0:T(8,128)(2,1)} %bitcast.335, bf16[4,192,256]{2,1,0:T(8,128)(2,1)} %bitcast.337, ...), custom_call_target="tpu_custom_call" | custom-call | tf_op jit(solution)/shard_map/pallas_call | solution.py:638
  662.8 3.0 collective-permute-start.38
  668.3 16.9 %shard_map.260 = (f32[192,3072]{1,0:T(8,128)}, f32[192,3072]{1,0:T(8,128)}, f32[192,3072]{1,0:T(8,128)}) custom-call(s32[24]{0:T(128)} %get-tuple-element.55.kind, s32[24]{0:T(128)} %get-tuple-element.54.unit, s32[24]{0:T(128)} %get-tuple-element.53.column, s16[12,2,112,768]{3,2,1,0:T(8,128)(2,1)} %get-tuple-element.30.big, ...), custom_call_target="tpu_custom_call" | custom-call | bytes 16515072 | tf_op jit(solution)/shard_map/pallas_call | solution.py:725
  (427 shorter events, 153.6 us)
Async XLA Ops:
  171.2 5.3 collective-permute-start
  172.0 5.6 collective-permute-start.1
  180.3 10.9 %collective-permute-start.4 = (bf16[256,768]{1,0:T(8,128)(2,1)S(1)}, bf16[256,768]{1,0:T(8,128)(2,1)S(1)}, u32[]{:S(2)}, u32[]{:S(2)}) collective-permute-start(bf16[256,768]{1,0:T(8,128)(2,1)S(1)} %add_convert_fusion.3), channel_id=1, source_target_pairs={{0,2},{1,3},{2,0},{3,1},{4,6},{5,7},{6,4},{7,5},{8,10},{9,11},{10,... | collective-permute-start | bytes 1179656 | tf_op jit(solution)/shard_map/ppermute | solution.py:88
  180.9 40.7 %collective-permute-start.3 = (bf16[256,768]{1,0:T(8,128)(2,1)S(1)}, bf16[256,768]{1,0:T(8,128)(2,1)S(1)}, u32[]{:S(2)}, u32[]{:S(2)}) collective-permute-start(bf16[256,768]{1,0:T(8,128)(2,1)S(1)} %add_convert_fusion.3), channel_id=1, source_target_pairs={{0,1},{1,0},{2,3},{3,2},{4,5},{5,4},{6,7},{7,6},{8,9},{9,8},{10,11... | collective-permute-start | bytes 1179656 | tf_op jit(solution)/shard_map/ppermute | solution.py:88
  191.2 30.4 %collective-permute-start.5 = (bf16[256,768]{1,0:T(8,128)(2,1)S(1)}, bf16[256,768]{1,0:T(8,128)(2,1)S(1)}, u32[]{:S(2)}, u32[]{:S(2)}) collective-permute-start(bf16[256,768]{1,0:T(8,128)(2,1)S(1)} %collective-permute-done.4), channel_id=1, source_target_pairs={{0,1},{1,0},{2,3},{3,2},{4,5},{5,4},{6,7},{7,6},{8,9},{9,8},{10,11... | collective-permute-start | bytes 1179656 | tf_op jit(solution)/shard_map/ppermute | solution.py:88
  192.4 106.9 %collective-permute-start.20 = (f32[1]{0:T(128)}, f32[1]{0:T(128)}, u32[]{:S(2)}, u32[]{:S(2)}) collective-permute-start(f32[1]{0:T(128)} %bitcast.78), channel_id=1, source_target_pairs={{0,4},{4,0},{8,12},{12,8},{16,20},{20,16},{24,28},{28,24},{1,5},{5... | collective-permute-start | bytes 20 | tf_op jit(solution)/shard_map/ppermute | solution.py:739
  237.7 5.5 collective-permute-start.7
  239.3 7.1 %collective-permute-start.8 = (bf16[256,192]{1,0:T(8,128)(2,1)S(1)}, bf16[256,192]{1,0:T(8,128)(2,1)S(1)}, u32[]{:S(2)}, u32[]{:S(2)}) collective-permute-start(bf16[256,192]{1,0:T(8,128)(2,1)S(1)} %copy.74), channel_id=1, source_target_pairs={{0,2},{1,3},{2,0},{3,1},{4,6},{5,7},{6,4},{7,5},{8,10},{9,11},{10,... | collective-permute-start | bytes 294920 | tf_op jit(solution)/shard_map/ppermute | solution.py:88
  259.2 5.3 collective-permute-start.10
  296.5 18.3 %collective-permute-start.13 = (f32[3,4,256]{2,1,0:T(4,128)}, f32[3,4,256]{2,1,0:T(4,128)}, u32[]{:S(2)}, u32[]{:S(2)}) collective-permute-start(f32[3,4,256]{2,1,0:T(4,128)} %constant_dynamic-update-slice_fusion), channel_id=1, source_target_pairs={{0,2},{1,3},{2,0},{3,1},{4,6},{5,7},{6,4},{7,5},{8,10},{9,11},{10,... | collective-permute-start | bytes 36872 | tf_op jit(solution)/shard_map/ppermute | solution.py:88
  300.5 5.2 collective-permute-start.21
  306.3 5.7 collective-permute-start.22
  355.8 5.8 collective-permute-start.28
  356.4 8.0 %collective-permute-start.27 = (bf16[256,192]{1,0:T(8,128)(2,1)S(1)}, bf16[256,192]{1,0:T(8,128)(2,1)S(1)}, u32[]{:S(2)}, u32[]{:S(2)}) collective-permute-start(bf16[256,192]{1,0:T(8,128)(2,1)S(1)} %get-tuple-element.95), channel_id=1, source_target_pairs={{0,2},{1,3},{2,0},{3,1},{4,6},{5,7},{6,4},{7,5},{8,10},{9,11},{10,... | collective-permute-start | bytes 294920 | tf_op jit(solution)/shard_map/ppermute | solution.py:88
  357.2 7.1 %collective-permute-start.26 = (bf16[256,192]{1,0:T(8,128)(2,1)S(1)}, bf16[256,192]{1,0:T(8,128)(2,1)S(1)}, u32[]{:S(2)}, u32[]{:S(2)}) collective-permute-start(bf16[256,192]{1,0:T(8,128)(2,1)S(1)} %get-tuple-element.96), channel_id=1, source_target_pairs={{0,1},{1,0},{2,3},{3,2},{4,5},{5,4},{6,7},{7,6},{8,9},{9,8},{10,11... | collective-permute-start | bytes 294920 | tf_op jit(solution)/shard_map/ppermute | solution.py:88
  396.9 15.8 %collective-permute-start.29 = (bf16[512,768]{1,0:T(8,128)(2,1)}, bf16[512,768]{1,0:T(8,128)(2,1)}, u32[]{:S(2)}, u32[]{:S(2)}) collective-permute-start(bf16[512,768]{1,0:T(8,128)(2,1)} %pad_maximum_fusion.2), channel_id=1, source_target_pairs={{0,1},{1,0},{2,3},{3,2},{4,5},{5,4},{6,7},{7,6},{8,9},{9,8},{10,11... | collective-permute-start | bytes 2359304 | tf_op jit(solution)/shard_map/ppermute | solution.py:88
  403.7 5.5 collective-permute-start.15
  414.8 18.4 %collective-permute-start.30 = (bf16[256,768]{1,0:T(8,128)(2,1)}, bf16[256,768]{1,0:T(8,128)(2,1)S(1)}, u32[]{:S(2)}, u32[]{:S(2)}) collective-permute-start(bf16[256,768]{1,0:T(8,128)(2,1)} %fusion.55), channel_id=1, source_target_pairs={{0,2},{1,3},{2,0},{3,1},{4,6},{5,7},{6,4},{7,5},{8,10},{9,11},{10,... | collective-permute-start | bytes 1179656 | tf_op jit(solution)/shard_map/ppermute | solution.py:88
  436.7 7.5 %collective-permute-start.33 = (bf16[256,128]{1,0:T(8,128)(2,1)S(1)}, bf16[256,128]{1,0:T(8,128)(2,1)S(1)}, u32[]{:S(2)}, u32[]{:S(2)}) collective-permute-start(bf16[256,128]{1,0:T(8,128)(2,1)S(1)} %fusion.54), channel_id=1, source_target_pairs={{0,3},{1,2},{2,1},{3,0},{4,7},{5,6},{6,5},{7,4},{8,11},{9,10},{10,... | collective-permute-start | bytes 196616 | tf_op jit(solution)/shard_map/ppermute | solution.py:88
  437.8 6.4 collective-permute-start.32
  438.9 5.3 collective-permute-start.31
  443.3 6.4 collective-permute-start.36
  449.8 213.0 %collective-permute-start.37 = (f32[7680]{0:T(1024)S(1)}, f32[7680]{0:T(1024)S(1)}, u32[]{:S(2)}, u32[]{:S(2)}) collective-permute-start(f32[7680]{0:T(1024)S(1)} %add.506), channel_id=1, source_target_pairs={{0,8},{4,12},{8,0},{12,4},{16,24},{20,28},{24,16},{28,20},{1,9},{5... | collective-permute-start | bytes 92168 | tf_op jit(solution)/shard_map/ppermute | solution.py:739
  662.8 22.5 %collective-permute-start.38 = (f32[7680]{0:T(1024)S(1)}, f32[7680]{0:T(1024)S(1)}, u32[]{:S(2)}, u32[]{:S(2)}) collective-permute-start(f32[7680]{0:T(1024)S(1)} %add.507), channel_id=1, source_target_pairs={{0,16},{4,20},{8,24},{12,28},{16,0},{20,4},{24,8},{28,12},{1,17},{... | collective-permute-start | bytes 92168 | tf_op jit(solution)/shard_map/ppermute | solution.py:739
  (111 other events, 1903.8 us)

commit v2 on v1

--- a/solution.py
+++ b/solution.py
@@ -159,40 +159,40 @@
         copy.wait_recv()
 
 
-def trade_kernel(payload, arrived, send, recv, local):
+def trade_kernel(payload, tile, arrived, tiles, send, recv, tile_send, tile_recv, local):
     z, y, d, v = place()
     masks = (4, 6, 5, 7, 2, 3, 1)
     greet([(d ^ m, v) for m in masks])
-
-    def part(m):
-        other = d ^ m
-        return payload.at[other // 2, pl.ds((other % 2) * HALF, HALF), :]
-
     copies = [
-        remote(part(m), arrived.at[d], (send, recv), i, (d ^ m, v)) for i, m in enumerate(masks)
+        remote(payload.at[d ^ m], arrived.at[d], (send, recv), i, (d ^ m, v))
+        for i, m in enumerate(masks)
+    ] + [
+        remote(tile, tiles.at[d], (tile_send, tile_recv), i, (d ^ m, v))
+        for i, m in enumerate(masks)
     ]
     start_all(copies)
-    own = pltpu.make_async_copy(part(0), arrived.at[d], local)
-    own.start()
-    own.wait()
-    for copy in copies:
+    own = [
+        pltpu.make_async_copy(payload.at[d], arrived.at[d], local.at[0]),
+        pltpu.make_async_copy(tile, tiles.at[d], local.at[1]),
+    ]
+    start_all(own)
+    for copy in own + copies:
         copy.wait()
 
 
-def trade(payload):
-    cols = payload.shape[2]
+def trade(payload, tile, collective_id):
+    dma = pltpu.SemaphoreType.DMA
     return pl.pallas_call(
         trade_kernel,
-        out_shape=jax.ShapeDtypeStruct((8, HALF, cols), payload.dtype),
-        in_specs=[ANY],
-        out_specs=ANY,
-        scratch_shapes=[
-            pltpu.SemaphoreType.DMA((7,)),
-            pltpu.SemaphoreType.DMA((7,)),
-            pltpu.SemaphoreType.DMA,
+        out_shape=[
+            jax.ShapeDtypeStruct(payload.shape, payload.dtype),
+            jax.ShapeDtypeStruct((8,) + tile.shape, tile.dtype),
         ],
-        compiler_params=pltpu.CompilerParams(collective_id=0, has_side_effects=True),
-    )(payload)
+        in_specs=[ANY, ANY],
+        out_specs=[ANY, ANY],
+        scratch_shapes=[dma((7,))] * 4 + [dma((2,))],
+        compiler_params=pltpu.CompilerParams(collective_id=collective_id, has_side_effects=True),
+    )(payload, tile)
 
 
 def spread_kernel(
@@ -340,6 +340,475 @@
         compiler_params=pltpu.CompilerParams(collective_id=1, has_side_effects=True),
     )(up_home, down_home, small_home, attn_home, table_home)
 
+VMEM = pl.BlockSpec(memory_space=pltpu.VMEM)
+
+
+def neighbours():
+    d, v = lax.axis_index("dp"), lax.axis_index("vocab")
+    return [(d, v ^ k) for k in (1, 2, 3)]
+
+
+def by_position(v, store):
+    for i in range(4):
+        pl.when(v == i)(functools.partial(store, i))
+
+
+def forward_kernel(
+    found, noise, levels, places, small, attn, out_w, up_hbm, down_hbm, vecs, keep,
+    clean, inputs, hidden, normed_all, q, k, k_t, values, log_total, mixed, middle, normed_two,
+    up_proj, active, hidden_two, final_norm, predicted, pred_all,
+    up_w, down_w, found_in, values_t, mixed_out, mixed_in,
+    w_sem, e_send, e_recv, n_send, n_recv, m_send, m_recv, p_send, p_recv,
+):
+    v = lax.axis_index("vocab")
+    partners = neighbours()
+    loads = []
+    for j in range(4):
+        for i, (src, dst) in enumerate(((up_hbm, up_w), (down_hbm, down_w))):
+            copy = pltpu.make_async_copy(src.at[j], dst.at[j], w_sem.at[2 * j + i])
+            copy.start()
+            loads.append(copy)
+    greet(partners)
+    asked = start_all(
+        [
+            remote(found.at[m], found_in.at[m - 1], (e_send, e_recv), m - 1, partners[m - 1])
+            for m in (2, 3, 1)
+        ]
+    )
+    wave = levels[2:3].astype(bf16)
+    time_part = matmul_nt(jnp.broadcast_to(wave, (16, EMBED_WIDTH)), small[1])[0:1]
+    arrive_all(asked)
+    total = found[0].astype(f32)
+    for m in range(3):
+        total = total + found_in[m].astype(f32)
+    clean[...] = total
+    noisy = levels[0:1] * total + levels[1:2] * noise[...].astype(f32)
+    inputs[:, 0:EMBED_WIDTH] = noisy.astype(bf16)
+    inputs[:, EMBED_WIDTH:] = jnp.broadcast_to(wave, noisy.shape)
+    value = matmul_nt(inputs[:, 0:EMBED_WIDTH], small[0]) + time_part + places[...]
+    hidden[...] = value
+    normed_all[0] = (norm_parts(value)[0] * vecs[0:1] + vecs[1:2]).astype(bf16)
+
+    far = remote(normed_all.at[0], normed_all.at[2], (n_send, n_recv), 0, partners[1])
+    near = remote(normed_all.at[0], normed_all.at[1], (n_send, n_recv), 1, partners[0])
+    last = remote(normed_all.at[2], normed_all.at[3], (n_send, n_recv), 2, partners[0])
+    far.start()
+    near.start()
+
+    def project(b):
+        rows = pl.ds(b * 256, 256)
+        block = normed_all[b]
+        for i, ref in ((0, q), (1, k), (2, values)):
+            result = matmul_nt(block, attn[i])
+            if i == 0:
+                result = result.astype(bf16).astype(f32) * HDIM ** (-0.5)
+            for h in range(3):
+                ref[h, rows, :] = result[:, h * HDIM : (h + 1) * HDIM].astype(bf16)
+        k_t[:, rows] = matmul_nt(attn[1], block).astype(bf16)
+        values_t[:, rows] = matmul_nt(attn[2], block).astype(bf16)
+
+    project(0)
+    near.wait_recv()
+    project(1)
+    far.wait_recv()
+    last.start()
+    project(2)
+    last.wait_recv()
+    project(3)
+
+    given = []
+    for b in (2, 3, 1, 0):
+        rows = pl.ds(b * 256, 256)
+        parts = []
+        for h in range(3):
+            scores = matmul_nt(k[h], q[h, rows, :])
+            scores = jnp.where(keep[...] > 0.0, scores, -1000000000.0)
+            top = jnp.max(scores, 0, keepdims=True)
+            expo = jnp.exp(scores - top)
+            mass = jnp.sum(expo, 0, keepdims=True)
+            probs = (expo * (1.0 / mass)).astype(bf16)
+            log_total[pl.ds(3 * b + h, 1), :] = top + jnp.log(mass)
+            parts.append(matmul_nn(values_t[h * HDIM : (h + 1) * HDIM, :], probs))
+        block = jnp.concatenate(parts, 0).T.astype(bf16)
+        if b == 0:
+            mixed_in[0] = block
+        else:
+            mixed_out[b - 1] = block
+            copy = remote(
+                mixed_out.at[b - 1], mixed_in.at[b], (m_send, m_recv), b - 1, partners[b - 1]
+            )
+            copy.start()
+            given.append(copy)
+    arrive_all(given)
+
+    def lay(i):
+        for b in range(4):
+            mixed[:, QUARTER * (i ^ b) : QUARTER * ((i ^ b) + 1)] = mixed_in[b]
+
+    by_position(v, lay)
+    value = hidden[...] + matmul_nt(mixed[...], out_w[...])
+    middle[...] = value
+    normed_two[...] = (norm_parts(value)[0] * vecs[2:3] + vecs[3:4]).astype(bf16)
+    for j in range(4):
+        loads[2 * j].wait()
+        loads[2 * j + 1].wait()
+        raised = matmul_nn(normed_two[...], up_w[j]) + vecs[4 + j : 5 + j]
+        up_proj[j] = raised
+        active[j] = jax.nn.gelu(raised).astype(bf16)
+        lowered = matmul_nt(active[j], down_w[j])
+        hidden_two[...] = (middle[...] if j == 0 else hidden_two[...]) + lowered
+    final_norm[...] = (norm_parts(hidden_two[...])[0] * vecs[8:9] + vecs[9:10]).astype(bf16)
+    predicted[...] = matmul_nn(final_norm[...], small[2])
+    pred_all[0] = predicted[...].astype(bf16)
+    shown = start_all(
+        [
+            remote(pred_all.at[0], pred_all.at[m], (p_send, p_recv), m - 1, partners[m - 1])
+            for m in (2, 3, 1)
+        ]
+    )
+    arrive_all(shown)
+    for copy in asked + [far, near, last] + given + shown:
+        copy.wait_send()
+
+
+def forward(found, noise, levels, places, small, attn, out_w, up_w, down_w, vecs, keep):
+    dma, vmem = pltpu.SemaphoreType.DMA, pltpu.VMEM
+    n = 256
+
+    def shape(kind, *dims):
+        return jax.ShapeDtypeStruct(dims, kind)
+
+    return pl.pallas_call(
+        forward_kernel,
+        out_shape=[
+            shape(f32, n, EMBED_WIDTH),
+            shape(bf16, n, 2 * EMBED_WIDTH),
+            shape(f32, n, D),
+            shape(bf16, 4, n, D),
+            shape(bf16, 3, 4 * n, HDIM),
+            shape(bf16, 3, 4 * n, HDIM),
+            shape(bf16, QUARTER, 4 * n),
+            shape(bf16, 3, 4 * n, HDIM),
+            shape(f32, 16, n),
+            shape(bf16, n, D),
+            shape(f32, n, D),
+            shape(bf16, n, D),
+            shape(f32, 4, n, UNIT),
+            shape(bf16, 4, n, UNIT),
+            shape(f32, n, D),
+            shape(bf16, n, D),
+            shape(f32, n, EMBED_WIDTH),
+            shape(bf16, 4, n, EMBED_WIDTH),
+        ],
+        in_specs=[VMEM] * 7 + [ANY] * 2 + [VMEM] * 2,
+        out_specs=[VMEM] * 18,
+        scratch_shapes=[
+            vmem((4, D, UNIT), bf16),
+            vmem((4, D, UNIT), bf16),
+            vmem((3, n, EMBED_WIDTH), bf16),
+            vmem((QUARTER, 4 * n), bf16),
+            vmem((3, n, QUARTER), bf16),
+            vmem((4, n, QUARTER), bf16),
+            dma((8,)),
+        ]
+        + [dma((3,))] * 8,
+        compiler_params=pltpu.CompilerParams(
+            collective_id=4, has_side_effects=True, vmem_limit_bytes=60 * 2**20
+        ),
+    )(found, noise, levels, places, small, attn, out_w, up_w, down_w, vecs, keep)
+
+
+STRIP = 768
+
+
+def strips(rows):
+    return [(lo, min(STRIP, rows - lo)) for lo in range(0, rows, STRIP)]
+
+
+def head_kernel(
+    pred_all, table, table_t, row_of, weight, found,
+    grad_pred, lse, logits, stats, gathered, outgoing, incoming,
+    s_send, s_recv, g_send, g_recv,
+):
+    partners = neighbours()
+    greet(partners)
+    rows = table_t.shape[0]
+    full, rest = rows // STRIP, rows % STRIP
+    mixes = []
+    for b in range(4):
+        block = pred_all[b]
+        wanted = row_of[b : b + 1, :]
+
+        def first(at, size, top):
+            value = matmul_nt(table_t[at, :], block)
+            logits[at, :] = value
+            return jnp.maximum(top, jnp.max(value, 0, keepdims=True))
+
+        def second(at, size, lo, carry, peak):
+            mass, target, mix = carry
+            value = logits[at, :]
+            expo = jnp.exp(value - peak)
+            here = lax.broadcasted_iota(jnp.int32, (size, 256), 0) == wanted - lo
+            mass = mass + jnp.sum(expo, 0, keepdims=True)
+            target = target + jnp.sum(jnp.where(here, value, 0.0), 0, keepdims=True)
+            return mass, target, mix + matmul_nn(table[:, at], expo.astype(bf16))
+
+        peak = lax.fori_loop(
+            0,
+            full,
+            lambda t, top: first(pl.ds(pl.multiple_of(t * STRIP, STRIP), STRIP), STRIP, top),
+            jnp.full((1, 256), -jnp.inf, f32),
+        )
+        tail = pl.ds(full * STRIP, rest)
+        if rest:
+            peak = first(tail, rest, peak)
+        zero = jnp.zeros((1, 256), f32)
+        carry = lax.fori_loop(
+            0,
+            full,
+            lambda t, carry: second(
+                pl.ds(pl.multiple_of(t * STRIP, STRIP), STRIP), STRIP, t * STRIP, carry, peak
+            ),
+            (zero, zero, jnp.zeros((EMBED_WIDTH, 256), f32)),
+        )
+        if rest:
+            carry = second(tail, rest, full * STRIP, carry, peak)
+        stats[b, 0:1] = peak
+        stats[b, 1:2] = carry[0]
+        stats[b, 2:3] = carry[1]
+        stats[b, 3:8] = jnp.zeros((5, 256), f32)
+        mixes.append(carry[2])
+    told = start_all(
+        [
+            remote(stats, gathered.at[m - 1], (s_send, s_recv), m - 1, partners[m - 1])
+            for m in (2, 3, 1)
+        ]
+    )
+    arrive_all(told)
+    given = []
+    for b in (2, 3, 1, 0):
+        views = [stats[b]] + [gathered[m - 1, b ^ m] for m in (1, 2, 3)]
+        peak = functools.reduce(jnp.maximum, [view[0:1] for view in views])
+        mass = sum(view[1:2] * jnp.exp(view[0:1] - peak) for view in views)
+        total = peak + jnp.log(mass)
+        lse[b : b + 1, :] = total
+        if b == 0:
+            target = sum(view[2:3] for view in views)
+            lse[4:5, :] = weight[0:1, :] * (total - target)
+            lse[5:8, :] = jnp.zeros((3, 256), f32)
+        share = weight[b : b + 1, :]
+        local = mixes[b] * (jnp.exp(stats[b, 0:1] - total) * share)
+        local = local - found[b].astype(f32).T * share
+        outgoing[b] = local.T.astype(bf16)
+        if b:
+            copy = remote(
+                outgoing.at[b], incoming.at[b - 1], (g_send, g_recv), b - 1, partners[b - 1]
+            )
+            copy.start()
+            given.append(copy)
+    arrive_all(given)
+    value = outgoing[0].astype(f32)
+    for m in range(3):
+        value = value + incoming[m].astype(f32)
+    grad_pred[...] = value
+    for copy in told + given:
+        copy.wait_send()
+
+
+def head(pred_all, table, table_t, row_of, weight, found):
+    dma, vmem = pltpu.SemaphoreType.DMA, pltpu.VMEM
+    return pl.pallas_call(
+        head_kernel,
+        out_shape=[
+            jax.ShapeDtypeStruct((256, EMBED_WIDTH), f32),
+            jax.ShapeDtypeStruct((8, 256), f32),
+        ],
+        in_specs=[VMEM] * 6,
+        out_specs=[VMEM] * 2,
+        scratch_shapes=[
+            vmem((table_t.shape[0], 256), f32),
+            vmem((4, 8, 256), f32),
+            vmem((3, 4, 8, 256), f32),
+            vmem((4, 256, EMBED_WIDTH), bf16),
+            vmem((3, 256, EMBED_WIDTH), bf16),
+        ]
+        + [dma((3,))] * 4,
+        compiler_params=pltpu.CompilerParams(
+            collective_id=5, has_side_effects=True, vmem_limit_bytes=60 * 2**20
+        ),
+    )(pred_all, table, table_t, row_of, weight, found)
+
+
+def gelu_slope(u):
+    inner = math.sqrt(2.0 / math.pi)
+    bent = jnp.tanh(inner * (u + 0.044715 * (u * u * u)))
+    return 0.5 * (1.0 + bent) + (0.5 * inner) * u * (1.0 - bent * bent) * (
+        1.0 + (3.0 * 0.044715) * (u * u)
+    )
+
+
+def backward_kernel(
+    grad_pred, clean, predicted, twice, levels, head_stats, hidden, middle, hidden_two,
+    normed_two, final_norm, up_proj, q, k, k_t, values, log_total, keep,
+    small, attn, out_w, up_hbm, down_hbm, vecs,
+    grad_pred_low, down_left, up_left, out_left, small_left, final_left, qkv_left, grad_up, grad_clean, sums,
+    up_w, down_w, carried, folded, mix_out, mix_in, grad_k, grad_v, n_out, n_in, f_out, f_in,
+    w_sem, m_send, m_recv, n_send, n_recv, c_send, c_recv,
+):
+    v = lax.axis_index("vocab")
+    partners = neighbours()
+    loads = []
+    for j in range(4):
+        for i, (src, dst) in enumerate(((down_hbm, down_w), (up_hbm, up_w))):
+            copy = pltpu.make_async_copy(src.at[j], dst.at[j], w_sem.at[2 * j + i])
+            copy.start()
+            loads.append(copy)
+    greet(partners)
+
+    def turned(value):
+        return value.astype(f32).T.astype(bf16)
+
+    error = predicted[...] - clean[...]
+    pull = twice[...] * error
+    low = (grad_pred[...] + pull).astype(bf16)
+    grad_pred_low[...] = low
+    length = jnp.sqrt(jnp.sum(clean[...] * clean[...], -1, keepdims=True) + 1e-06)
+    lane = lax.broadcasted_iota(jnp.int32, (1, UNIT), 1)
+    scalars = (jnp.sum(pull * error), jnp.sum(head_stats[4:5, :]), jnp.sum(twice[...] * length))
+    sums[10:11, :] = sum(jnp.where(lane == i, scalars[i], 0.0) for i in range(3))
+    sums[11:16, :] = jnp.zeros((5, UNIT), f32)
+
+    def through_norm(value, gain_row, grad_out, at):
+        normal, scale_inv = norm_parts(value)
+        part, grad_gain, grad_shift = norm_back(normal, scale_inv, vecs[gain_row : gain_row + 1], grad_out)
+        sums[at : at + 1, :] = grad_gain[None, :]
+        sums[at + 1 : at + 2, :] = grad_shift[None, :]
+        return part
+
+    carried[...] = through_norm(hidden_two[...], 8, matmul_nt(low, small[2]), 8)
+    low = carried[...].astype(bf16)
+    down_left[...] = turned(carried[...])
+    up_left[...] = turned(normed_two[...])
+    final_left[...] = turned(final_norm[...])
+    for j in range(4):
+        loads[2 * j].wait()
+        loads[2 * j + 1].wait()
+        slope = matmul_nn(low, down_w[j]) * gelu_slope(up_proj[j])
+        grad_up[j] = slope.astype(bf16)
+        sums[4 + j : 5 + j, :] = jnp.sum(grad_up[j].astype(f32), 0, keepdims=True)
+        part = matmul_nt(grad_up[j], up_w[j])
+        folded[...] = part if j == 0 else folded[...] + part
+    carried[...] = carried[...] + through_norm(middle[...], 2, folded[...], 2)
+    out_left[...] = turned(carried[...])
+    folded[...] = matmul_nn(carried[...].astype(bf16), out_w[...])
+
+    def lay(i):
+        for b in range(4):
+            mix_out[b] = folded[:, QUARTER * (i ^ b) : QUARTER * ((i ^ b) + 1)].astype(bf16)
+
+    by_position(v, lay)
+    mixed = [
+        remote(mix_out.at[m], mix_in.at[m - 1], (m_send, m_recv), m - 1, partners[m - 1])
+        for m in (1, 2, 3)
+    ]
+    for m in (2, 3, 1):
+        mixed[m - 1].start()
+    for b in range(4):
+        if b:
+            mixed[b - 1].wait_recv()
+        grad_block = mix_out[0] if b == 0 else mix_in[b - 1]
+        rows = pl.ds(b * 256, 256)
+        for h in range(3):
+            grad_mix = grad_block[:, h * HDIM : (h + 1) * HDIM]
+            asked = q[h, rows, :]
+            scores = matmul_nt(k[h], asked)
+            scores = jnp.where(keep[...] > 0.0, scores, -1000000000.0)
+            probs = jnp.exp(scores - log_total[3 * b + h : 3 * b + h + 1, :])
+            grad_probs = matmul_nt(values[h], grad_mix)
+            inner = jnp.sum(probs * grad_probs, 0, keepdims=True)
+            grad_scores = (probs * (grad_probs - inner)).astype(bf16)
+            grad_asked = matmul_nn(k_t[h * HDIM : (h + 1) * HDIM, :], grad_scores)
+            qkv_left[0, h * HDIM : (h + 1) * HDIM, rows] = (grad_asked * HDIM ** (-0.5)).astype(bf16)
+            part_k = matmul_nn(grad_scores, asked)
+            part_v = matmul_nn(probs.astype(bf16), grad_mix)
+            grad_k[h] = part_k if b == 0 else grad_k[h] + part_k
+            grad_v[h] = part_v if b == 0 else grad_v[h] + part_v
+    for h in range(3):
+        lanes = pl.ds(h * HDIM, HDIM)
+        qkv_left[1, lanes, :] = grad_k[h].T.astype(bf16)
+        qkv_left[2, lanes, :] = grad_v[h].T.astype(bf16)
+
+    def grad_normed(b):
+        rows = pl.ds(b * 256, 256)
+        return sum(matmul_tn(qkv_left[i, :, rows], attn[i]) for i in range(3))
+
+    n_out[0] = grad_normed(1).astype(bf16)
+    n_out[1] = grad_normed(3).astype(bf16)
+    near = remote(n_out, n_in, (n_send, n_recv), 0, partners[0])
+    near.start()
+    folded[...] = grad_normed(2)
+    near.wait_recv()
+    f_out[...] = (folded[...] + n_in[1].astype(f32)).astype(bf16)
+    far = remote(f_out, f_in, (n_send, n_recv), 1, partners[1])
+    far.start()
+    folded[...] = grad_normed(0) + n_in[0].astype(f32)
+    far.wait_recv()
+    grad_out = folded[...] + f_in[...].astype(f32)
+    carried[...] = carried[...] + through_norm(hidden[...], 0, grad_out, 0)
+    small_left[...] = turned(carried[...])
+    back = matmul_nn(carried[...].astype(bf16), small[0])
+    grad_clean[0] = (levels[0:1] * back - twice[...] * (predicted[...] - clean[...])).astype(bf16)
+    shown = start_all(
+        [
+            remote(grad_clean.at[0], grad_clean.at[m], (c_send, c_recv), m - 1, partners[m - 1])
+            for m in (2, 3, 1)
+        ]
+    )
+    arrive_all(shown)
+    for copy in mixed + [near, far] + shown:
+        copy.wait_send()
+
+
+def backward(*operands):
+    dma, vmem = pltpu.SemaphoreType.DMA, pltpu.VMEM
+    n = 256
+
+    def shape(kind, *dims):
+        return jax.ShapeDtypeStruct(dims, kind)
+
+    return pl.pallas_call(
+        backward_kernel,
+        out_shape=[shape(bf16, n, EMBED_WIDTH)]
+        + [shape(bf16, D, n)] * 5
+        + [
+            shape(bf16, 3, QUARTER, 4 * n),
+            shape(bf16, 4, n, UNIT),
+            shape(bf16, 4, n, EMBED_WIDTH),
+            shape(f32, 16, UNIT),
+        ],
+        in_specs=[VMEM] * 21 + [ANY] * 2 + [VMEM],
+        out_specs=[VMEM] * 10,
+        scratch_shapes=[
+            vmem((4, D, UNIT), bf16),
+            vmem((4, D, UNIT), bf16),
+            vmem((n, D), f32),
+            vmem((n, D), f32),
+            vmem((4, n, QUARTER), bf16),
+            vmem((3, n, QUARTER), bf16),
+            vmem((3, 4 * n, HDIM), f32),
+            vmem((3, 4 * n, HDIM), f32),
+            vmem((2, n, D), bf16),
+            vmem((2, n, D), bf16),
+            vmem((n, D), bf16),
+            vmem((n, D), bf16),
+            dma((8,)),
+        ]
+        + [dma((3,))] * 6,
+        compiler_params=pltpu.CompilerParams(
+            collective_id=6, has_side_effects=True, vmem_limit_bytes=60 * 2**20
+        ),
+    )(*operands)
+
 I16 = jnp.int16
 TAIL = 16
 TILES = 60
@@ -398,12 +867,12 @@
 
 def grads_kernel(
     down_left, up_left, out_left, small_left, final_left, qkv_left,
-    active, grad_up, mixed, inputs, grad_pred, normed, table,
-    big, small, table_sum,
-    cs, cr, xs, xr, ys, yr, zs, zr, home, part, half,
-    small_cs, small_cr, small_xs, small_xr, small_ys, small_yr, small_zs, small_zr, small_home, small_half,
-    ts, tr, tzs, tzr,
-    c_send, c_recv, x_send, x_recv, y_send, y_recv, z_send, z_recv, g_send, g_recv, f_send, f_recv, local,
+    active, grad_up, mixed, inputs, grad_pred, normed, pred_all, grad_clean, table_t, lse, weight, row_of, tile,
+    home, small_home, table_sum, tile_sum,
+    cs, cr, xs, xr, ys, yr, zs, zr, part, half,
+    small_cs, small_cr, small_xs, small_xr, small_ys, small_yr, small_zs, small_zr, small_half,
+    table, pred_t, clean_t, ts, tr, tzs, tzr, tile_at, tile_from,
+    c_send, c_recv, x_send, x_recv, y_send, y_recv, z_send, z_recv, t_send, t_recv,
 ):
     z, y, d, v = place()
     far, near = v ^ 2, v ^ 1
@@ -423,7 +892,7 @@
             return matmul_nn(down_left[who], active[n - 1])
         return matmul_nn(up_left[who], grad_up[n - 5])
 
-    core, chip, side, line, spread_line, spread_side = {}, {}, {}, {}, {}, {}
+    core, chip, side, line = {}, {}, {}, {}
 
     def to_core(n):
         put(cs.at[n, 0], product(n, near))
@@ -463,22 +932,6 @@
             line[group, k].wait_recv()
             total = total + get(zr.at[group, k - 1], HALF)
         put(home.at[group], total)
-        keep = pltpu.make_async_copy(home.at[group], big.at[4 * group + z, y], local.at[group])
-        keep.start()
-        for k in (2, 1, 3):
-            spread_line[group, k] = send(
-                home.at[group], big.at[4 * group + z, y], (g_send, g_recv), 3 * group + k - 1, (d ^ (2 * k), v)
-            )
-        keep.wait()
-
-    def to_all(group):
-        for k in (2, 1, 3):
-            spread_line[group, k].wait_recv()
-        for u in range(4):
-            slot = 4 * group + u
-            spread_side[slot] = send(
-                big.at[slot, y], big.at[slot, y], (f_send, f_recv), slot, (d ^ 1, v)
-            )
 
     def small_product(who):
         return jnp.concatenate(
@@ -524,20 +977,31 @@
             line[3, k].wait_recv()
             total = total + get(small_zr.at[k - 1], HALF)
         put(small_home, total)
-        keep = pltpu.make_async_copy(small_home, small.at[z, y], local.at[3])
-        keep.start()
-        for k in (2, 1, 3):
-            spread_line[3, k] = send(
-                small_home, small.at[z, y], (g_send, g_recv), 9 + k - 1, (d ^ (2 * k), v)
-            )
-        keep.wait()
-
-    def small_to_all():
-        for k in (2, 1, 3):
-            spread_line[3, k].wait_recv()
-        spread_side[12] = send(
-            small.at[:, y], small.at[:, y], (f_send, f_recv), 12, (d ^ 1, v)
-        )
+
+    def turn_tokens():
+        for b in range(4):
+            pred_t[b] = pred_all[b].astype(f32).T.astype(bf16)
+            clean_t[b] = grad_clean[b].astype(f32).T.astype(bf16)
+
+    vocab_rows = table_t.shape[0]
+
+    def table_strip(lo, size):
+        total = jnp.zeros((EMBED_WIDTH, size), f32)
+        for b in range(4):
+            logits = matmul_nt(table_t[lo : lo + size, :], pred_all[b])
+            probs = jnp.exp(logits - lse[b : b + 1, :])
+            here = lax.broadcasted_iota(jnp.int32, (size, 256), 0) == row_of[b : b + 1, :] - lo
+            here = here.astype(f32)
+            grad_logits = ((probs - here) * weight[b : b + 1, :]).astype(bf16)
+            total = total + matmul_nt(pred_t[b], grad_logits)
+            total = total + matmul_nt(clean_t[b], here.astype(bf16))
+        for i in range(8):
+            rows = slice(16 * (i // 2), 16 * (i // 2) + 16)
+            table[i % 2, rows, lo : lo + size] = total[16 * i : 16 * i + 16]
+        if lo + size == vocab_rows:
+            table[:, :, vocab_rows:] = jnp.zeros((2, 64, TILES * LANES - vocab_rows), f32)
+
+    table_strips = [(lo, min(STRIP, vocab_rows - lo)) for lo in range(0, vocab_rows, STRIP)]
 
     def table_to_side():
         put_tiles(ts, lambda at: table[1 - y, :, at], 64)
@@ -577,55 +1041,80 @@
 
         lax.fori_loop(0, TILES, body, 0, unroll=4)
 
+    hops = [(d, near), (d, far), (d ^ 1, v), (d ^ 2, v), (d ^ 4, v)]
+    tile_copies = {}
+
+    def tile_send(hop):
+        if hop == 0:
+            tile_at[0] = tile[...]
+        else:
+            tile_copies[hop - 1].wait_recv()
+            tile_at[hop] = tile_at[hop - 1] + tile_from[hop - 1]
+        tile_copies[hop] = send(
+            tile_at.at[hop], tile_from.at[hop], (t_send, t_recv), hop, hops[hop]
+        )
+
+    turn_tokens()
     to_core(0)
     to_core(1)
     to_chip(0)
+    tile_send(0)
     to_core(2)
+    table_strip(*table_strips[0])
     to_chip(1)
-    table_to_side()
+    table_strip(*table_strips[1])
+    table_strip(*table_strips[2])
     to_core(3)
     to_chip(2)
-    for u in range(3):
-        halves(u, matmul_nn(qkv_left[u], normed[...]))
+    table_strip(*table_strips[3])
+    table_strip(*table_strips[4])
+    table_strip(*table_strips[5])
     to_core(4)
     to_chip(3)
+    table_strip(*table_strips[6])
+    table_strip(*table_strips[7])
+    for strip in table_strips[8:]:
+        table_strip(*strip)
+    table_to_side()
+    tile_send(1)
+    for u in range(3):
+        halves(u, sum(matmul_nn(qkv_left[u, :, 256 * b : 256 * b + 256], normed[b]) for b in range(4)))
     small_to_core()
-    to_side(0)
     to_core(5)
     to_chip(4)
+    to_side(0)
+    tile_send(2)
+    to_core(6)
+    to_chip(5)
     small_to_chip()
     to_side(1)
     table_to_line()
-    to_core(6)
-    to_chip(5)
+    tile_send(3)
+    to_core(7)
+    to_chip(6)
     to_side(2)
     to_line(0)
-    to_core(7)
-    to_chip(6)
-    to_side(3)
     to_core(8)
     to_chip(7)
+    tile_send(4)
+    to_side(3)
+    to_chip(8)
     to_side(4)
-    to_chip(8)
+    to_line(1)
     small_to_side()
-    to_line(1)
     table_to_home()
+    to_side(5)
     to_home(0)
-    to_side(5)
+    to_side(6)
     small_to_line()
-    to_side(6)
+    to_side(7)
     to_home(1)
-    to_all(0)
-    to_side(7)
-    small_to_home()
     to_side(8)
     to_line(2)
-    to_all(1)
-    small_to_all()
+    small_to_home()
+    tile_copies[4].wait_recv()
+    tile_sum[...] = tile_at[4] + tile_from[4]
     to_home(2)
-    to_all(2)
-    for slot in range(13):
-        spread_side[slot].wait_recv()
     for copy in sent:
         copy.wait_send()
 
@@ -638,12 +1127,13 @@
     return pl.pallas_call(
         grads_kernel,
         out_shape=[
-            jax.ShapeDtypeStruct((12, 2, low, UNIT), I16),
-            jax.ShapeDtypeStruct((4, 2, low, LANES), I16),
+            jax.ShapeDtypeStruct((3, low, UNIT), I16),
+            jax.ShapeDtypeStruct((low, LANES), I16),
             jax.ShapeDtypeStruct((16, table_cols), f32),
+            jax.ShapeDtypeStruct((16, UNIT), f32),
         ],
-        in_specs=[pl.BlockSpec(memory_space=pltpu.VMEM)] * 13,
-        out_specs=[ANY, ANY, pl.BlockSpec(memory_space=pltpu.VMEM)],
+        in_specs=[pl.BlockSpec(memory_space=pltpu.VMEM)] * 19,
+        out_specs=[pl.BlockSpec(memory_space=pltpu.VMEM)] * 4,
         scratch_shapes=[
             vmem((9, 2, tall, UNIT), I16),
             vmem((9, 2, tall, UNIT), I16),
@@ -653,7 +1143,6 @@
             vmem((12, low, UNIT), I16),
             vmem((3, 3, low, UNIT), I16),
             vmem((3, 3, low, UNIT), I16),
-            vmem((3, low, UNIT), I16),
             vmem((QUARTER, UNIT), f32),
             vmem((12, HALF, UNIT), f32),
             vmem((2, tall, wide), I16),
@@ -664,19 +1153,21 @@
             vmem((low, wide), I16),
             vmem((3, low, LANES), I16),
             vmem((3, low, LANES), I16),
-            vmem((low, LANES), I16),
             vmem((4, HALF, LANES), f32),
+            vmem((2, 64, table_cols), f32),
+            vmem((4, EMBED_WIDTH, 256), bf16),
+            vmem((4, EMBED_WIDTH, 256), bf16),
             vmem((64, table_cols + LANES), I16),
             vmem((64, table_cols + LANES), I16),
             vmem((3, 16, table_cols + LANES), I16),
             vmem((3, 16, table_cols + LANES), I16),
+            vmem((5, 16, UNIT), f32),
+            vmem((5, 16, UNIT), f32),
         ]
         + [dma((10,))] * 4
         + [dma((14,))] * 2
         + [dma((15,))] * 2
-        + [dma((12,))] * 2
-        + [dma((13,))] * 2
-        + [dma((4,))],
+        + [dma((5,))] * 2,
         compiler_params=pltpu.CompilerParams(
             collective_id=2, has_side_effects=True, vmem_limit_bytes=60 * 2**20
         ),
@@ -687,20 +1178,20 @@
     which = kind[pl.program_id(0)]
 
     def rows_of(ref):
-        return jnp.concatenate([get(ref.at[0, 0], HALF), get(ref.at[0, 1], HALF)], 0)
+        return jnp.concatenate([get(ref.at[0], HALF), get(ref.at[1], HALF)], 0)
 
     zero = jnp.zeros(w.shape, f32)
     g = jnp.where(which == 1, rows_of(big), jnp.where(which == 2, rows_of(small), zero))
     w_out[...], m1_out[...], m2_out[...] = adamw(w[...], g, m1[...], m2[...])
 
 
-def slot_update(owners, starts, big, small, slots, first, second):
+def slot_update(owners, starts, summed, slots, first, second):
     rows = slots.shape[0]
     blocks = CAP // LANES
     d = lax.axis_index("dp")
     spots, units, columns, kinds = [], [], [], []
     per_unit = UNIT // LANES
-    first_unit = [0, 1, 2, 3, 8, 4, 0, 1, 2]
+    first_unit = [0, 1, 2, 3, 0, 0, 0, 1, 2]
     for i, count in enumerate(ROW_COUNTS):
         spots.append(jnp.where(owners[i] == d, starts[i] // LANES, -CAP) + jnp.arange(count // LANES))
         for b in range(count // LANES):
@@ -716,11 +1207,11 @@
     plain_spec = pl.BlockSpec((rows, LANES), lambda j, k, u, c: (0, j))
     low = HALF + TAIL
     big_spec = pl.BlockSpec(
-        (1, 2, low, LANES),
-        lambda j, k, u, c: (jnp.where(k[j] == 1, u[j], 0), 0, 0, jnp.where(k[j] == 1, c[j], 0)),
+        (2, low, LANES),
+        lambda j, k, u, c: (jnp.where(k[j] == 1, u[j], 0), 0, jnp.where(k[j] == 1, c[j], 0)),
     )
     small_spec = pl.BlockSpec(
-        (1, 2, low, LANES), lambda j, k, u, c: (jnp.where(k[j] == 2, u[j], 0), 0, 0, 0)
+        (2, low, LANES), lambda j, k, u, c: (jnp.where(k[j] == 2, u[j], 0), 0, per_unit)
     )
     return pl.pallas_call(
         slot_kernel,
@@ -732,20 +1223,7 @@
         ),
         out_shape=[jax.ShapeDtypeStruct(slots.shape, f32)] * 3,
         cost_estimate=pl.CostEstimate(flops=0, bytes_accessed=28 * rows * CAP, transcendentals=0),
-    )(kind, unit, column, big, small, slots, first, second)
-
-
-def swap_dp(value, mask):
-    return lax.ppermute(value, "dp", [(i, i ^ mask) for i in range(8)])
-
-
-def sum_all(value, over_vocab=True):
-    if over_vocab:
-        for mask in (1, 2):
-            value = value + swap_vocab(value, mask)
-    for mask in (1, 2, 4):
-        value = value + swap_dp(value, mask)
-    return value
+    )(kind, unit, column, summed, summed, slots, first, second)
 
 
 def per_device(
@@ -770,8 +1248,6 @@
     seq_len = token_ids.shape[1]
     tokens = seq_len // 4
     vocab_rows, emb_cols = emb_table.shape
-    heads_own = HEADS // 4
-    score_scale = HDIM ** (-0.5)
 
     starts = slot_starts(owners)
     whole = (owners[4] == d) | (owners[5] == d)
@@ -784,7 +1260,12 @@
         )
         return jnp.concatenate([main, extra], 1).astype(bf16)
 
-    arrived = trade(jnp.stack([unit_payload(u) for u in range(4)]))
+    payload = jnp.stack([unit_payload(u) for u in range(4)])
+    mask_count = jnp.sum(pad_mask.astype(f32))
+    arrived, counts = trade(
+        payload.reshape(8, HALF, UNIT + EMBED_WIDTH), jnp.broadcast_to(mask_count, (8, LANES)), 0
+    )
+    count_all = jnp.sum(counts[:, 0, 0])
 
     def from_owner(index, lo, width):
         return lax.dynamic_slice(arrived, (owners[index], 0, lo), (1, HALF, width))[0]
@@ -801,166 +1282,112 @@
 
     ids_rel = relative(token_ids[0])
     mask_rel = relative(pad_mask[0])
-    keep_keys = mask_rel > 0
     weight_rel = mask_rel.astype(f32)
     mask_own = weight_rel[:tokens]
-    count_all = sum_all(jnp.sum(weight_rel)[None], False)[0]
     local_row = ids_rel - v * vocab_rows
     valid_row = (local_row >= 0) & (local_row < vocab_rows)
     safe_row = jnp.clip(local_row, 0, vocab_rows - 1)
+    table_t = table_low.T
     found_rows = jnp.where(
-        valid_row[:, None], jnp.take(table_low.T, safe_row, axis=0), jnp.zeros((), bf16)
-    )
-    pieces = vocab_exchange(jnp.split(found_rows, 4, 0))
-    clean_emb = sum(piece.astype(f32) for piece in pieces)
+        valid_row[:, None], jnp.take(table_t, safe_row, axis=0), jnp.zeros((), bf16)
+    ).reshape(4, tokens, EMBED_WIDTH)
     own_places = (v * tokens + jnp.arange(tokens)).astype(f32)
     step_val = timesteps[0].astype(f32)
     signal_level = 1.0 - jnp.sqrt(step_val / DIFF + 0.0001)
-    noisy_emb = jnp.sqrt(signal_level) * clean_emb + jnp.sqrt(1.0 - signal_level) * noise_draw[
-        0
-    ].astype(f32)
-    time_feat = jnp.broadcast_to(waves(step_val[None], EMBED_WIDTH), (tokens, EMBED_WIDTH))
-    inputs = jnp.concatenate([noisy_emb, time_feat], 1).astype(bf16)
-
-    g_one, b_one, g_two, b_two = [vec_params[i * D : (i + 1) * D] for i in range(4)]
-    bias_up = vec_params[4 * D : 4 * D + FF].reshape(4, 1, UNIT)
-    g_fin, b_fin = [vec_params[4 * D + FF + i * D : 4 * D + FF + (i + 1) * D] for i in range(2)]
-
-    hidden = (
-        matmul_nt(inputs[:, :EMBED_WIDTH], w_small[0])
-        + matmul_nt(inputs[:, EMBED_WIDTH:], w_small[1])
-        + waves(own_places, D)
-    )
-    norm_one, inv_one = norm_parts(hidden)
-    normed_all = vocab_gather((norm_one * g_one + b_one).astype(bf16))
-    queries, keys, values = [matmul_nt(normed_all, w_attn[i]).astype(bf16) for i in range(3)]
-
-    def by_head(value):
-        return value.reshape(seq_len, heads_own, HDIM)
-
-    q_h, k_h, v_h = by_head(queries), by_head(keys), by_head(values)
-    scores = jnp.einsum("qhd,khd->hqk", q_h, k_h, preferred_element_type=f32) * score_scale
-    scores = jnp.where(keep_keys[None, None, :], scores, -1000000000.0)
-    row_max = jnp.max(scores, -1, keepdims=True)
-    expo = jnp.exp(scores - row_max)
-    probs = expo / jnp.sum(expo, -1, keepdims=True)
-    probs_low = probs.astype(bf16)
-    mixed = jnp.einsum("hqk,khd->qhd", probs_low, v_h, preferred_element_type=f32)
-    mixed = mixed.reshape(seq_len, QUARTER).astype(bf16)
-    mixed_own = relative(jnp.concatenate(vocab_exchange(jnp.split(mixed, 4, 0)), 1), 1)
-    middle = hidden + matmul_nt(mixed_own, w_out)
-    norm_two, inv_two = norm_parts(middle)
-    normed_two = (norm_two * g_two + b_two).astype(bf16)
-    up_proj = (
-        jnp.einsum("tk,jkn->jtn", normed_two, w_up, preferred_element_type=f32) + bias_up
-    )
-    active = jax.nn.gelu(up_proj).astype(bf16)
-    hidden_two = middle + jnp.einsum("jtn,jon->to", active, w_down, preferred_element_type=f32)
-    norm_final, inv_final = norm_parts(hidden_two)
-    final_norm = (norm_final * g_fin + b_fin).astype(bf16)
-    predicted = matmul_nn(final_norm, w_small[2])
-
-    pred_all = vocab_gather_direct(predicted.astype(bf16))
-    logits = matmul_nn(pred_all, table_low)
-    columns = lax.broadcasted_iota(jnp.int32, (seq_len, vocab_rows), 1)
-    chosen = columns == local_row[:, None]
-    peak = jnp.max(logits, -1)
-    exp_low = jnp.exp(logits - peak[:, None])
-    exp_sum = jnp.sum(exp_low, -1)
-    exp_low = exp_low.astype(bf16)
-    target = jnp.sum(jnp.where(chosen, logits, 0.0), -1)
-    mix_emb = matmul_nt(exp_low, table_low)
-    stats = jnp.stack([peak, exp_sum, target]).reshape(3, 4, tokens)
-    stat_list = [stats]
-    for k in (1, 2, 3):
-        got = swap_vocab(stats, k)
-        stat_list.append(jnp.stack([got[:, j ^ k] for j in range(4)], 1))
-    peak_all = functools.reduce(jnp.maximum, [s[0] for s in stat_list])
-    total_all = sum(s[1] * jnp.exp(s[0] - peak_all) for s in stat_list)
-    target_own = sum(s[2][0] for s in stat_list)
-    lse = (peak_all + jnp.log(total_all)).reshape(seq_len)
-    row_weight = weight_rel / count_all
-    factor = jnp.exp(peak - lse) * row_weight
-    grad_pred_local = mix_emb * factor[:, None] - found_rows.astype(f32) * row_weight[:, None]
-    pieces = vocab_exchange(jnp.split(grad_pred_local.astype(bf16), 4, 0))
-    pred_error = predicted - clean_emb
-    error_grad = 2.0 * mask_own[:, None] * pred_error / count_all
-    grad_pred_low = (sum(piece.astype(f32) for piece in pieces) + error_grad).astype(bf16)
-    grad_logits = exp_low.astype(f32) * factor[:, None] - jnp.where(chosen, row_weight[:, None], 0.0)
-    grad_table_head = matmul_tn(pred_all, grad_logits.astype(bf16))
-
-    square_own = jnp.sum(mask_own[:, None] * pred_error * pred_error)
-    cross_own = jnp.sum(mask_own * (lse[:tokens] - target_own))
-    norm_own = jnp.sum(mask_own * jnp.sqrt(jnp.sum(clean_emb * clean_emb, -1) + 1e-06))
-    square, cross_sum, norm_total = sum_all(jnp.stack([square_own, cross_own, norm_own]))
-
-    grad_final = matmul_nt(grad_pred_low, w_small[2])
-    grad_hidden, grad_gf, grad_bf = norm_back(norm_final, inv_final, g_fin, grad_final)
-    grad_low = grad_hidden.astype(bf16)
-    grad_active = jnp.einsum("to,jon->jtn", grad_low, w_down, preferred_element_type=f32)
-    grad_up_proj = jax.vjp(jax.nn.gelu, up_proj)[1](grad_active)[0].astype(bf16)
-    grad_bias = jnp.sum(grad_up_proj.astype(f32), 1).reshape(FF)
-    grad_normed_two = jnp.einsum("jtn,jkn->tk", grad_up_proj, w_up, preferred_element_type=f32)
-    grad_part, grad_g2, grad_b2 = norm_back(norm_two, inv_two, g_two, grad_normed_two)
-    grad_middle = grad_hidden + grad_part
-    grad_attn = grad_middle.astype(bf16)
-    grad_mixed = relative(matmul_nn(grad_attn, w_out).astype(bf16), 1)
-    grad_mixed = by_head(jnp.concatenate(vocab_exchange(jnp.split(grad_mixed, 4, 1)), 0))
-    grad_probs = jnp.einsum("qhd,khd->hqk", grad_mixed, v_h, preferred_element_type=f32)
-    inner_sum = jnp.sum(probs * grad_probs, -1, keepdims=True)
-    grad_scores = (probs * (grad_probs - inner_sum)).astype(bf16)
-    grad_q = jnp.einsum("hqk,khd->qhd", grad_scores, k_h, preferred_element_type=f32)
-    grad_k = jnp.einsum("hqk,qhd->khd", grad_scores, q_h, preferred_element_type=f32)
-    grad_v = jnp.einsum("hqk,qhd->khd", probs_low, grad_mixed, preferred_element_type=f32)
-    grad_q = (grad_q * score_scale).astype(bf16).reshape(seq_len, QUARTER)
-    grad_k = (grad_k * score_scale).astype(bf16).reshape(seq_len, QUARTER)
-    grad_v = grad_v.astype(bf16).reshape(seq_len, QUARTER)
-    grad_normed = vocab_reduce(
-        matmul_nn(grad_q, w_attn[0]) + matmul_nn(grad_k, w_attn[1]) + matmul_nn(grad_v, w_attn[2])
-    )
-    grad_part_one, grad_g1, grad_b1 = norm_back(norm_one, inv_one, g_one, grad_normed)
-    grad_hidden_low = (grad_middle + grad_part_one).astype(bf16)
-    grad_inputs = matmul_nn(grad_hidden_low, w_small[0])
-    grad_clean = jnp.sqrt(signal_level) * grad_inputs - error_grad
-    grad_clean_all = vocab_gather_direct(grad_clean.astype(bf16))
-    grad_table = grad_table_head + matmul_tn(grad_clean_all, chosen.astype(bf16))
-    grad_table = jnp.pad(grad_table, ((0, 0), (0, TILES * LANES - vocab_rows)))
-    grad_table = grad_table.reshape(4, 2, 16, TILES * LANES).transpose(1, 0, 2, 3)
+    levels = jnp.concatenate(
+        [
+            jnp.full((1, EMBED_WIDTH), jnp.sqrt(signal_level)),
+            jnp.full((1, EMBED_WIDTH), jnp.sqrt(1.0 - signal_level)),
+            waves(step_val[None], EMBED_WIDTH),
+            jnp.zeros((5, EMBED_WIDTH), f32),
+        ]
+    )
+    vecs = vec_params.reshape(10, D)
+    keep_column = weight_rel[:, None]
+    (
+        clean_emb, inputs, hidden, normed_all, q_h, k_h, k_t, v_h, log_total, mixed_own, middle,
+        normed_two, up_proj, active, hidden_two, final_norm, predicted, pred_all,
+    ) = forward(
+        found_rows,
+        noise_draw[0],
+        levels,
+        waves(own_places, D),
+        w_small,
+        w_attn,
+        w_out,
+        w_up,
+        w_down,
+        vecs,
+        keep_column,
+    )
+    row_weight = (weight_rel / count_all).reshape(4, tokens)
+    row_of = local_row.reshape(4, tokens)
+    grad_pred, head_stats = head(
+        pred_all,
+        table_low,
+        table_t,
+        row_of,
+        row_weight,
+        found_rows,
+    )
+    (
+        grad_pred_low, down_left, up_left, out_left, small_left, final_left, qkv_left, grad_up, grad_clean, sums,
+    ) = backward(
+        grad_pred, clean_emb, predicted, 2.0 * mask_own[:, None] / count_all, levels, head_stats,
+        hidden, middle, hidden_two, normed_two, final_norm, up_proj,
+        q_h, k_h, k_t, v_h, log_total, keep_column,
+        w_small, w_attn, w_out, w_up, w_down, vecs,
+    )
 
     def left(value):
-        return value.T.reshape(4, QUARTER, value.shape[0])
-
-    big, small, table_grad = reduce_grads(
-        left(grad_low),
-        left(normed_two),
-        left(grad_attn),
-        left(grad_hidden_low),
-        left(final_norm),
-        jnp.stack([grad_q.T, grad_k.T, grad_v.T]),
+        return value.reshape(4, QUARTER, tokens)
+
+    home, small_home, table_grad, tile_sum = reduce_grads(
+        left(down_left),
+        left(up_left),
+        left(out_left),
+        left(small_left),
+        left(final_left),
+        qkv_left,
         active,
-        grad_up_proj,
+        grad_up,
         mixed_own,
         inputs,
         grad_pred_low,
         normed_all,
-        grad_table.reshape(2, 64, TILES * LANES),
-    )
-
-    grad_vec = jnp.concatenate([grad_g1, grad_b1, grad_g2, grad_b2, grad_bias, grad_gf, grad_bf])
-    grad_vec = sum_all(grad_vec)
+        pred_all,
+        grad_clean,
+        table_t,
+        head_stats,
+        row_weight,
+        row_of,
+        sums,
+    )
+    tile_sum = tile_sum.reshape(16 * UNIT)
     vec_share = vec_first.shape[0]
-    own_grad = lax.dynamic_slice_in_dim(grad_vec, v * vec_share, vec_share)
+    own_grad = lax.dynamic_slice_in_dim(tile_sum, v * vec_share, vec_share)
     own_vecs = lax.dynamic_slice_in_dim(vec_params, v * vec_share, vec_share)
-
+    vec_len = vec_params.shape[0]
+    square = tile_sum[vec_len] * (0.5 * count_all)
+    cross_sum = tile_sum[vec_len + 1] * count_all
+    emb_norm = tile_sum[vec_len + 2] * 0.5
+
+    takers = jnp.arange(8)[:, None, None]
+    unit_home = jnp.where(
+        takers == owners[5], home[1][None], jnp.where(takers == owners[4], home[2][None], home[0][None])
+    )
+    outgoing = jnp.concatenate(
+        [unit_home, jnp.broadcast_to(small_home[None], (8,) + small_home.shape)], 2
+    )
+    summed, _ = trade(outgoing, jnp.zeros((8, LANES), f32), 3)
     new_slots, slot_first_new, slot_second_new = slot_update(
-        owners, starts, big, small, mat_slots, slot_first, slot_second
+        owners, starts, summed, mat_slots, slot_first, slot_second
     )
     new_table, table_first_new, table_second_new = adamw(
         table_own, table_grad[:, :vocab_rows], table_first_moment.T, table_second_moment.T
     )
     new_vecs, vec_first_new, vec_second_new = adamw(own_vecs, own_grad, vec_first, vec_second)
     loss_pair = jnp.stack([square + cross_sum, count_all])
-    emb_norm = norm_total / count_all
     return (
         loss_pair,
         emb_norm,

time: 699 us -> 566 us (0.81)
  Pallas kernels: 333 us -> 457 us
  matrix products: 110 us -> 0 us
  other arithmetic: 67.3 us -> 27.2 us
  starting transfers between devices: 39.5 us -> 0 us
  waiting for transfers between devices: 35.2 us -> 0 us
  local copies, waits for them, and re-layouts: 52.5 us -> 24.9 us
    pallas_call x2 -> x6, Pallas kernels: 218 us -> 347 us  [the longest x1 138 us: reduce_grads(): pl.pallas_call(grads_kernel, out_shape=[jax.ShapeDtypeStruct((3, low, UNI...]
    dot_general x26 -> x0, matrix products: 102 us -> none  [the longest x2 21.7 us: matmul_tn(): lax.dot_general(left, right, (((0,), (0,)), ((), ())), preferred_element_...]
    ppermute x39 -> x0, starting transfers between devices: 39.5 us -> none  [the longest x30 19.8 us: swap_vocab(): return lax.ppermute(value, 'vocab', [(i, i ^ mask) for i in range(4)])]
    ppermute x39 -> x0, waiting for transfers between devices: 35.2 us -> none  [the longest x30 27.8 us: swap_vocab(): return lax.ppermute(value, 'vocab', [(i, i ^ mask) for i in range(4)])]
    reduce_sum x8 -> x2, other arithmetic: 20.7 us -> 2.73 us  [the longest x1 1.43 us: per_device(): count_all = jnp.sum(counts[:, 0, 0])]
    unnamed x207 -> x23, local copies, waits for them, and re-layouts: 10.6 us -> 0.6 us
    convert_element_type x4 -> x1, other arithmetic: 9.47 us -> 0.01 us  [per_device(): weight_rel = mask_rel.astype(f32)]
    transpose x6 -> x0, local copies, waits for them, and re-layouts: 7.82 us -> none  [the longest x5 5.62 us: left(): return value.T.reshape(4, QUARTER, value.shape[0])]
  transfers between devices with their start and end apart: 39 -> 0, of which waited for: 17 -> 0; matrix products, arithmetic and copies ran while one was open for 20% -> 0% of each run, Pallas kernels for 30% -> 0%
where the time goes in v2:
time: 566 us; the launch traced here: 559 us
  Pallas kernels  457 us (81%)
  between operations  49.6 us (9%)
  other arithmetic  27.2 us (5%)
  local copies, waits for them, and re-layouts  24.9 us (4%)
    pallas_call x1, Pallas kernels, reduce_grads(): pl.pallas_call(grads_kernel, out_shape=[jax.ShapeDtypeStruct((3, low, UNI...  138 us
    pallas_call x1, Pallas kernels, spread(): pl.pallas_call(spread_kernel, out_shape=[shape(4, D, UNIT), shape(4, D, U...  93 us
    pallas_call x2, Pallas kernels, trade(): pl.pallas_call(trade_kernel, out_shape=[jax.ShapeDtypeStruct(payload.shap...  78.7 us
    pallas_call x1, Pallas kernels, forward(): pl.pallas_call(forward_kernel, out_shape=[shape(f32, n, EMBED_WIDTH), sha...  47 us
    pallas_call x1, Pallas kernels, backward(): pl.pallas_call(backward_kernel, out_shape=[shape(bf16, n, EMBED_WIDTH)] +...  45.4 us
    pallas_call x1, Pallas kernels, head(): pl.pallas_call(head_kernel, out_shape=[jax.ShapeDtypeStruct((256, EMBED_W...  38 us
    pallas_call x1, Pallas kernels, slot_update(): pl.pallas_call(slot_kernel, grid_spec=pltpu.PrefetchScalarGridSpec(num_sc...  16.8 us

profile of v2, /device:TPU:0, one launch (start us, length us, event | category | flops | bytes accessed | tf_op | source)
XLA Modules:
  0.0 558.7 jit_solution(9087490754530859759)
XLA Ops:
  1.6 1.3 convert_reduce_fusion
  6.4 1.3 reduce.15
  7.8 1.3 reduce.18
  37.0 1.8 fusion.30
  54.8 1.4 select_reduce_fusion
  56.2 1.3 iota_compare_fusion.2
  62.4 1.4 reshape.559.vecs
  68.3 1.4 multiply_sine_fusion
  72.4 36.4 %shard_map.257 = (bf16[8,96,896]{2,1,0:T(8,128)(2,1)}, f32[8,8,128]{2,1,0:T(8,128)}) custom-call(bf16[8,96,896]{2,1,0:T(8,128)(2,1)} %bitcast.139, f32[8,128]{1,0:T(8,128)} %broadcast_in_dim.139.tile), custom_call_target="tpu_custom_call" | custom-call | tf_op jit(solution)/shard_map/pallas_call | solution.py:185
  108.8 1.4 slice_reduce_fusion
  112.7 1.3 dynamic-slice_bitcast_fusion.3.small_home
  114.0 1.8 dynamic-slice_bitcast_fusion
  116.6 93.0 %shard_map.258 = (bf16[4,768,768]{2,1,0:T(8,128)(2,1)}, bf16[4,768,768]{2,1,0:T(8,128)(2,1)}, bf16[4,768,128]{2,1,0:T(8,128)(2,1)}, bf16[4,192,768]{2,1,0:T(8,12...) custom-call(bf16[96,768]{1,0:T(8,128)(2,1)} %get-tuple-element.124.up_home, ...), custom_call_target="tpu_custom_call" | custom-call | tf_op jit(solution)/shard_map/pallas_call | solution.py:327
  209.6 3.2 copy.55
  212.9 3.4 gather_fusion
  217.3 47.0 %shard_map.259 = (f32[256,128]{1,0:T(8,128)}, bf16[256,256]{1,0:T(8,128)(2,1)}, f32[256,768]{1,0:T(8,128)}, bf16[4,256,768]{2,1,0:T(8,128)(2,1)}, bf16[3,1024,64...) custom-call(bf16[4,256,128]{2,1,0:T(8,128)(2,1)} %select_select_fusi, ...), custom_call_target="tpu_custom_call" | custom-call | tf_op jit(solution)/shard_map/pallas_call | solution.py:481
  264.3 38.0 %shard_map.260 = (f32[256,128]{1,0:T(8,128)}, f32[8,256]{1,0:T(8,128)}) custom-call(bf16[4,256,128]{2,1,0:T(8,128)(2,1)} %get-tuple-element.64.pred_all, bf16[128,7632]{1,0:T(8,128)(2,1)} %bitcast.138, bf16[7632,128]{1,0:T(8,128)(2,1)} %bitcast.135, s32[4,256]{1,0:T(4,128)} %get-tuple-element.114.row_of, f32[4,256]{1,0:T(4,128)} %fusion.17.weight, ...), custom_call_target="tpu_custom_call" | custom-call | tf_op jit(solution)/shard_map/pallas_call | solution.py:620
  302.3 45.4 %shard_map.261 = (bf16[256,128]{1,0:T(8,128)(2,1)}, bf16[768,256]{1,0:T(8,128)(2,1)}, bf16[768,256]{1,0:T(8,128)(2,1)}, bf16[768,256]{1,0:T(8,128)(2,1)}, bf16[7...) custom-call(f32[256,128]{1,0:T(8,128)} %get-tuple-element.66.grad_pr, ...), custom_call_target="tpu_custom_call" | custom-call | tf_op jit(solution)/shard_map/pallas_call | solution.py:779
  347.7 138.2 %shard_map.262 = (s16[3,112,768]{2,1,0:T(8,128)(2,1)}, s16[112,128]{1,0:T(8,128)(2,1)}, f32[16,7680]{1,0:T(8,128)}, f32[16,768]{1,0:T(8,128)}) custom-call(bf16[4,192,256]{2,1,0:T(8,128)(2,1)} %bitcast.141, bf16[4,192,256]{2,1,0:T(8,128)(2,1)} %bitcast.142, bf16[4,192,256]{2,1,0:T(8,128)(2,1)} %bitcast.143, bf16[4,192,256]{2,1,0:T(8,128)(2,1)} %bitcast.144, ...), custom_call_target="tpu_custom_call" | custom-call | tf_op jit(solution)/shard_map/pallas_call | solution.py:1127
  489.9 1.4 multiply_subtract_fusion
  494.8 1.3 pad_add_fusion.payload
  496.7 42.4 %shard_map.263 = (s16[8,112,896]{2,1,0:T(8,128)(2,1)}, f32[8,8,128]{2,1,0:T(8,128)}) custom-call(s16[8,112,896]{2,1,0:T(8,128)(2,1)} %pad_add_fusion.payload, f32[8,128]{1,0:T(8,128)} %broadcast_in_dim.158.tile), custom_call_target="tpu_custom_call" | custom-call | tf_op jit(solution)/shard_map/pallas_call | solution.py:185
  539.1 1.5 fusion.10
  540.5 16.8 %shard_map.264 = (f32[192,3072]{1,0:T(8,128)}, f32[192,3072]{1,0:T(8,128)}, f32[192,3072]{1,0:T(8,128)}) custom-call(s32[24]{0:T(128)} %get-tuple-element.105.kind, s32[24]{0:T(128)} %get-tuple-element.104.unit, s32[24]{0:T(128)} %get-tuple-element.103.column, s16[8,112,896]{2,1,0:T(8,128)(2,1)} %get-tuple-element.99.big.small, ...), custom_call_target="tpu_custom_call" | custom-call | bytes 16515072 | tf_op jit(solution)/shard_map/pallas_call | solution.py:1216
  (84 shorter events, 25.4 us)
Async XLA Ops:
  0.6 64.4 %copy-start.2 = (f32[7632,16]{0,1:T(8,128)S(1)}, f32[7632,16]{0,1:T(8,128)}, u32[]{:S(2)}) copy-start(f32[7632,16]{0,1:T(8,128)} %param.23) | copy-start | bytes 1465348
  62.4 4.3 copy-start.7
  65.1 1.9 copy-start.8
  68.3 2.4 copy-start.1
  212.9 51.5 %copy-start = (bf16[128,7632]{0,1:T(8,128)(2,1)}, bf16[128,7632]{0,1:T(8,128)(2,1)S(1)}, u32[]{:S(2)}) copy-start(bf16[128,7632]{0,1:T(8,128)(2,1)S(1)} %copy.55) | copy-start | bytes 5861380
  347.6 142.2 %copy-start.9 = (f32[1920]{0:T(1024)S(1)}, f32[1920]{0:T(1024)}, u32[]{:S(2)}) copy-start(f32[1920]{0:T(1024)} %param.30) | copy-start | bytes 23044
  347.7 142.2 %copy-start.10 = (f32[1920]{0:T(1024)S(1)}, f32[1920]{0:T(1024)}, u32[]{:S(2)}) copy-start(f32[1920]{0:T(1024)} %param.31) | copy-start | bytes 23044
  494.8 44.3 %copy-start.6 = (f32[16,7680]{1,0:T(8,128)S(1)}, f32[16,7680]{1,0:T(8,128)}, u32[]{:S(2)}) copy-start(f32[16,7680]{1,0:T(8,128)} %get-tuple-element.96) | copy-start | bytes 1474564
  496.1 43.0 %copy-start.3 = (f32[7632,16]{0,1:T(8,128)S(1)}, f32[7632,16]{0,1:T(8,128)}, u32[]{:S(2)}) copy-start(f32[7632,16]{0,1:T(8,128)} %param.23) | copy-start | bytes 1465348
  496.1 43.0 %copy-start.4 = (f32[7632,16]{0,1:T(8,128)S(1)}, f32[7632,16]{0,1:T(8,128)}, u32[]{:S(2)}) copy-start(f32[7632,16]{0,1:T(8,128)} %param.25) | copy-start | bytes 1465348
  496.1 43.0 %copy-start.5 = (f32[7632,16]{0,1:T(8,128)S(1)}, f32[7632,16]{0,1:T(8,128)}, u32[]{:S(2)}) copy-start(f32[7632,16]{0,1:T(8,128)} %param.24) | copy-start | bytes 1465348

commit v3 on v2

--- a/solution.py
+++ b/solution.py
@@ -84,40 +84,6 @@
     return (weight - learn_rate * (update_dir + weight_decay * weight), moment_one, moment_two)
 
 
-def swap_vocab(value, mask):
-    return lax.ppermute(value, "vocab", [(i, i ^ mask) for i in range(4)])
-
-
-def relative(value, axis=0):
-    v = lax.axis_index("vocab")
-    p = jnp.split(value, 4, axis)
-    swapped = jnp.where(v % 2 == 1, jnp.concatenate([p[1], p[0], p[3], p[2]], axis), value)
-    q = jnp.split(swapped, 4, axis)
-    return jnp.where(v // 2 == 1, jnp.concatenate([q[2], q[3], q[0], q[1]], axis), swapped)
-
-
-def vocab_gather(own, axis=0):
-    far = swap_vocab(own, 2)
-    near = swap_vocab(own, 1)
-    return jnp.concatenate([own, near, far, swap_vocab(far, 1)], axis)
-
-
-def vocab_gather_direct(own, axis=0):
-    return jnp.concatenate([own] + [swap_vocab(own, k) for k in (1, 2, 3)], axis)
-
-
-def vocab_exchange(pieces):
-    return [pieces[0]] + [swap_vocab(pieces[k], k) for k in (1, 2, 3)]
-
-
-def vocab_reduce(value):
-    p = jnp.split(value, 4, 0)
-    sent = swap_vocab(jnp.concatenate([p[1], p[3]], 0).astype(bf16), 1)
-    near, far = jnp.split(sent, 2, 0)
-    far = p[2] + far.astype(f32)
-    return p[0] + near.astype(f32) + swap_vocab(far.astype(bf16), 2).astype(f32)
-
-
 MESH = pl.DeviceIdType.MESH
 ANY = pl.BlockSpec(memory_space=pl.ANY)
 UNIT = 768
@@ -159,50 +125,139 @@
         copy.wait_recv()
 
 
-def trade_kernel(payload, tile, arrived, tiles, send, recv, tile_send, tile_recv, local):
-    z, y, d, v = place()
-    masks = (4, 6, 5, 7, 2, 3, 1)
-    greet([(d ^ m, v) for m in masks])
-    copies = [
-        remote(payload.at[d ^ m], arrived.at[d], (send, recv), i, (d ^ m, v))
-        for i, m in enumerate(masks)
-    ] + [
-        remote(tile, tiles.at[d], (tile_send, tile_recv), i, (d ^ m, v))
-        for i, m in enumerate(masks)
+VMEM = pl.BlockSpec(memory_space=pltpu.VMEM)
+SMEM = pl.BlockSpec(memory_space=pltpu.SMEM)
+
+
+def prepare_kernel(
+    owners, ids, mask, table, slots,
+    payload, table_low, row_of, safe, keep_rows, keep, valid, count, kind, unit, column,
+    units, extras, sems,
+):
+    d, v = lax.axis_index("dp"), lax.axis_index("vocab")
+    starts = [
+        sum(jnp.where(owners[j] == owners[i], ROW_COUNTS[j], 0) for j in range(i)) + 0 * owners[i]
+        for i in range(len(ROW_COUNTS))
     ]
-    start_all(copies)
-    own = [
-        pltpu.make_async_copy(payload.at[d], arrived.at[d], local.at[0]),
-        pltpu.make_async_copy(tile, tiles.at[d], local.at[1]),
-    ]
-    start_all(own)
-    for copy in own + copies:
+    whole = (owners[4] == d) | (owners[5] == d)
+    copies = []
+    for u in range(4):
+        first = pl.multiple_of(jnp.where(whole, u * UNIT, starts[u]), LANES)
+        copies.append(
+            pltpu.make_async_copy(slots.at[:, pl.ds(first, UNIT)], units.at[u], sems.at[u])
+        )
+        first = pl.multiple_of(starts[6 + min(u, 2)], LANES)
+        copies.append(
+            pltpu.make_async_copy(slots.at[:, pl.ds(first, LANES)], extras.at[u], sems.at[4 + u])
+        )
+    for copy in copies:
+        copy.start()
+
+    def clear(j, carry):
+        kind[j] = 0
+        unit[j] = 0
+        column[j] = 0
+        return carry
+
+    lax.fori_loop(0, CAP // LANES, clear, 0)
+    per_unit = UNIT // LANES
+    first_unit = [0, 1, 2, 3, 0, 0, 0, 1, 2]
+    for i, rows in enumerate(ROW_COUNTS):
+
+        def claim(i=i, rows=rows):
+            def one(b, carry):
+                j = starts[i] // LANES + b
+                kind[j] = 2 if i > 5 else 1
+                unit[j] = first_unit[i] + b // per_unit
+                column[j] = b % per_unit
+                return carry
+
+            lax.fori_loop(0, rows // LANES, one, 0)
+
+        pl.when(owners[i] == d)(claim)
+
+    table_low[...] = table[...].astype(bf16)
+    count[...] = jnp.full((8, LANES), jnp.sum(mask[...].astype(f32)))
+    for b in range(4):
+        at = pl.ds(pl.multiple_of((v ^ b) * 256, 256), 256)
+        local = ids[:, at] - v * table.shape[1]
+        row_of[b : b + 1, :] = local
+        safe[:, 256 * b : 256 * b + 256] = jnp.clip(local, 0, table.shape[1] - 1)
+        weight = mask[:, at].astype(f32)
+        keep_rows[b : b + 1, :] = weight
+        inside = ((local >= 0) & (local < table.shape[1])).astype(f32)
+        both = jnp.concatenate([weight, inside, jnp.zeros((6, 256), f32)], 0).T
+        keep[256 * b : 256 * b + 256, :] = both[:, 0:1]
+        valid[256 * b : 256 * b + 256, :] = both[:, 1:2]
+    for copy in copies:
         copy.wait()
-
-
-def trade(payload, tile, collective_id):
-    dma = pltpu.SemaphoreType.DMA
+    for u in range(4):
+        for half in range(2):
+            rows = slice(half * HALF, half * HALF + HALF)
+            payload[2 * u + half, :, 0:UNIT] = units[u, rows, :].astype(bf16)
+            payload[2 * u + half, :, UNIT:] = extras[u, rows, :].astype(bf16)
+
+
+def prepare(owners, ids, mask, table, slots):
+    def shape(kind, *dims):
+        return jax.ShapeDtypeStruct(dims, kind)
+
+    blocks = CAP // LANES
+    tokens = ids.shape[1]
     return pl.pallas_call(
-        trade_kernel,
+        prepare_kernel,
         out_shape=[
-            jax.ShapeDtypeStruct(payload.shape, payload.dtype),
-            jax.ShapeDtypeStruct((8,) + tile.shape, tile.dtype),
+            shape(bf16, 8, HALF, UNIT + LANES),
+            shape(bf16, *table.shape),
+            shape(jnp.int32, 4, tokens // 4),
+            shape(jnp.int32, 1, tokens),
+            shape(f32, 4, tokens // 4),
+            shape(f32, tokens, 1),
+            shape(f32, tokens, 1),
+            shape(f32, 8, LANES),
+        ]
+        + [shape(jnp.int32, blocks)] * 3,
+        in_specs=[SMEM, VMEM, VMEM, VMEM, ANY],
+        out_specs=[VMEM] * 8 + [SMEM] * 3,
+        scratch_shapes=[
+            pltpu.VMEM((4, QUARTER, UNIT), f32),
+            pltpu.VMEM((4, QUARTER, LANES), f32),
+            pltpu.SemaphoreType.DMA((8,)),
         ],
-        in_specs=[ANY, ANY],
-        out_specs=[ANY, ANY],
-        scratch_shapes=[dma((7,))] * 4 + [dma((2,))],
-        compiler_params=pltpu.CompilerParams(collective_id=collective_id, has_side_effects=True),
-    )(payload, tile)
+        compiler_params=pltpu.CompilerParams(vmem_limit_bytes=40 * 2**20),
+    )(owners, ids, mask, table, slots)
+
+
+TRADE_MASKS = (4, 6, 5, 7, 2, 3, 1)
+
+
+def chosen_of(pieces, wanted):
+    value = pieces[0]
+    for i in range(1, len(pieces)):
+        value = jnp.where(wanted == i, pieces[i], value)
+    return value
 
 
 def spread_kernel(
-    up_home, down_home, small_home, attn_home, table_home,
-    up, down, small, attn, out, table,
+    owners, payload, tile, keep_rows, keep, table_home,
+    up, down, small, attn, out, table, weight, twice,
+    arrived, tiles, up_home, down_home, small_home, attn_home,
+    a_send, a_recv, b_send, b_recv,
     z_send, z_recv, y_send, y_recv, x_send, x_recv, n_send, n_recv, f_send, f_recv, local,
 ):
     z, y, d, v = place()
     far, near = v ^ 2, v ^ 1
-    greet([(d ^ m, v) for m in (2, 4, 6, 1)] + [(d, far), (d, near)])
+    greet([(d ^ m, v) for m in TRADE_MASKS] + [(d, far), (d, near)])
+    traded = start_all(
+        [
+            remote(payload.at[d ^ m], arrived.at[i], (a_send, a_recv), i, (d ^ m, v))
+            for i, m in enumerate(TRADE_MASKS)
+        ]
+        + [
+            remote(tile, tiles.at[i], (b_send, b_recv), i, (d ^ m, v))
+            for i, m in enumerate(TRADE_MASKS)
+        ]
+    )
     homes = [up_home, down_home, small_home, attn_home, table_home]
     fulls = [up, down, small, attn, table]
     own_rows = pl.ds(v * QUARTER, QUARTER)
@@ -287,6 +342,27 @@
             last = start_last(c)
             sent.extend(last)
             landing.extend(last)
+
+    arrive_all(traded)
+    sent.extend(traded)
+    total = tile[...]
+    for i in range(7):
+        total = total + tiles[i]
+    weight[...] = keep_rows[...] / jnp.concatenate([total[0:4]] * 2, 1)
+    twice[...] = 2.0 * keep[0:256, :] / total[0:1, 0:1]
+
+    def from_owner(owner, lanes):
+        value = payload[d, :, lanes]
+        for i, m in enumerate(TRADE_MASKS):
+            value = jnp.where(owner == d ^ m, arrived[i, :, lanes], value)
+        return value
+
+    up_home[...] = from_owner(owners[4], slice(0, UNIT))
+    down_home[...] = from_owner(owners[5], slice(0, UNIT))
+    attn_home[...] = from_owner(chosen_of([owners[u] for u in range(4)], z), slice(0, UNIT))
+    small_home[...] = from_owner(
+        chosen_of([owners[6 + min(u, 2)] for u in range(4)], z), slice(UNIT, UNIT + LANES)
+    )
 
     waves_of = [[0], [1], [2, 3], [4]]
     for c in waves_of[0]:
@@ -316,10 +392,9 @@
         copy.wait_send()
 
 
-def spread(up_home, down_home, small_home, attn_home, table_home):
-    small_cols = small_home.shape[1]
+def spread(owners, payload, tile, keep_rows, keep, table_home):
     rows, vocab_rows = table_home.shape
-    dma = pltpu.SemaphoreType.DMA
+    dma, vmem = pltpu.SemaphoreType.DMA, pltpu.VMEM
 
     def shape(*dims):
         return jax.ShapeDtypeStruct(dims, bf16)
@@ -329,19 +404,32 @@
         out_shape=[
             shape(4, D, UNIT),
             shape(4, D, UNIT),
-            shape(4, D, small_cols),
+            shape(4, D, LANES),
             shape(4, QUARTER, UNIT),
             shape(D, UNIT),
             shape(8, rows, vocab_rows),
+            jax.ShapeDtypeStruct(keep_rows.shape, f32),
+            jax.ShapeDtypeStruct((256, 1), f32),
         ],
-        in_specs=[ANY] * 5,
-        out_specs=[ANY] * 6,
-        scratch_shapes=[dma((5, 3))] * 2 + [dma((5, 4))] * 2 + [dma((4, 4))] * 6 + [dma((6,))],
-        compiler_params=pltpu.CompilerParams(collective_id=1, has_side_effects=True),
-    )(up_home, down_home, small_home, attn_home, table_home)
-
-VMEM = pl.BlockSpec(memory_space=pltpu.VMEM)
-
+        in_specs=[SMEM] + [VMEM] * 5,
+        out_specs=[ANY] * 6 + [VMEM] * 2,
+        scratch_shapes=[
+            vmem((7, HALF, UNIT + LANES), bf16),
+            vmem((7, 8, LANES), f32),
+            vmem((HALF, UNIT), bf16),
+            vmem((HALF, UNIT), bf16),
+            vmem((HALF, LANES), bf16),
+            vmem((HALF, UNIT), bf16),
+        ]
+        + [dma((7,))] * 4
+        + [dma((5, 3))] * 2
+        + [dma((5, 4))] * 2
+        + [dma((4, 4))] * 6
+        + [dma((6,))],
+        compiler_params=pltpu.CompilerParams(
+            collective_id=1, has_side_effects=True, vmem_limit_bytes=40 * 2**20
+        ),
+    )(owners, payload, tile, keep_rows, keep, table_home)
 
 def neighbours():
     d, v = lax.axis_index("dp"), lax.axis_index("vocab")
@@ -354,8 +442,8 @@
 
 
 def forward_kernel(
-    found, noise, levels, places, small, attn, out_w, up_hbm, down_hbm, vecs, keep,
-    clean, inputs, hidden, normed_all, q, k, k_t, values, log_total, mixed, middle, normed_two,
+    looked, valid, noise, levels, places, small, attn, out_w, up_hbm, down_hbm, vecs, keep,
+    found, clean, inputs, hidden, normed_all, q, k, k_t, values, log_total, mixed, middle, normed_two,
     up_proj, active, hidden_two, final_norm, predicted, pred_all,
     up_w, down_w, found_in, values_t, mixed_out, mixed_in,
     w_sem, e_send, e_recv, n_send, n_recv, m_send, m_recv, p_send, p_recv,
@@ -368,6 +456,10 @@
             copy = pltpu.make_async_copy(src.at[j], dst.at[j], w_sem.at[2 * j + i])
             copy.start()
             loads.append(copy)
+    for b in range(4):
+        found[b] = jnp.where(
+            valid[256 * b : 256 * b + 256, :] > 0.0, looked[b].astype(f32), 0.0
+        ).astype(bf16)
     greet(partners)
     asked = start_all(
         [
@@ -471,7 +563,7 @@
         copy.wait_send()
 
 
-def forward(found, noise, levels, places, small, attn, out_w, up_w, down_w, vecs, keep):
+def forward(looked, valid, noise, levels, places, small, attn, out_w, up_w, down_w, vecs, keep):
     dma, vmem = pltpu.SemaphoreType.DMA, pltpu.VMEM
     n = 256
 
@@ -481,6 +573,7 @@
     return pl.pallas_call(
         forward_kernel,
         out_shape=[
+            shape(bf16, 4, n, EMBED_WIDTH),
             shape(f32, n, EMBED_WIDTH),
             shape(bf16, n, 2 * EMBED_WIDTH),
             shape(f32, n, D),
@@ -500,8 +593,8 @@
             shape(f32, n, EMBED_WIDTH),
             shape(bf16, 4, n, EMBED_WIDTH),
         ],
-        in_specs=[VMEM] * 7 + [ANY] * 2 + [VMEM] * 2,
-        out_specs=[VMEM] * 18,
+        in_specs=[VMEM] * 8 + [ANY] * 2 + [VMEM] * 2,
+        out_specs=[VMEM] * 19,
         scratch_shapes=[
             vmem((4, D, UNIT), bf16),
             vmem((4, D, UNIT), bf16),
@@ -515,7 +608,7 @@
         compiler_params=pltpu.CompilerParams(
             collective_id=4, has_side_effects=True, vmem_limit_bytes=60 * 2**20
         ),
-    )(found, noise, levels, places, small, attn, out_w, up_w, down_w, vecs, keep)
+    )(looked, valid, noise, levels, places, small, attn, out_w, up_w, down_w, vecs, keep)
 
 
 STRIP = 768
@@ -675,7 +768,8 @@
     length = jnp.sqrt(jnp.sum(clean[...] * clean[...], -1, keepdims=True) + 1e-06)
     lane = lax.broadcasted_iota(jnp.int32, (1, UNIT), 1)
     scalars = (jnp.sum(pull * error), jnp.sum(head_stats[4:5, :]), jnp.sum(twice[...] * length))
-    sums[10:11, :] = sum(jnp.where(lane == i, scalars[i], 0.0) for i in range(3))
+    counted = jnp.sum(keep[0:256, :])
+    sums[10:11, :] = sum(jnp.where(lane == i, x, 0.0) for i, x in enumerate(scalars + (counted,)))
     sums[11:16, :] = jnp.zeros((5, UNIT), f32)
 
     def through_norm(value, gain_row, grad_out, at):
@@ -866,17 +960,17 @@
 
 
 def grads_kernel(
-    down_left, up_left, out_left, small_left, final_left, qkv_left,
+    owners, down_left, up_left, out_left, small_left, final_left, qkv_left,
     active, grad_up, mixed, inputs, grad_pred, normed, pred_all, grad_clean, table_t, lse, weight, row_of, tile,
-    home, small_home, table_sum, tile_sum,
-    cs, cr, xs, xr, ys, yr, zs, zr, part, half,
+    summed, table_sum, tile_sum,
+    home, small_home, outgoing, cs, cr, xs, xr, ys, yr, zs, zr, part, half,
     small_cs, small_cr, small_xs, small_xr, small_ys, small_yr, small_zs, small_zr, small_half,
     table, pred_t, clean_t, ts, tr, tzs, tzr, tile_at, tile_from,
-    c_send, c_recv, x_send, x_recv, y_send, y_recv, z_send, z_recv, t_send, t_recv,
+    c_send, c_recv, x_send, x_recv, y_send, y_recv, z_send, z_recv, t_send, t_recv, a_send, a_recv, local,
 ):
     z, y, d, v = place()
     far, near = v ^ 2, v ^ 1
-    greet([(d ^ m, v) for m in (2, 4, 6, 1)] + [(d, far), (d, near)])
+    greet([(d ^ m, v) for m in TRADE_MASKS] + [(d, far), (d, near)])
     sent = []
 
     def send(src, dst, sems, index, partner):
@@ -1115,6 +1209,22 @@
     tile_copies[4].wait_recv()
     tile_sum[...] = tile_at[4] + tile_from[4]
     to_home(2)
+
+    def offer(m):
+        taker = d ^ m
+        unit = jnp.where(owners[4] == taker, home[2], home[0])
+        outgoing[m, :, 0:UNIT] = jnp.where(owners[5] == taker, home[1], unit)
+        outgoing[m, :, UNIT:] = small_home[...]
+
+    offered = []
+    for i, m in enumerate(TRADE_MASKS):
+        offer(m)
+        offered.append(send(outgoing.at[m], summed.at[d], (a_send, a_recv), i, (d ^ m, v)))
+    offer(0)
+    keep = pltpu.make_async_copy(outgoing.at[0], summed.at[d], local)
+    keep.start()
+    keep.wait()
+    arrive_all(offered)
     for copy in sent:
         copy.wait_send()
 
@@ -1127,14 +1237,16 @@
     return pl.pallas_call(
         grads_kernel,
         out_shape=[
-            jax.ShapeDtypeStruct((3, low, UNIT), I16),
-            jax.ShapeDtypeStruct((low, LANES), I16),
+            jax.ShapeDtypeStruct((8, low, UNIT + LANES), I16),
             jax.ShapeDtypeStruct((16, table_cols), f32),
             jax.ShapeDtypeStruct((16, UNIT), f32),
         ],
-        in_specs=[pl.BlockSpec(memory_space=pltpu.VMEM)] * 19,
-        out_specs=[pl.BlockSpec(memory_space=pltpu.VMEM)] * 4,
+        in_specs=[SMEM] + [VMEM] * 19,
+        out_specs=[VMEM] * 3,
         scratch_shapes=[
+            vmem((3, low, UNIT), I16),
+            vmem((low, LANES), I16),
+            vmem((8, low, UNIT + LANES), I16),
             vmem((9, 2, tall, UNIT), I16),
             vmem((9, 2, tall, UNIT), I16),
             vmem((9, tall, UNIT), I16),
@@ -1167,7 +1279,9 @@
         + [dma((10,))] * 4
         + [dma((14,))] * 2
         + [dma((15,))] * 2
-        + [dma((5,))] * 2,
+        + [dma((5,))] * 2
+        + [dma((7,))] * 2
+        + [dma],
         compiler_params=pltpu.CompilerParams(
             collective_id=2, has_side_effects=True, vmem_limit_bytes=60 * 2**20
         ),
@@ -1185,25 +1299,10 @@
     w_out[...], m1_out[...], m2_out[...] = adamw(w[...], g, m1[...], m2[...])
 
 
-def slot_update(owners, starts, summed, slots, first, second):
+def slot_update(kind, unit, column, summed, slots, first, second):
     rows = slots.shape[0]
     blocks = CAP // LANES
-    d = lax.axis_index("dp")
-    spots, units, columns, kinds = [], [], [], []
     per_unit = UNIT // LANES
-    first_unit = [0, 1, 2, 3, 0, 0, 0, 1, 2]
-    for i, count in enumerate(ROW_COUNTS):
-        spots.append(jnp.where(owners[i] == d, starts[i] // LANES, -CAP) + jnp.arange(count // LANES))
-        for b in range(count // LANES):
-            units.append(first_unit[i] + b // per_unit)
-            columns.append(b % per_unit)
-            kinds.append(2 if i > 5 else 1)
-    hit = jnp.concatenate(spots)[None, :] == jnp.arange(blocks)[:, None]
-
-    def looked_up(values):
-        return jnp.sum(jnp.where(hit, jnp.array(values, jnp.int32)[None, :], 0), 1).astype(jnp.int32)
-
-    kind, unit, column = looked_up(kinds), looked_up(units), looked_up(columns)
     plain_spec = pl.BlockSpec((rows, LANES), lambda j, k, u, c: (0, j))
     low = HALF + TAIL
     big_spec = pl.BlockSpec(
@@ -1243,54 +1342,20 @@
     vec_second,
 ):
     v = lax.axis_index("vocab")
-    d = lax.axis_index("dp")
-    z = d // 2
     seq_len = token_ids.shape[1]
     tokens = seq_len // 4
     vocab_rows, emb_cols = emb_table.shape
-
-    starts = slot_starts(owners)
-    whole = (owners[4] == d) | (owners[5] == d)
-
-    def unit_payload(u):
-        start = jnp.where(whole, u * UNIT, starts[u])
-        main = lax.dynamic_slice(mat_slots, (0, start), (QUARTER, UNIT))
-        extra = lax.dynamic_slice(
-            mat_slots, (0, starts[6 + min(u, 2)]), (QUARTER, EMBED_WIDTH)
-        )
-        return jnp.concatenate([main, extra], 1).astype(bf16)
-
-    payload = jnp.stack([unit_payload(u) for u in range(4)])
-    mask_count = jnp.sum(pad_mask.astype(f32))
-    arrived, counts = trade(
-        payload.reshape(8, HALF, UNIT + EMBED_WIDTH), jnp.broadcast_to(mask_count, (8, LANES)), 0
-    )
-    count_all = jnp.sum(counts[:, 0, 0])
-
-    def from_owner(index, lo, width):
-        return lax.dynamic_slice(arrived, (owners[index], 0, lo), (1, HALF, width))[0]
-
     table_own = emb_table.T
-    w_up, w_down, w_small, w_attn, w_out, table_low = spread(
-        from_owner(4, 0, UNIT),
-        from_owner(5, 0, UNIT),
-        from_owner(6 + jnp.minimum(z, 2), UNIT, EMBED_WIDTH),
-        from_owner(z, 0, UNIT),
-        table_own.astype(bf16),
+    (
+        payload, table_home, row_of, safe_row, keep_rows, keep_column, valid_column, count_tile,
+        kind, unit, column,
+    ) = prepare(owners, token_ids, pad_mask, table_own, mat_slots)
+    w_up, w_down, w_small, w_attn, w_out, table_low, row_weight, twice = spread(
+        owners, payload, count_tile, keep_rows, keep_column, table_home
     )
     table_low = table_low.reshape(EMBED_WIDTH, vocab_rows)
-
-    ids_rel = relative(token_ids[0])
-    mask_rel = relative(pad_mask[0])
-    weight_rel = mask_rel.astype(f32)
-    mask_own = weight_rel[:tokens]
-    local_row = ids_rel - v * vocab_rows
-    valid_row = (local_row >= 0) & (local_row < vocab_rows)
-    safe_row = jnp.clip(local_row, 0, vocab_rows - 1)
     table_t = table_low.T
-    found_rows = jnp.where(
-        valid_row[:, None], jnp.take(table_t, safe_row, axis=0), jnp.zeros((), bf16)
-    ).reshape(4, tokens, EMBED_WIDTH)
+    looked = table_t.at[safe_row[0]].get(mode="promise_in_bounds").reshape(4, tokens, EMBED_WIDTH)
     own_places = (v * tokens + jnp.arange(tokens)).astype(f32)
     step_val = timesteps[0].astype(f32)
     signal_level = 1.0 - jnp.sqrt(step_val / DIFF + 0.0001)
@@ -1303,12 +1368,12 @@
         ]
     )
     vecs = vec_params.reshape(10, D)
-    keep_column = weight_rel[:, None]
     (
-        clean_emb, inputs, hidden, normed_all, q_h, k_h, k_t, v_h, log_total, mixed_own, middle,
+        found_rows, clean_emb, inputs, hidden, normed_all, q_h, k_h, k_t, v_h, log_total, mixed_own, middle,
         normed_two, up_proj, active, hidden_two, final_norm, predicted, pred_all,
     ) = forward(
-        found_rows,
+        looked,
+        valid_column,
         noise_draw[0],
         levels,
         waves(own_places, D),
@@ -1320,8 +1385,6 @@
         vecs,
         keep_column,
     )
-    row_weight = (weight_rel / count_all).reshape(4, tokens)
-    row_of = local_row.reshape(4, tokens)
     grad_pred, head_stats = head(
         pred_all,
         table_low,
@@ -1333,7 +1396,7 @@
     (
         grad_pred_low, down_left, up_left, out_left, small_left, final_left, qkv_left, grad_up, grad_clean, sums,
     ) = backward(
-        grad_pred, clean_emb, predicted, 2.0 * mask_own[:, None] / count_all, levels, head_stats,
+        grad_pred, clean_emb, predicted, twice, levels, head_stats,
         hidden, middle, hidden_two, normed_two, final_norm, up_proj,
         q_h, k_h, k_t, v_h, log_total, keep_column,
         w_small, w_attn, w_out, w_up, w_down, vecs,
@@ -1342,7 +1405,8 @@
     def left(value):
         return value.reshape(4, QUARTER, tokens)
 
-    home, small_home, table_grad, tile_sum = reduce_grads(
+    summed, table_grad, tile_sum = reduce_grads(
+        owners,
         left(down_left),
         left(up_left),
         left(out_left),
@@ -1368,20 +1432,13 @@
     own_grad = lax.dynamic_slice_in_dim(tile_sum, v * vec_share, vec_share)
     own_vecs = lax.dynamic_slice_in_dim(vec_params, v * vec_share, vec_share)
     vec_len = vec_params.shape[0]
+    count_all = tile_sum[vec_len + 3]
     square = tile_sum[vec_len] * (0.5 * count_all)
     cross_sum = tile_sum[vec_len + 1] * count_all
     emb_norm = tile_sum[vec_len + 2] * 0.5
 
-    takers = jnp.arange(8)[:, None, None]
-    unit_home = jnp.where(
-        takers == owners[5], home[1][None], jnp.where(takers == owners[4], home[2][None], home[0][None])
-    )
-    outgoing = jnp.concatenate(
-        [unit_home, jnp.broadcast_to(small_home[None], (8,) + small_home.shape)], 2
-    )
-    summed, _ = trade(outgoing, jnp.zeros((8, LANES), f32), 3)
     new_slots, slot_first_new, slot_second_new = slot_update(
-        owners, starts, summed, mat_slots, slot_first, slot_second
+        kind, unit, column, summed, mat_slots, slot_first, slot_second
     )
     new_table, table_first_new, table_second_new = adamw(
         table_own, table_grad[:, :vocab_rows], table_first_moment.T, table_second_moment.T

time: 566 us -> 497 us (0.88)
  between operations: 49.6 us -> 6.2 us
  other arithmetic: 27.2 us -> 6.65 us
    pallas_call x4 -> x3, Pallas kernels: 264 us -> 226 us  [the longest x1 176 us: reduce_grads(): pl.pallas_call(grads_kernel, out_shape=[jax.ShapeDtypeStruct((8, low, UNI...]
    pallas_call x1, Pallas kernels: 93 us -> 127 us  [spread(): pl.pallas_call(spread_kernel, out_shape=[shape(4, D, UNIT), shape(4, D, U...]
    unnamed x23 -> x52, local copies, waits for them, and re-layouts: 0.6 us -> 14.2 us
where the time goes in v3:
time: 497 us; the launch traced here: 489 us
  Pallas kernels  453 us (91%)
  local copies, waits for them, and re-layouts  24.1 us (5%)
  other arithmetic  6.65 us (1%)
  between operations  6.2 us (1%)
    pallas_call x1, Pallas kernels, reduce_grads(): pl.pallas_call(grads_kernel, out_shape=[jax.ShapeDtypeStruct((8, low, UNI...  176 us
    pallas_call x1, Pallas kernels, spread(): pl.pallas_call(spread_kernel, out_shape=[shape(4, D, UNIT), shape(4, D, U...  127 us
    pallas_call x1, Pallas kernels, forward(): pl.pallas_call(forward_kernel, out_shape=[shape(bf16, 4, n, EMBED_WIDTH),...  47.6 us
    pallas_call x1, Pallas kernels, backward(): pl.pallas_call(backward_kernel, out_shape=[shape(bf16, n, EMBED_WIDTH)] +...  45.2 us
    pallas_call x1, Pallas kernels, head(): pl.pallas_call(head_kernel, out_shape=[jax.ShapeDtypeStruct((256, EMBED_W...  37.7 us
    pallas_call x1, Pallas kernels, slot_update(): pl.pallas_call(slot_kernel, grid_spec=pltpu.PrefetchScalarGridSpec(num_sc...  16.9 us
    unnamed x52, local copies, waits for them, and re-layouts  14.2 us

profile of v3, /device:TPU:0, one launch (start us, length us, event | category | flops | bytes accessed | tf_op | source)
XLA Modules:
  0.0 489.5 jit_solution(7259154295192136422)
XLA Ops:
  0.7 1.7 copy-done.1
  2.3 1.0 copy-done.7
  4.0 0.7 copy-done.14
  4.7 0.7 copy-done.15
  5.4 2.1 shard_map.221
  7.5 0.8 copy-done.9
  10.6 127.2 %shard_map.222 = (bf16[4,768,768]{2,1,0:T(8,128)(2,1)S(1)}, bf16[4,768,768]{2,1,0:T(8,128)(2,1)}, bf16[4,768,128]{2,1,0:T(8,128)(2,1)S(1)}, bf16[4,192,768]{2,1,...) custom-call(s32[9]{0:T(128)S(1)} %copy-done.13, ...), custom_call_target="tpu_custom_call" | custom-call | tf_op jit(solution)/shard_map/pallas_call | solution.py:402
  137.7 2.2 copy-done
  139.9 1.0 copy-done.3
  140.9 1.0 copy-done.4
  142.0 0.9 copy-done.6
  144.1 2.5 copy.27
  146.6 6.1 %gather_fusion = bf16[1024,128]{1,0:T(8,128)(2,1)} fusion(bf16[7632,128]{1,0:T(8,128)(2,1)} %bitcast.39, s32[1024]{0:T(1024)S(1)} %broadcast_clamp_fusion), kind=kCustom, calls=%fused_computation | custom fusion | bytes 528384 | tf_op jit(solution)/shard_map/gather | solution.py:1358
  153.7 0.7 maximum_maximum_fusion.levels
  154.4 1.4 multiply_sine_fusion
  155.8 0.9 pad_maximum_fusion.places
  157.4 47.6 %shard_map.223 = (bf16[4,256,128]{2,1,0:T(8,128)(2,1)}, f32[256,128]{1,0:T(8,128)}, bf16[256,256]{1,0:T(8,128)(2,1)}, f32[256,768]{1,0:T(8,128)}, bf16[4,256,768...) custom-call(bf16[4,256,128]{2,1,0:T(8,128)(2,1)} %bitcast.42, ...), custom_call_target="tpu_custom_call" | custom-call | tf_op jit(solution)/shard_map/pallas_call | solution.py:573
  205.0 37.7 %shard_map.224 = (f32[256,128]{1,0:T(8,128)}, f32[8,256]{1,0:T(8,128)}) custom-call(bf16[4,256,128]{2,1,0:T(8,128)(2,1)} %get-tuple-element.80.pred_all, bf16[128,7632]{1,0:T(8,128)(2,1)} %bitcast.37, bf16[7632,128]{1,0:T(8,128)(2,1)} %bitcast.40, s32[4,256]{1,0:T(4,128)} %copy-done.11, f32[4,256]{1,0:T(4,128)} %copy-done.12, ...), custom_call_target="tpu_custom_call" | custom-call | tf_op jit(solution)/shard_map/pallas_call | solution.py:713
  242.7 45.2 %shard_map.225 = (bf16[256,128]{1,0:T(8,128)(2,1)}, bf16[768,256]{1,0:T(8,128)(2,1)}, bf16[768,256]{1,0:T(8,128)(2,1)}, bf16[768,256]{1,0:T(8,128)(2,1)}, bf16[7...) custom-call(f32[256,128]{1,0:T(8,128)} %get-tuple-element.84.grad_pr, ...), custom_call_target="tpu_custom_call" | custom-call | tf_op jit(solution)/shard_map/pallas_call | solution.py:873
  287.9 175.9 %shard_map.226 = (s16[8,112,896]{2,1,0:T(8,128)(2,1)}, f32[16,7680]{1,0:T(8,128)}, f32[16,768]{1,0:T(8,128)}) custom-call(s32[9]{0:T(128)} %owners.5, bf16[4,192,256]{2,1,0:T(8,128)(2,1)} %bitcast.43, bf16[4,192,256]{2,1,0:T(8,128)(2,1)} %bitcast.44, bf16[4,192,256]{2,1,0:T(8,128)(2,1)} %bitcast.45, bf16[4,192,256]{2,1,0:T(8,128)(2,1)} %bitcast.46, ...), custom_call_target="tpu_custom_call" | custom-call | tf_op jit(solution)/shard_map/pallas_call | solution.py:1237
  463.8 16.9 %shard_map.227 = (f32[192,3072]{1,0:T(8,128)}, f32[192,3072]{1,0:T(8,128)}, f32[192,3072]{1,0:T(8,128)}) custom-call(s32[24]{0:T(128)} %copy-done.16, s32[24]{0:T(128)} %copy-done.17, s32[24]{0:T(128)} %copy-done.18, s16[8,112,896]{2,1,0:T(8,128)(2,1)} %get-tuple-element.119.big.small, s16[8,112,896]{2,1,0:T(8,128)(2,1)} %get-tuple-element.119.big.small, ...), custom_call_target="tpu_custom_call" | custom-call | bytes 16515072 | tf_op jit(solution)/shard_map/pallas_call | solution.py:1315
  480.8 1.5 fusion.2
  482.3 0.7 multiply_subtract_fusion
  486.3 1.3 pad_maximum_fusion.2
  (54 shorter events, 5.7 us)
Async XLA Ops:
  0.6 1.7 copy-start.1
  2.3 1.0 copy-start.7
  3.3 0.7 copy-start.13
  4.0 0.7 copy-start.14
  4.7 0.7 copy-start.15
  7.5 0.8 copy-start.9
  8.3 0.6 copy-start.11
  9.4 0.6 copy-start.17
  10.6 136.0 %copy-start.5 = (f32[1024,1]{1,0:T(8,128)}, f32[1024,1]{1,0:T(8,128)S(1)}, u32[]{:S(2)}) copy-start(f32[1024,1]{1,0:T(8,128)S(1)} %get-tuple-element.70.keep) | copy-start | bytes 12292
  137.7 2.2 copy-start
  139.9 1.0 copy-start.3
  140.9 1.0 copy-start.4
  142.0 0.9 copy-start.6
  142.9 0.7 copy-start.10
  143.5 0.6 copy-start.12
  144.1 2.5 copy-start.2
  146.6 10.2 %copy-start.22 = (f32[7680]{0:T(1024)S(1)}, f32[7680]{0:T(1024)}, u32[]{:S(2)}) copy-start(f32[7680]{0:T(1024)} %param.25) | copy-start | bytes 92164
  463.8 17.0 %copy-start.8 = (f32[7632,16]{0,1:T(8,128)S(1)}, f32[7632,16]{0,1:T(8,128)}, u32[]{:S(2)}) copy-start(f32[7632,16]{0,1:T(8,128)} %param.19) | copy-start | bytes 1465348
  463.8 17.0 %copy-start.19 = (f32[7632,16]{0,1:T(8,128)S(1)}, f32[7632,16]{0,1:T(8,128)}, u32[]{:S(2)}) copy-start(f32[7632,16]{0,1:T(8,128)} %param.21) | copy-start | bytes 1465348
  463.8 17.0 %copy-start.20 = (f32[7632,16]{0,1:T(8,128)S(1)}, f32[7632,16]{0,1:T(8,128)}, u32[]{:S(2)}) copy-start(f32[7632,16]{0,1:T(8,128)} %param.20) | copy-start | bytes 1465348
  463.8 17.0 %copy-start.21 = (f32[16,7680]{1,0:T(8,128)S(1)}, f32[16,7680]{1,0:T(8,128)}, u32[]{:S(2)}) copy-start(f32[16,7680]{1,0:T(8,128)} %get-tuple-element.115) | copy-start | bytes 1474564
  480.8 1.5 copy-start.23
  480.8 1.5 copy-start.24
  480.8 1.5 copy-start.25
  (2 other events, 1.1 us)

commit v4 on v3

--- a/solution.py
+++ b/solution.py
@@ -268,80 +268,60 @@
         first = y * HALF if c == 3 else v * QUARTER + y * HALF
         return fulls[c].at[unit, pl.ds(first, HALF), :]
 
-    def start_line(c):
-        keep = pltpu.make_async_copy(homes[c], spot(c, z), local.at[c])
-        keep.start()
-        return [keep] + start_all(
-            [
-                remote(homes[c], spot(c, z), (z_send, z_recv), (c, k - 1), (d ^ (2 * k), v))
-                for k in (2, 1, 3)
-            ]
-        )
-
-    def wait_line(copies):
-        copies[0].wait()
-        arrive_all(copies[1:])
-        return copies[1:]
-
-    def start_side(c):
-        return start_all(
-            [remote(spot(c, u), spot(c, u), (y_send, y_recv), (c, u), (d ^ 1, v)) for u in range(4)]
-        )
-
-    def strips(c, rows):
-        if c == 3:
-            return [out.at[rows, :]]
-        return [fulls[c].at[u, rows, :] for u in range(4)]
-
-    def sources(c):
-        return [attn.at[3]] if c == 3 else strips(c, own_rows)
-
-    def start_far(c):
-        return start_all(
-            [
-                remote(s, t, (x_send, x_recv), (c, u), (d, far))
-                for u, (s, t) in enumerate(zip(sources(c), strips(c, own_rows)))
-            ]
-        )
-
-    def start_near(c):
-        return start_all(
-            [
-                remote(s, t, (n_send, n_recv), (c, u), (d, near))
-                for u, (s, t) in enumerate(zip(sources(c), strips(c, own_rows)))
-            ]
-        )
-
-    def start_last(c):
-        rows = pl.ds(far * QUARTER, QUARTER)
-        return start_all(
-            [
-                remote(s, s, (f_send, f_recv), (c, u), (d, near))
-                for u, s in enumerate(strips(c, rows))
-            ]
-        )
-
+    keeps, line, side, chip = {}, {}, {}, {}
     sent, landing = [], []
-    line, side, chip = {}, {}, {}
-
-    def begin_chip(c):
-        arrive_all(side[c])
+
+    def note(copy, store=None, at=None):
+        copy.start()
+        sent.append(copy)
+        if store is not None:
+            store[at] = copy
+        return copy
+
+    def start_class(c):
+        keeps[c] = pltpu.make_async_copy(homes[c], spot(c, z), local.at[c])
+        keeps[c].start()
+        for k in (2, 1, 3):
+            note(
+                remote(homes[c], spot(c, z), (z_send, z_recv), (c, k - 1), (d ^ (2 * k), v)),
+                line,
+                (c, k),
+            )
+        note(remote(homes[c], spot(c, z), (y_send, y_recv), (c, 0), (d ^ 1, v)), side, (c, 0))
+
+    def relay(c, then=()):
+        for k in (2, 1, 3):
+            if k == 3:
+                for other in then:
+                    start_class(other)
+            line[c, k].wait_recv()
+            slab = spot(c, z ^ k)
+            note(remote(slab, slab, (y_send, y_recv), (c, k), (d ^ 1, v)), side, (c, k))
+
+    def chip_slab(c, k, source, target):
+        note(remote(source, target, (x_send, x_recv), (c, k), (d, far)), chip, (c, k))
+        landing.append(note(remote(source, target, (n_send, n_recv), (c, k), (d, near))))
+
+    def to_chip(c):
+        for k in (0, 2, 1, 3):
+            side[c, k].wait_recv()
+            if k == 0:
+                keeps[c].wait()
+            if c < 3:
+                slab = fulls[c].at[z ^ k, own_rows, :]
+                chip_slab(c, k, slab, slab)
         if c == 3:
             keep = pltpu.make_async_copy(attn.at[3], out.at[own_rows, :], local.at[5])
             keep.start()
+            chip_slab(c, 0, attn.at[3], out.at[own_rows, :])
             keep.wait()
-        if c != 4:
-            chip[c] = start_far(c)
-            near_copies = start_near(c)
-            sent.extend(chip[c] + near_copies)
-            landing.extend(near_copies)
-
-    def begin_last(c):
-        if c != 4:
-            arrive_all(chip[c])
-            last = start_last(c)
-            sent.extend(last)
-            landing.extend(last)
+
+    def to_last(c):
+        rows = pl.ds(far * QUARTER, QUARTER)
+        for k in (0,) if c == 3 else (0, 2, 1, 3):
+            chip[c, k].wait_recv()
+            slab = out.at[rows, :] if c == 3 else fulls[c].at[z ^ k, rows, :]
+            landing.append(note(remote(slab, slab, (f_send, f_recv), (c, k), (d, near))))
 
     arrive_all(traded)
     sent.extend(traded)
@@ -364,29 +344,21 @@
         chosen_of([owners[6 + min(u, 2)] for u in range(4)], z), slice(UNIT, UNIT + LANES)
     )
 
-    waves_of = [[0], [1], [2, 3], [4]]
-    for c in waves_of[0]:
-        line[c] = start_line(c)
-    for i, wave in enumerate(waves_of):
-        for c in wave:
-            sent.extend(wait_line(line[c]))
-        if i + 1 < len(waves_of):
-            for c in waves_of[i + 1]:
-                line[c] = start_line(c)
-        for c in wave:
-            side[c] = start_side(c)
-            sent.extend(side[c])
-        if i >= 1:
-            for c in waves_of[i - 1]:
-                begin_chip(c)
-        if i >= 2:
-            for c in waves_of[i - 2]:
-                begin_last(c)
-    for c in waves_of[-1]:
-        begin_chip(c)
-    for wave in waves_of[-2:]:
-        for c in wave:
-            begin_last(c)
+    start_class(0)
+    relay(0, (1,))
+    to_chip(0)
+    relay(1, (2, 3))
+    to_chip(1)
+    relay(2)
+    relay(3, (4,))
+    to_chip(2)
+    to_chip(3)
+    to_last(0)
+    relay(4)
+    to_last(1)
+    to_last(2)
+    to_last(3)
+    to_chip(4)
     arrive_all(landing)
     for copy in sent:
         copy.wait_send()
@@ -906,6 +878,8 @@
 I16 = jnp.int16
 TAIL = 16
 TILES = 60
+PART_TILES = 30
+PART = 3840
 
 
 def exponent(peak):
@@ -944,13 +918,13 @@
         ref[:, at] = coded(value, power)
         return jnp.where(lane == tile, power, powers)
 
-    powers = lax.fori_loop(0, TILES, body, jnp.zeros((rows, LANES), f32), unroll=6)
-    ref[:, TILES * LANES :] = powers.astype(jnp.int32).astype(I16)
+    powers = lax.fori_loop(0, PART_TILES, body, jnp.zeros((rows, LANES), f32), unroll=6)
+    ref[:, PART:] = powers.astype(jnp.int32).astype(I16)
 
 
 def tile_getter(ref, rows):
     lane = lax.broadcasted_iota(jnp.int32, (rows, LANES), 1)
-    powers = ref[:, TILES * LANES :].astype(jnp.int32).astype(f32)
+    powers = ref[:, PART:].astype(jnp.int32).astype(f32)
 
     def read(tile, at):
         power = jnp.sum(jnp.where(lane == tile, powers, 0.0), 1, keepdims=True)
@@ -1097,43 +1071,50 @@
 
     table_strips = [(lo, min(STRIP, vocab_rows - lo)) for lo in range(0, vocab_rows, STRIP)]
 
-    def table_to_side():
-        put_tiles(ts, lambda at: table[1 - y, :, at], 64)
-        side[13] = send(ts, tr, (y_send, y_recv), 13, (d ^ 1, v))
-
-    def table_line_value(which):
+    def shifted(at, p):
+        return pl.ds(pl.multiple_of(at.start + p * PART, LANES), LANES)
+
+    def table_to_side(p):
+        put_tiles(ts.at[p], lambda at: table[1 - y, :, shifted(at, p)], 64)
+        side[13 + p] = send(ts.at[p], tr.at[p], (y_send, y_recv), 13 + p, (d ^ 1, v))
+
+    def table_line_value(which, p):
         rows = pl.ds(pl.multiple_of(which * 16, 16), 16)
-        read = tile_getter(tr.at[rows, :], 16)
+        read = tile_getter(tr.at[p, rows, :], 16)
         return rows, read
 
-    def table_to_line():
-        side[13].wait_recv()
+    def table_to_line(p):
+        side[13 + p].wait_recv()
         for k in (2, 1, 3):
-            rows, read = table_line_value(z ^ k)
+            rows, read = table_line_value(z ^ k, p)
 
             def source(at, rows=rows, read=read):
-                return table[y, rows, at] + read(at.start // LANES, at)
-
-            put_tiles(tzs.at[k - 1], source, 16)
-            line[4, k] = send(
-                tzs.at[k - 1], tzr.at[k - 1], (z_send, z_recv), 12 + k - 1, (d ^ (2 * k), v)
+                return table[y, rows, shifted(at, p)] + read(at.start // LANES, at)
+
+            put_tiles(tzs.at[p, k - 1], source, 16)
+            line[4 + p, k] = send(
+                tzs.at[p, k - 1],
+                tzr.at[p, k - 1],
+                (z_send, z_recv),
+                12 + 3 * p + k - 1,
+                (d ^ (2 * k), v),
             )
 
-    def table_to_home():
+    def table_to_home(p):
         for k in (2, 1, 3):
-            line[4, k].wait_recv()
-        rows, read = table_line_value(z)
-        others = [tile_getter(tzr.at[k], 16) for k in range(3)]
+            line[4 + p, k].wait_recv()
+        rows, read = table_line_value(z, p)
+        others = [tile_getter(tzr.at[p, k], 16) for k in range(3)]
 
         def body(tile, carry):
             at = pl.ds(pl.multiple_of(tile * LANES, LANES), LANES)
-            value = table[y, rows, at] + read(tile, at)
+            value = table[y, rows, shifted(at, p)] + read(tile, at)
             for other in others:
                 value = value + other(tile, at)
-            table_sum[:, at] = value
+            table_sum[:, shifted(at, p)] = value
             return carry
 
-        lax.fori_loop(0, TILES, body, 0, unroll=4)
+        lax.fori_loop(0, PART_TILES, body, 0, unroll=5)
 
     hops = [(d, near), (d, far), (d ^ 1, v), (d ^ 2, v), (d ^ 4, v)]
     tile_copies = {}
@@ -1148,63 +1129,73 @@
             tile_at.at[hop], tile_from.at[hop], (t_send, t_recv), hop, hops[hop]
         )
 
+    def token_products():
+        for u in range(3):
+            halves(
+                u,
+                sum(matmul_nn(qkv_left[u, :, 256 * b : 256 * b + 256], normed[b]) for b in range(4)),
+            )
+
     turn_tokens()
+    token_products()
     to_core(0)
     to_core(1)
     to_chip(0)
     tile_send(0)
+    table_strip(*table_strips[0])
+    table_strip(*table_strips[1])
     to_core(2)
-    table_strip(*table_strips[0])
     to_chip(1)
-    table_strip(*table_strips[1])
+    to_side(0)
     table_strip(*table_strips[2])
+    table_strip(*table_strips[3])
     to_core(3)
     to_chip(2)
-    table_strip(*table_strips[3])
     table_strip(*table_strips[4])
+    table_to_side(0)
+    to_line(0)
+    to_side(1)
     table_strip(*table_strips[5])
+    table_strip(*table_strips[6])
     to_core(4)
     to_chip(3)
-    table_strip(*table_strips[6])
     table_strip(*table_strips[7])
-    for strip in table_strips[8:]:
+    table_strip(*table_strips[8])
+    for strip in table_strips[9:]:
         table_strip(*strip)
-    table_to_side()
-    tile_send(1)
-    for u in range(3):
-        halves(u, sum(matmul_nn(qkv_left[u, :, 256 * b : 256 * b + 256], normed[b]) for b in range(4)))
-    small_to_core()
+    table_to_side(1)
+    to_side(2)
     to_core(5)
     to_chip(4)
-    to_side(0)
-    tile_send(2)
+    tile_send(1)
+    table_to_line(0)
     to_core(6)
     to_chip(5)
-    small_to_chip()
-    to_side(1)
-    table_to_line()
-    tile_send(3)
+    to_side(3)
     to_core(7)
     to_chip(6)
-    to_side(2)
-    to_line(0)
+    small_to_core()
     to_core(8)
     to_chip(7)
-    tile_send(4)
-    to_side(3)
+    small_to_chip()
     to_chip(8)
     to_side(4)
+    tile_send(2)
+    table_to_line(1)
     to_line(1)
-    small_to_side()
-    table_to_home()
     to_side(5)
     to_home(0)
+    tile_send(3)
+    small_to_side()
     to_side(6)
+    table_to_home(0)
     small_to_line()
+    tile_send(4)
     to_side(7)
     to_home(1)
     to_side(8)
     to_line(2)
+    table_to_home(1)
     small_to_home()
     tile_copies[4].wait_recv()
     tile_sum[...] = tile_at[4] + tile_from[4]
@@ -1269,16 +1260,16 @@
             vmem((2, 64, table_cols), f32),
             vmem((4, EMBED_WIDTH, 256), bf16),
             vmem((4, EMBED_WIDTH, 256), bf16),
-            vmem((64, table_cols + LANES), I16),
-            vmem((64, table_cols + LANES), I16),
-            vmem((3, 16, table_cols + LANES), I16),
-            vmem((3, 16, table_cols + LANES), I16),
+            vmem((2, 64, PART + LANES), I16),
+            vmem((2, 64, PART + LANES), I16),
+            vmem((2, 3, 16, PART + LANES), I16),
+            vmem((2, 3, 16, PART + LANES), I16),
             vmem((5, 16, UNIT), f32),
             vmem((5, 16, UNIT), f32),
         ]
         + [dma((10,))] * 4
-        + [dma((14,))] * 2
         + [dma((15,))] * 2
+        + [dma((18,))] * 2
         + [dma((5,))] * 2
         + [dma((7,))] * 2
         + [dma],
@@ -1288,41 +1279,37 @@
     )(*operands)
 
 
-def slot_kernel(kind, unit, column, big, small, w, m1, m2, w_out, m1_out, m2_out):
-    which = kind[pl.program_id(0)]
-
-    def rows_of(ref):
-        return jnp.concatenate([get(ref.at[0], HALF), get(ref.at[1], HALF)], 0)
-
-    zero = jnp.zeros(w.shape, f32)
-    g = jnp.where(which == 1, rows_of(big), jnp.where(which == 2, rows_of(small), zero))
-    w_out[...], m1_out[...], m2_out[...] = adamw(w[...], g, m1[...], m2[...])
+def slot_kernel(kind, unit, column, summed, w, m1, m2, w_out, m1_out, m2_out):
+    per_unit = UNIT // LANES
+    for b in range(per_unit):
+        j = pl.program_id(0) * per_unit + b
+        first = jnp.where(kind[j] == 2, per_unit, column[j])
+        at = pl.ds(pl.multiple_of(first * LANES, LANES), LANES)
+        lanes = slice(b * LANES, b * LANES + LANES)
+        for half in range(2):
+            rows = slice(half * HALF, half * HALF + HALF)
+            g = get(summed.at[2 * unit[j] + half, :, at], HALF)
+            g = jnp.where(kind[j] > 0, g, jnp.zeros_like(g))
+            w_out[rows, lanes], m1_out[rows, lanes], m2_out[rows, lanes] = adamw(
+                w[rows, lanes], g, m1[rows, lanes], m2[rows, lanes]
+            )
 
 
 def slot_update(kind, unit, column, summed, slots, first, second):
     rows = slots.shape[0]
-    blocks = CAP // LANES
-    per_unit = UNIT // LANES
-    plain_spec = pl.BlockSpec((rows, LANES), lambda j, k, u, c: (0, j))
-    low = HALF + TAIL
-    big_spec = pl.BlockSpec(
-        (2, low, LANES),
-        lambda j, k, u, c: (jnp.where(k[j] == 1, u[j], 0), 0, jnp.where(k[j] == 1, c[j], 0)),
-    )
-    small_spec = pl.BlockSpec(
-        (2, low, LANES), lambda j, k, u, c: (jnp.where(k[j] == 2, u[j], 0), 0, per_unit)
-    )
+    plain_spec = pl.BlockSpec((rows, UNIT), lambda j, k, u, c: (0, j))
     return pl.pallas_call(
         slot_kernel,
         grid_spec=pltpu.PrefetchScalarGridSpec(
             num_scalar_prefetch=3,
-            grid=(blocks,),
-            in_specs=[big_spec, small_spec, plain_spec, plain_spec, plain_spec],
-            out_specs=[plain_spec, plain_spec, plain_spec],
+            grid=(CAP // UNIT,),
+            in_specs=[pl.BlockSpec(summed.shape, lambda j, k, u, c: (0, 0, 0))] + [plain_spec] * 3,
+            out_specs=[plain_spec] * 3,
         ),
         out_shape=[jax.ShapeDtypeStruct(slots.shape, f32)] * 3,
         cost_estimate=pl.CostEstimate(flops=0, bytes_accessed=28 * rows * CAP, transcendentals=0),
-    )(kind, unit, column, summed, summed, slots, first, second)
+        compiler_params=pltpu.CompilerParams(vmem_limit_bytes=40 * 2**20),
+    )(kind, unit, column, summed, slots, first, second)
 
 
 def per_device(

time: 497 us -> 442 us (0.89)
  Pallas kernels: 453 us -> 398 us
    pallas_call x1, Pallas kernels: 176 us -> 146 us  [reduce_grads(): pl.pallas_call(grads_kernel, out_shape=[jax.ShapeDtypeStruct((8, low, UNI...]
    pallas_call x1, Pallas kernels: 127 us -> 114 us  [spread(): pl.pallas_call(spread_kernel, out_shape=[shape(4, D, UNIT), shape(4, D, U...]
    pallas_call x1, Pallas kernels: 16.9 us -> 4.95 us  [slot_update(): pl.pallas_call(slot_kernel, grid_spec=pltpu.PrefetchScalarGridSpec(num_sc...]
    unnamed x52 -> x54, local copies, waits for them, and re-layouts: 14.2 us -> 17.3 us
where the time goes in v4:
time: 442 us; the launch traced here: 438 us
  Pallas kernels  398 us (90%)
  local copies, waits for them, and re-layouts  27.1 us (6%)
  other arithmetic  6.54 us (1%)
  between operations  6.06 us (1%)
    pallas_call x1, Pallas kernels, reduce_grads(): pl.pallas_call(grads_kernel, out_shape=[jax.ShapeDtypeStruct((8, low, UNI...  146 us
    pallas_call x1, Pallas kernels, spread(): pl.pallas_call(spread_kernel, out_shape=[shape(4, D, UNIT), shape(4, D, U...  114 us
    pallas_call x1, Pallas kernels, forward(): pl.pallas_call(forward_kernel, out_shape=[shape(bf16, 4, n, EMBED_WIDTH),...  47.6 us
    pallas_call x1, Pallas kernels, backward(): pl.pallas_call(backward_kernel, out_shape=[shape(bf16, n, EMBED_WIDTH)] +...  45.3 us
    pallas_call x1, Pallas kernels, head(): pl.pallas_call(head_kernel, out_shape=[jax.ShapeDtypeStruct((256, EMBED_W...  37.7 us
    unnamed x54, local copies, waits for them, and re-layouts  17.3 us

profile of v4, /device:TPU:0, one launch (start us, length us, event | category | flops | bytes accessed | tf_op | source)
XLA Modules:
  0.0 437.7 jit_solution(1115751854158063265)
XLA Ops:
  0.7 1.7 copy-done.1
  2.3 1.0 copy-done.10
  5.4 2.4 shard_map.221
  7.8 0.8 copy-done.13
  9.2 113.9 %shard_map.222 = (bf16[4,768,768]{2,1,0:T(8,128)(2,1)S(1)}, bf16[4,768,768]{2,1,0:T(8,128)(2,1)}, bf16[4,768,128]{2,1,0:T(8,128)(2,1)S(1)}, bf16[4,192,768]{2,1,...) custom-call(s32[9]{0:T(128)S(1)} %copy-done.17, ...), custom_call_target="tpu_custom_call" | custom-call | tf_op jit(solution)/shard_map/pallas_call | solution.py:374
  123.2 2.2 copy-done
  125.3 1.0 copy-done.4
  126.4 1.1 copy-done.5
  127.4 0.9 copy-done.7
  129.6 2.5 copy.27
  132.1 6.0 %gather_fusion = bf16[1024,128]{1,0:T(8,128)(2,1)} fusion(bf16[7632,128]{1,0:T(8,128)(2,1)} %bitcast.39, s32[1024]{0:T(1024)S(1)} %broadcast_clamp_fusion), kind=kCustom, calls=%fused_computation | custom fusion | bytes 528384 | tf_op jit(solution)/shard_map/gather | solution.py:1345
  139.8 1.4 multiply_sine_fusion
  141.3 1.0 pad_maximum_fusion.places
  142.8 47.6 %shard_map.223 = (bf16[4,256,128]{2,1,0:T(8,128)(2,1)}, f32[256,128]{1,0:T(8,128)}, bf16[256,256]{1,0:T(8,128)(2,1)}, f32[256,768]{1,0:T(8,128)}, bf16[4,256,768...) custom-call(bf16[4,256,128]{2,1,0:T(8,128)(2,1)} %bitcast.42, ...), custom_call_target="tpu_custom_call" | custom-call | tf_op jit(solution)/shard_map/pallas_call | solution.py:545
  190.4 37.7 %shard_map.224 = (f32[256,128]{1,0:T(8,128)}, f32[8,256]{1,0:T(8,128)}) custom-call(bf16[4,256,128]{2,1,0:T(8,128)(2,1)} %get-tuple-element.80.pred_all, bf16[128,7632]{1,0:T(8,128)(2,1)} %bitcast.37, bf16[7632,128]{1,0:T(8,128)(2,1)} %bitcast.40, s32[4,256]{1,0:T(4,128)} %copy-done.15, f32[4,256]{1,0:T(4,128)} %copy-done.16, ...), custom_call_target="tpu_custom_call" | custom-call | tf_op jit(solution)/shard_map/pallas_call | solution.py:685
  228.1 45.3 %shard_map.225 = (bf16[256,128]{1,0:T(8,128)(2,1)}, bf16[768,256]{1,0:T(8,128)(2,1)}, bf16[768,256]{1,0:T(8,128)(2,1)}, bf16[768,256]{1,0:T(8,128)(2,1)}, bf16[7...) custom-call(f32[256,128]{1,0:T(8,128)} %get-tuple-element.84.grad_pr, ...), custom_call_target="tpu_custom_call" | custom-call | tf_op jit(solution)/shard_map/pallas_call | solution.py:845
  273.4 146.1 %shard_map.226 = (s16[8,112,896]{2,1,0:T(8,128)(2,1)}, f32[16,7680]{1,0:T(8,128)}, f32[16,768]{1,0:T(8,128)}) custom-call(s32[9]{0:T(128)} %owners.5, bf16[4,192,256]{2,1,0:T(8,128)(2,1)} %bitcast.43, bf16[4,192,256]{2,1,0:T(8,128)(2,1)} %bitcast.44, bf16[4,192,256]{2,1,0:T(8,128)(2,1)} %bitcast.45, bf16[4,192,256]{2,1,0:T(8,128)(2,1)} %bitcast.46, ...), custom_call_target="tpu_custom_call" | custom-call | tf_op jit(solution)/shard_map/pallas_call | solution.py:1228
  419.6 1.7 copy-done.8
  421.2 1.7 copy-done.9
  422.9 1.4 copy-done.12
  424.3 4.9 %shard_map.227 = (f32[192,3072]{1,0:T(8,128)}, f32[192,3072]{1,0:T(8,128)}, f32[192,3072]{1,0:T(8,128)}) custom-call(s32[24]{0:T(128)S(1)} %get-tuple-element.116.kind, s32[24]{0:T(128)S(1)} %get-tuple-element.117.unit, s32[24]{0:T(128)S(1)} %get-tuple-element.118.column, s16[8,112,896]{2,1,0:T(8,128)(2,1)S(1)} %copy-done.12, f32[192,3072]{1,0:T(8,128)S(1)} %copy-done.2, ...), custom_call_target="tpu_custom_call" | custom-call | bytes 16515072 | tf_op jit(solution)/shard_map/pallas_call | solution.py:1301
  429.3 1.5 fusion.2
  430.8 0.7 multiply_subtract_fusion
  434.5 1.2 pad_maximum_fusion.2
  (56 shorter events, 6.1 us)
Async XLA Ops:
  0.6 1.7 copy-start.1
  2.3 1.0 copy-start.10
  3.3 0.7 copy-start.17
  4.0 0.7 copy-start.18
  4.7 0.7 copy-start.19
  7.8 0.8 copy-start.13
  9.2 122.8 %copy-start.6 = (f32[1024,1]{1,0:T(8,128)}, f32[1024,1]{1,0:T(8,128)S(1)}, u32[]{:S(2)}) copy-start(f32[1024,1]{1,0:T(8,128)S(1)} %get-tuple-element.70.keep) | copy-start | bytes 12292
  123.2 2.2 copy-start
  125.3 1.0 copy-start.4
  126.4 1.1 copy-start.5
  127.4 0.9 copy-start.7
  129.6 2.5 copy-start.3
  132.1 10.2 %copy-start.23 = (f32[7680]{0:T(1024)S(1)}, f32[7680]{0:T(1024)}, u32[]{:S(2)}) copy-start(f32[7680]{0:T(1024)} %param.25) | copy-start | bytes 92164
  273.4 146.1 %copy-start.2 = (f32[192,3072]{1,0:T(8,128)S(1)}, f32[192,3072]{1,0:T(8,128)}, u32[]{:S(2)}) copy-start(f32[192,3072]{1,0:T(8,128)} %w.1) | copy-start | bytes 7077892
  419.5 1.7 copy-start.8
  421.2 1.7 copy-start.9
  422.9 1.4 copy-start.12
  424.3 5.0 %copy-start.11 = (f32[7632,16]{0,1:T(8,128)S(1)}, f32[7632,16]{0,1:T(8,128)}, u32[]{:S(2)}) copy-start(f32[7632,16]{0,1:T(8,128)} %param.19) | copy-start | bytes 1465348
  424.3 5.0 %copy-start.20 = (f32[7632,16]{0,1:T(8,128)S(1)}, f32[7632,16]{0,1:T(8,128)}, u32[]{:S(2)}) copy-start(f32[7632,16]{0,1:T(8,128)} %param.21) | copy-start | bytes 1465348
  424.3 5.0 %copy-start.21 = (f32[7632,16]{0,1:T(8,128)S(1)}, f32[7632,16]{0,1:T(8,128)}, u32[]{:S(2)}) copy-start(f32[7632,16]{0,1:T(8,128)} %param.20) | copy-start | bytes 1465348
  424.3 5.0 %copy-start.22 = (f32[16,7680]{1,0:T(8,128)S(1)}, f32[16,7680]{1,0:T(8,128)}, u32[]{:S(2)}) copy-start(f32[16,7680]{1,0:T(8,128)} %get-tuple-element.115) | copy-start | bytes 1474564
  429.3 1.5 copy-start.24
  429.3 1.5 copy-start.25
  429.3 1.5 copy-start.26
  (3 other events, 1.8 us)

commit v5 on v4

--- a/solution.py
+++ b/solution.py
@@ -130,9 +130,9 @@
 
 
 def prepare_kernel(
-    owners, ids, mask, table, slots,
+    owners, ids_from, mask_from, table_from, slots,
     payload, table_low, row_of, safe, keep_rows, keep, valid, count, kind, unit, column,
-    units, extras, sems,
+    units, extras, ids, mask, table, sems, own_sems,
 ):
     d, v = lax.axis_index("dp"), lax.axis_index("vocab")
     starts = [
@@ -140,6 +140,12 @@
         for i in range(len(ROW_COUNTS))
     ]
     whole = (owners[4] == d) | (owners[5] == d)
+    fetched = [
+        pltpu.make_async_copy(src, dst, own_sems.at[i])
+        for i, (src, dst) in enumerate(((ids_from, ids), (mask_from, mask), (table_from, table)))
+    ]
+    for copy in fetched:
+        copy.start()
     copies = []
     for u in range(4):
         first = pl.multiple_of(jnp.where(whole, u * UNIT, starts[u]), LANES)
@@ -176,6 +182,8 @@
 
         pl.when(owners[i] == d)(claim)
 
+    for copy in fetched:
+        copy.wait()
     table_low[...] = table[...].astype(bf16)
     count[...] = jnp.full((8, LANES), jnp.sum(mask[...].astype(f32)))
     for b in range(4):
@@ -217,14 +225,18 @@
             shape(f32, 8, LANES),
         ]
         + [shape(jnp.int32, blocks)] * 3,
-        in_specs=[SMEM, VMEM, VMEM, VMEM, ANY],
+        in_specs=[SMEM, ANY, ANY, ANY, ANY],
         out_specs=[VMEM] * 8 + [SMEM] * 3,
         scratch_shapes=[
             pltpu.VMEM((4, QUARTER, UNIT), f32),
             pltpu.VMEM((4, QUARTER, LANES), f32),
+            pltpu.VMEM(ids.shape, jnp.int32),
+            pltpu.VMEM(mask.shape, jnp.int32),
+            pltpu.VMEM(table.shape, f32),
             pltpu.SemaphoreType.DMA((8,)),
+            pltpu.SemaphoreType.DMA((3,)),
         ],
-        compiler_params=pltpu.CompilerParams(vmem_limit_bytes=40 * 2**20),
+        compiler_params=pltpu.CompilerParams(vmem_limit_bytes=60 * 2**20),
     )(owners, ids, mask, table, slots)
 
 
@@ -239,11 +251,11 @@
 
 
 def spread_kernel(
-    owners, payload, tile, keep_rows, keep, table_home,
-    up, down, small, attn, out, table, weight, twice,
-    arrived, tiles, up_home, down_home, small_home, attn_home,
+    owners, steps, payload, tile, keep_rows, keep, table_home,
+    up_to, down_to, small_to, attn_to, out_to, table_to, weight, twice, places, levels,
+    up, down, small, attn, out, table, arrived, tiles, up_home, down_home, small_home, attn_home,
     a_send, a_recv, b_send, b_recv,
-    z_send, z_recv, y_send, y_recv, x_send, x_recv, n_send, n_recv, f_send, f_recv, local,
+    z_send, z_recv, y_send, y_recv, x_send, x_recv, n_send, n_recv, f_send, f_recv, local, o_sem,
 ):
     z, y, d, v = place()
     far, near = v ^ 2, v ^ 1
@@ -269,7 +281,7 @@
         return fulls[c].at[unit, pl.ds(first, HALF), :]
 
     keeps, line, side, chip = {}, {}, {}, {}
-    sent, landing = [], []
+    sent, landing, stores = [], {c: [] for c in range(4)}, []
 
     def note(copy, store=None, at=None):
         copy.start()
@@ -300,7 +312,7 @@
 
     def chip_slab(c, k, source, target):
         note(remote(source, target, (x_send, x_recv), (c, k), (d, far)), chip, (c, k))
-        landing.append(note(remote(source, target, (n_send, n_recv), (c, k), (d, near))))
+        landing[c].append(note(remote(source, target, (n_send, n_recv), (c, k), (d, near))))
 
     def to_chip(c):
         for k in (0, 2, 1, 3):
@@ -321,8 +333,23 @@
         for k in (0,) if c == 3 else (0, 2, 1, 3):
             chip[c, k].wait_recv()
             slab = out.at[rows, :] if c == 3 else fulls[c].at[z ^ k, rows, :]
-            landing.append(note(remote(slab, slab, (f_send, f_recv), (c, k), (d, near))))
-
+            landing[c].append(note(remote(slab, slab, (f_send, f_recv), (c, k), (d, near))))
+
+    def angles(position, width, count):
+        lane = lax.broadcasted_iota(jnp.int32, (count, width), 1).astype(f32)
+        return position * jnp.exp(-math.log(10000.0) * lane / width)
+
+    position = v * 256 + lax.broadcasted_iota(jnp.int32, (256, D // 2), 0)
+    angle = angles(position.astype(f32), D // 2, 256)
+    places[:, 0 : D // 2] = jnp.sin(angle)
+    places[:, D // 2 :] = jnp.cos(angle)
+    step = jnp.full((8, EMBED_WIDTH), steps[0], jnp.int32).astype(f32)
+    signal = 1.0 - jnp.sqrt(step / DIFF + 0.0001)
+    angle = angles(step[:, 0 : EMBED_WIDTH // 2], EMBED_WIDTH // 2, 8)
+    levels[0:1] = jnp.sqrt(signal[0:1])
+    levels[1:2] = jnp.sqrt(1.0 - signal[0:1])
+    levels[2:3] = jnp.concatenate([jnp.sin(angle), jnp.cos(angle)], 1)[0:1]
+    levels[3:8] = jnp.zeros((5, EMBED_WIDTH), f32)
     arrive_all(traded)
     sent.extend(traded)
     total = tile[...]
@@ -343,6 +370,18 @@
     small_home[...] = from_owner(
         chosen_of([owners[6 + min(u, 2)] for u in range(4)], z), slice(UNIT, UNIT + LANES)
     )
+
+    def store(src, dst, index):
+        copy = pltpu.make_async_copy(src, dst, o_sem.at[index])
+        copy.start()
+        stores.append(copy)
+
+    def finish(c):
+        arrive_all(landing[c])
+        if c == 3:
+            store(out, out_to, 3)
+        else:
+            store(fulls[c], (up_to, down_to, small_to)[c], c)
 
     start_class(0)
     relay(0, (1,))
@@ -353,18 +392,25 @@
     relay(3, (4,))
     to_chip(2)
     to_chip(3)
+    store(attn, attn_to, 4)
     to_last(0)
     relay(4)
+    finish(0)
     to_last(1)
     to_last(2)
     to_last(3)
     to_chip(4)
-    arrive_all(landing)
+    store(table, table_to, 5)
+    finish(1)
+    finish(2)
+    finish(3)
+    for copy in stores:
+        copy.wait()
     for copy in sent:
         copy.wait_send()
 
 
-def spread(owners, payload, tile, keep_rows, keep, table_home):
+def spread(owners, steps, payload, tile, keep_rows, keep, table_home):
     rows, vocab_rows = table_home.shape
     dma, vmem = pltpu.SemaphoreType.DMA, pltpu.VMEM
 
@@ -382,10 +428,18 @@
             shape(8, rows, vocab_rows),
             jax.ShapeDtypeStruct(keep_rows.shape, f32),
             jax.ShapeDtypeStruct((256, 1), f32),
+            jax.ShapeDtypeStruct((256, D), f32),
+            jax.ShapeDtypeStruct((8, EMBED_WIDTH), f32),
         ],
-        in_specs=[SMEM] + [VMEM] * 5,
-        out_specs=[ANY] * 6 + [VMEM] * 2,
+        in_specs=[SMEM] * 2 + [VMEM] * 5,
+        out_specs=[ANY] * 6 + [VMEM] * 4,
         scratch_shapes=[
+            vmem((4, D, UNIT), bf16),
+            vmem((4, D, UNIT), bf16),
+            vmem((4, D, LANES), bf16),
+            vmem((4, QUARTER, UNIT), bf16),
+            vmem((D, UNIT), bf16),
+            vmem((8, rows, vocab_rows), bf16),
             vmem((7, HALF, UNIT + LANES), bf16),
             vmem((7, 8, LANES), f32),
             vmem((HALF, UNIT), bf16),
@@ -397,11 +451,11 @@
         + [dma((5, 3))] * 2
         + [dma((5, 4))] * 2
         + [dma((4, 4))] * 6
-        + [dma((6,))],
+        + [dma((6,))] * 2,
         compiler_params=pltpu.CompilerParams(
-            collective_id=1, has_side_effects=True, vmem_limit_bytes=40 * 2**20
+            collective_id=1, has_side_effects=True, vmem_limit_bytes=60 * 2**20
         ),
-    )(owners, payload, tile, keep_rows, keep, table_home)
+    )(owners, steps, payload, tile, keep_rows, keep, table_home)
 
 def neighbours():
     d, v = lax.axis_index("dp"), lax.axis_index("vocab")
@@ -414,14 +468,20 @@
 
 
 def forward_kernel(
-    looked, valid, noise, levels, places, small, attn, out_w, up_hbm, down_hbm, vecs, keep,
+    looked, valid, levels, places, vecs, keep, noise_hbm, small_hbm, attn_hbm, out_hbm, up_hbm, down_hbm,
     found, clean, inputs, hidden, normed_all, q, k, k_t, values, log_total, mixed, middle, normed_two,
     up_proj, active, hidden_two, final_norm, predicted, pred_all,
-    up_w, down_w, found_in, values_t, mixed_out, mixed_in,
-    w_sem, e_send, e_recv, n_send, n_recv, m_send, m_recv, p_send, p_recv,
+    noise, small, attn, out_w, up_w, down_w, found_in, values_t, mixed_out, mixed_in, seen,
+    w_sem, s_sem, e_send, e_recv, n_send, n_recv, m_send, m_recv, p_send, p_recv,
 ):
     v = lax.axis_index("vocab")
     partners = neighbours()
+    sources = ((noise_hbm, noise), (small_hbm, small), (attn_hbm, attn), (out_hbm, out_w))
+    first = [
+        pltpu.make_async_copy(src, dst, s_sem.at[i]) for i, (src, dst) in enumerate(sources)
+    ]
+    for copy in first:
+        copy.start()
     loads = []
     for j in range(4):
         for i, (src, dst) in enumerate(((up_hbm, up_w), (down_hbm, down_w))):
@@ -439,6 +499,9 @@
             for m in (2, 3, 1)
         ]
     )
+    seen[...] = jnp.broadcast_to(keep[...], seen.shape)
+    for copy in first:
+        copy.wait()
     wave = levels[2:3].astype(bf16)
     time_part = matmul_nt(jnp.broadcast_to(wave, (16, EMBED_WIDTH)), small[1])[0:1]
     arrive_all(asked)
@@ -486,7 +549,7 @@
         parts = []
         for h in range(3):
             scores = matmul_nt(k[h], q[h, rows, :])
-            scores = jnp.where(keep[...] > 0.0, scores, -1000000000.0)
+            scores = jnp.where(seen[...] > 0.0, scores, -1000000000.0)
             top = jnp.max(scores, 0, keepdims=True)
             expo = jnp.exp(scores - top)
             mass = jnp.sum(expo, 0, keepdims=True)
@@ -535,7 +598,7 @@
         copy.wait_send()
 
 
-def forward(looked, valid, noise, levels, places, small, attn, out_w, up_w, down_w, vecs, keep):
+def forward(*operands):
     dma, vmem = pltpu.SemaphoreType.DMA, pltpu.VMEM
     n = 256
 
@@ -565,22 +628,28 @@
             shape(f32, n, EMBED_WIDTH),
             shape(bf16, 4, n, EMBED_WIDTH),
         ],
-        in_specs=[VMEM] * 8 + [ANY] * 2 + [VMEM] * 2,
+        in_specs=[VMEM] * 6 + [ANY] * 6,
         out_specs=[VMEM] * 19,
         scratch_shapes=[
+            vmem((n, EMBED_WIDTH), bf16),
+            vmem((4, D, LANES), bf16),
+            vmem((4, QUARTER, UNIT), bf16),
+            vmem((D, UNIT), bf16),
             vmem((4, D, UNIT), bf16),
             vmem((4, D, UNIT), bf16),
             vmem((3, n, EMBED_WIDTH), bf16),
             vmem((QUARTER, 4 * n), bf16),
             vmem((3, n, QUARTER), bf16),
             vmem((4, n, QUARTER), bf16),
+            vmem((4 * n, n), f32),
             dma((8,)),
+            dma((4,)),
         ]
         + [dma((3,))] * 8,
         compiler_params=pltpu.CompilerParams(
             collective_id=4, has_side_effects=True, vmem_limit_bytes=60 * 2**20
         ),
-    )(looked, valid, noise, levels, places, small, attn, out_w, up_w, down_w, vecs, keep)
+    )(*operands)
 
 
 STRIP = 768
@@ -591,8 +660,8 @@
 
 
 def head_kernel(
-    pred_all, table, table_t, row_of, weight, found,
-    grad_pred, lse, logits, stats, gathered, outgoing, incoming,
+    pred_all, table, table_t, weight, found,
+    grad_pred, lse, found_t, stats, gathered, outgoing, incoming,
     s_send, s_recv, g_send, g_recv,
 ):
     partners = neighbours()
@@ -602,45 +671,33 @@
     mixes = []
     for b in range(4):
         block = pred_all[b]
-        wanted = row_of[b : b + 1, :]
-
-        def first(at, size, top):
+
+        def strip(at, carry):
+            peak, mass, mix = carry
             value = matmul_nt(table_t[at, :], block)
-            logits[at, :] = value
-            return jnp.maximum(top, jnp.max(value, 0, keepdims=True))
-
-        def second(at, size, lo, carry, peak):
-            mass, target, mix = carry
-            value = logits[at, :]
-            expo = jnp.exp(value - peak)
-            here = lax.broadcasted_iota(jnp.int32, (size, 256), 0) == wanted - lo
-            mass = mass + jnp.sum(expo, 0, keepdims=True)
-            target = target + jnp.sum(jnp.where(here, value, 0.0), 0, keepdims=True)
-            return mass, target, mix + matmul_nn(table[:, at], expo.astype(bf16))
-
-        peak = lax.fori_loop(
-            0,
-            full,
-            lambda t, top: first(pl.ds(pl.multiple_of(t * STRIP, STRIP), STRIP), STRIP, top),
-            jnp.full((1, 256), -jnp.inf, f32),
-        )
-        tail = pl.ds(full * STRIP, rest)
-        if rest:
-            peak = first(tail, rest, peak)
-        zero = jnp.zeros((1, 256), f32)
+            top = jnp.maximum(peak, jnp.max(value, 0, keepdims=True))
+            expo = jnp.exp(value - top)
+            fade = jnp.exp(peak - top)
+            mass = mass * fade + jnp.sum(expo, 0, keepdims=True)
+            return top, mass, mix * fade + matmul_nn(table[:, at], expo.astype(bf16))
+
         carry = lax.fori_loop(
             0,
             full,
-            lambda t, carry: second(
-                pl.ds(pl.multiple_of(t * STRIP, STRIP), STRIP), STRIP, t * STRIP, carry, peak
+            lambda t, carry: strip(pl.ds(pl.multiple_of(t * STRIP, STRIP), STRIP), carry),
+            (
+                jnp.full((1, 256), -jnp.inf, f32),
+                jnp.zeros((1, 256), f32),
+                jnp.zeros((EMBED_WIDTH, 256), f32),
             ),
-            (zero, zero, jnp.zeros((EMBED_WIDTH, 256), f32)),
+            unroll=3,
         )
         if rest:
-            carry = second(tail, rest, full * STRIP, carry, peak)
-        stats[b, 0:1] = peak
-        stats[b, 1:2] = carry[0]
-        stats[b, 2:3] = carry[1]
+            carry = strip(pl.ds(full * STRIP, rest), carry)
+        found_t[b] = found[b].astype(f32).T
+        stats[b, 2:3] = jnp.sum(block.astype(f32).T * found_t[b], 0, keepdims=True)
+        stats[b, 0:1] = carry[0]
+        stats[b, 1:2] = carry[1]
         stats[b, 3:8] = jnp.zeros((5, 256), f32)
         mixes.append(carry[2])
     told = start_all(
@@ -663,7 +720,7 @@
             lse[5:8, :] = jnp.zeros((3, 256), f32)
         share = weight[b : b + 1, :]
         local = mixes[b] * (jnp.exp(stats[b, 0:1] - total) * share)
-        local = local - found[b].astype(f32).T * share
+        local = local - found_t[b] * share
         outgoing[b] = local.T.astype(bf16)
         if b:
             copy = remote(
@@ -680,7 +737,7 @@
         copy.wait_send()
 
 
-def head(pred_all, table, table_t, row_of, weight, found):
+def head(pred_all, table, table_t, weight, found):
     dma, vmem = pltpu.SemaphoreType.DMA, pltpu.VMEM
     return pl.pallas_call(
         head_kernel,
@@ -688,10 +745,10 @@
             jax.ShapeDtypeStruct((256, EMBED_WIDTH), f32),
             jax.ShapeDtypeStruct((8, 256), f32),
         ],
-        in_specs=[VMEM] * 6,
+        in_specs=[VMEM] * 5,
         out_specs=[VMEM] * 2,
         scratch_shapes=[
-            vmem((table_t.shape[0], 256), f32),
+            vmem((4, EMBED_WIDTH, 256), f32),
             vmem((4, 8, 256), f32),
             vmem((3, 4, 8, 256), f32),
             vmem((4, 256, EMBED_WIDTH), bf16),
@@ -701,7 +758,7 @@
         compiler_params=pltpu.CompilerParams(
             collective_id=5, has_side_effects=True, vmem_limit_bytes=60 * 2**20
         ),
-    )(pred_all, table, table_t, row_of, weight, found)
+    )(pred_all, table, table_t, weight, found)
 
 
 def gelu_slope(u):
@@ -717,7 +774,7 @@
     normed_two, final_norm, up_proj, q, k, k_t, values, log_total, keep,
     small, attn, out_w, up_hbm, down_hbm, vecs,
     grad_pred_low, down_left, up_left, out_left, small_left, final_left, qkv_left, grad_up, grad_clean, sums,
-    up_w, down_w, carried, folded, mix_out, mix_in, grad_k, grad_v, n_out, n_in, f_out, f_in,
+    up_w, down_w, carried, folded, mix_out, mix_in, grad_k, grad_v, n_out, n_in, f_out, f_in, seen,
     w_sem, m_send, m_recv, n_send, n_recv, c_send, c_recv,
 ):
     v = lax.axis_index("vocab")
@@ -728,6 +785,7 @@
             copy = pltpu.make_async_copy(src.at[j], dst.at[j], w_sem.at[2 * j + i])
             copy.start()
             loads.append(copy)
+    seen[...] = jnp.broadcast_to(keep[...], seen.shape)
     greet(partners)
 
     def turned(value):
@@ -788,7 +846,7 @@
             grad_mix = grad_block[:, h * HDIM : (h + 1) * HDIM]
             asked = q[h, rows, :]
             scores = matmul_nt(k[h], asked)
-            scores = jnp.where(keep[...] > 0.0, scores, -1000000000.0)
+            scores = jnp.where(seen[...] > 0.0, scores, -1000000000.0)
             probs = jnp.exp(scores - log_total[3 * b + h : 3 * b + h + 1, :])
             grad_probs = matmul_nt(values[h], grad_mix)
             inner = jnp.sum(probs * grad_probs, 0, keepdims=True)
@@ -867,6 +925,7 @@
             vmem((2, n, D), bf16),
             vmem((n, D), bf16),
             vmem((n, D), bf16),
+            vmem((4 * n, n), f32),
             dma((8,)),
         ]
         + [dma((3,))] * 6,
@@ -1279,8 +1338,23 @@
     )(*operands)
 
 
-def slot_kernel(kind, unit, column, summed, w, m1, m2, w_out, m1_out, m2_out):
+def slot_kernel(
+    kind, unit, column, summed, table_grad, sums, w, m1, m2, tw, t1, t2,
+    w_out, m1_out, m2_out, tw_out, t1_out, t2_out, loss, norm,
+):
     per_unit = UNIT // LANES
+
+    def once():
+        g = table_grad[:, 0 : tw.shape[1]]
+        tw_out[...], t1_out[...], t2_out[...] = adamw(tw[...], g, t1[...], t2[...])
+        row = sums[10:11, :]
+        lane = lax.broadcasted_iota(jnp.int32, row.shape, 1)
+        square, cross, length, count = [jnp.sum(jnp.where(lane == i, row, 0.0)) for i in range(4)]
+        loss[0] = (0.5 * square + cross) * count
+        loss[1] = count
+        norm[0] = 0.5 * length
+
+    pl.when(pl.program_id(0) == 0)(once)
     for b in range(per_unit):
         j = pl.program_id(0) * per_unit + b
         first = jnp.where(kind[j] == 2, per_unit, column[j])
@@ -1295,21 +1369,29 @@
             )
 
 
-def slot_update(kind, unit, column, summed, slots, first, second):
+def slot_update(kind, unit, column, summed, table_grad, sums, slots, first, second, *table):
     rows = slots.shape[0]
     plain_spec = pl.BlockSpec((rows, UNIT), lambda j, k, u, c: (0, j))
+
+    def whole(value):
+        return pl.BlockSpec(value.shape, lambda j, k, u, c: (0,) * len(value.shape))
+
     return pl.pallas_call(
         slot_kernel,
         grid_spec=pltpu.PrefetchScalarGridSpec(
             num_scalar_prefetch=3,
             grid=(CAP // UNIT,),
-            in_specs=[pl.BlockSpec(summed.shape, lambda j, k, u, c: (0, 0, 0))] + [plain_spec] * 3,
-            out_specs=[plain_spec] * 3,
+            in_specs=[whole(summed), whole(table_grad), whole(sums)]
+            + [plain_spec] * 3
+            + [whole(value) for value in table],
+            out_specs=[plain_spec] * 3 + [whole(value) for value in table] + [SMEM] * 2,
         ),
-        out_shape=[jax.ShapeDtypeStruct(slots.shape, f32)] * 3,
+        out_shape=[jax.ShapeDtypeStruct(slots.shape, f32)] * 3
+        + [jax.ShapeDtypeStruct(table[0].shape, f32)] * 3
+        + [jax.ShapeDtypeStruct((2,), f32), jax.ShapeDtypeStruct((1,), f32)],
         cost_estimate=pl.CostEstimate(flops=0, bytes_accessed=28 * rows * CAP, transcendentals=0),
-        compiler_params=pltpu.CompilerParams(vmem_limit_bytes=40 * 2**20),
-    )(kind, unit, column, summed, slots, first, second)
+        compiler_params=pltpu.CompilerParams(vmem_limit_bytes=60 * 2**20),
+    )(kind, unit, column, summed, table_grad, sums, slots, first, second, *table)
 
 
 def per_device(
@@ -1337,46 +1419,24 @@
         payload, table_home, row_of, safe_row, keep_rows, keep_column, valid_column, count_tile,
         kind, unit, column,
     ) = prepare(owners, token_ids, pad_mask, table_own, mat_slots)
-    w_up, w_down, w_small, w_attn, w_out, table_low, row_weight, twice = spread(
-        owners, payload, count_tile, keep_rows, keep_column, table_home
+    w_up, w_down, w_small, w_attn, w_out, table_low, row_weight, twice, places, levels = spread(
+        owners, timesteps, payload, count_tile, keep_rows, keep_column, table_home
     )
     table_low = table_low.reshape(EMBED_WIDTH, vocab_rows)
     table_t = table_low.T
     looked = table_t.at[safe_row[0]].get(mode="promise_in_bounds").reshape(4, tokens, EMBED_WIDTH)
-    own_places = (v * tokens + jnp.arange(tokens)).astype(f32)
-    step_val = timesteps[0].astype(f32)
-    signal_level = 1.0 - jnp.sqrt(step_val / DIFF + 0.0001)
-    levels = jnp.concatenate(
-        [
-            jnp.full((1, EMBED_WIDTH), jnp.sqrt(signal_level)),
-            jnp.full((1, EMBED_WIDTH), jnp.sqrt(1.0 - signal_level)),
-            waves(step_val[None], EMBED_WIDTH),
-            jnp.zeros((5, EMBED_WIDTH), f32),
-        ]
-    )
     vecs = vec_params.reshape(10, D)
     (
         found_rows, clean_emb, inputs, hidden, normed_all, q_h, k_h, k_t, v_h, log_total, mixed_own, middle,
         normed_two, up_proj, active, hidden_two, final_norm, predicted, pred_all,
     ) = forward(
-        looked,
-        valid_column,
-        noise_draw[0],
-        levels,
-        waves(own_places, D),
-        w_small,
-        w_attn,
-        w_out,
-        w_up,
-        w_down,
-        vecs,
-        keep_column,
+        looked, valid_column, levels, places, vecs, keep_column,
+        noise_draw[0], w_small, w_attn, w_out, w_up, w_down,
     )
     grad_pred, head_stats = head(
         pred_all,
         table_low,
         table_t,
-        row_of,
         row_weight,
         found_rows,
     )
@@ -1414,27 +1474,20 @@
         row_of,
         sums,
     )
+    (
+        new_slots, slot_first_new, slot_second_new, new_table, table_first_new, table_second_new, loss_pair, emb_norm,
+    ) = slot_update(
+        kind, unit, column, summed, table_grad, tile_sum, mat_slots, slot_first, slot_second,
+        table_own, table_first_moment.T, table_second_moment.T,
+    )
     tile_sum = tile_sum.reshape(16 * UNIT)
     vec_share = vec_first.shape[0]
     own_grad = lax.dynamic_slice_in_dim(tile_sum, v * vec_share, vec_share)
     own_vecs = lax.dynamic_slice_in_dim(vec_params, v * vec_share, vec_share)
-    vec_len = vec_params.shape[0]
-    count_all = tile_sum[vec_len + 3]
-    square = tile_sum[vec_len] * (0.5 * count_all)
-    cross_sum = tile_sum[vec_len + 1] * count_all
-    emb_norm = tile_sum[vec_len + 2] * 0.5
-
-    new_slots, slot_first_new, slot_second_new = slot_update(
-        kind, unit, column, summed, mat_slots, slot_first, slot_second
-    )
-    new_table, table_first_new, table_second_new = adamw(
-        table_own, table_grad[:, :vocab_rows], table_first_moment.T, table_second_moment.T
-    )
     new_vecs, vec_first_new, vec_second_new = adamw(own_vecs, own_grad, vec_first, vec_second)
-    loss_pair = jnp.stack([square + cross_sum, count_all])
     return (
         loss_pair,
-        emb_norm,
+        emb_norm[0],
         new_table.T,
         table_first_new.T,
         table_second_new.T,

time: 442 us -> 422 us (0.955)
  local copies, waits for them, and re-layouts: 27.1 us -> 8.37 us
  Pallas kernels: 398 us -> 407 us
  other arithmetic: 6.54 us -> 0.72 us
    unnamed x54 -> x12, local copies, waits for them, and re-layouts: 17.3 us -> 0.04 us
    pallas_call x1, Pallas kernels: 114 us -> 120 us  [spread(): pl.pallas_call(spread_kernel, out_shape=[shape(4, D, UNIT), shape(4, D, U...]
    pallas_call x1, Pallas kernels: 4.95 us -> 10 us  [slot_update(): pl.pallas_call(slot_kernel, grid_spec=pltpu.PrefetchScalarGridSpec(num_sc...]
where the time goes in v5:
time: 422 us; the launch traced here: 418 us
  Pallas kernels  407 us (96%)
  local copies, waits for them, and re-layouts  8.37 us (2%)
    pallas_call x1, Pallas kernels, reduce_grads(): pl.pallas_call(grads_kernel, out_shape=[jax.ShapeDtypeStruct((8, low, UNI...  146 us
    pallas_call x1, Pallas kernels, spread(): pl.pallas_call(spread_kernel, out_shape=[shape(4, D, UNIT), shape(4, D, U...  120 us
    pallas_call x1, Pallas kernels, forward(): pl.pallas_call(forward_kernel, out_shape=[shape(bf16, 4, n, EMBED_WIDTH),...  46.8 us
    pallas_call x1, Pallas kernels, backward(): pl.pallas_call(backward_kernel, out_shape=[shape(bf16, n, EMBED_WIDTH)] +...  45.6 us
    pallas_call x1, Pallas kernels, head(): pl.pallas_call(head_kernel, out_shape=[jax.ShapeDtypeStruct((256, EMBED_W...  34.3 us
    pallas_call x1, Pallas kernels, slot_update(): pl.pallas_call(slot_kernel, grid_spec=pltpu.PrefetchScalarGridSpec(num_sc...  10 us

profile of v5, /device:TPU:0, one launch (start us, length us, event | category | flops | bytes accessed | tf_op | source)
XLA Modules:
  0.0 417.8 jit_solution(476306668758417183)
XLA Ops:
  0.6 4.5 %shard_map.221 = (bf16[8,96,896]{2,1,0:T(8,128)(2,1)}, bf16[16,7632]{1,0:T(8,128)(2,1)}, s32[4,256]{1,0:T(4,128)}, s32[1,1024]{1,0:T(1,128)}, f32[4,256]{1,0:T(4...) custom-call(s32[9]{0:T(128)} %owners.5, ...), custom_call_target="tpu_custom_call" | custom-call | tf_op jit(solution)/shard_map/pallas_call | solution.py:215
  5.8 119.6 %shard_map.222 = (bf16[4,768,768]{2,1,0:T(8,128)(2,1)}, bf16[4,768,768]{2,1,0:T(8,128)(2,1)}, bf16[4,768,128]{2,1,0:T(8,128)(2,1)}, bf16[4,192,768]{2,1,0:T(8,12...) custom-call(s32[9]{0:T(128)} %owners.5, ...), custom_call_target="tpu_custom_call" | custom-call | tf_op jit(solution)/shard_map/pallas_call | solution.py:420
  125.4 0.0 copy-start.5
  125.4 3.2 copy.27
  128.7 0.0 copy-start
  128.7 0.0 copy-start.2
  128.7 0.0 copy-done.5
  128.8 4.5 %gather_fusion = bf16[1024,128]{1,0:T(8,128)(2,1)} fusion(bf16[7632,128]{1,0:T(8,128)(2,1)S(1)} %bitcast.19, s32[1024]{0:T(1024)S(1)} %broadcast_clamp_fusion), kind=kCustom, calls=%fused_computation | custom fusion | bytes 528384 | tf_op jit(solution)/shard_map/gather | solution.py:1427
  133.2 0.0 copy-done.2
  133.2 0.6 reshape.79.vecs
  133.9 46.8 %shard_map.223 = (bf16[4,256,128]{2,1,0:T(8,128)(2,1)}, f32[256,128]{1,0:T(8,128)}, bf16[256,256]{1,0:T(8,128)(2,1)}, f32[256,768]{1,0:T(8,128)}, bf16[4,256,768...) custom-call(bf16[4,256,128]{2,1,0:T(8,128)(2,1)} %bitcast.26, ...), custom_call_target="tpu_custom_call" | custom-call | tf_op jit(solution)/shard_map/pallas_call | solution.py:608
  180.6 0.0 copy-done
  180.6 34.3 %shard_map.224 = (f32[256,128]{1,0:T(8,128)}, f32[8,256]{1,0:T(8,128)}) custom-call(bf16[4,256,128]{2,1,0:T(8,128)(2,1)} %get-tuple-element.92.pred_all, bf16[128,7632]{1,0:T(8,128)(2,1)} %bitcast.23, bf16[7632,128]{1,0:T(8,128)(2,1)} %bitcast.20, f32[4,256]{1,0:T(4,128)} %get-tuple-element.93.weight, bf16[4,256,128]{2,1,0:T(8,128)(2,1)} %get-tuple-element.94.found), custom_call_target="tpu_custom_call" | custom-call | tf_op jit(solution)/shard_map/pallas_call | solution.py:742
  215.0 45.6 %shard_map.225 = (bf16[256,128]{1,0:T(8,128)(2,1)}, bf16[768,256]{1,0:T(8,128)(2,1)}, bf16[768,256]{1,0:T(8,128)(2,1)}, bf16[768,256]{1,0:T(8,128)(2,1)}, bf16[7...) custom-call(f32[256,128]{1,0:T(8,128)} %get-tuple-element.95.grad_pr, ...), custom_call_target="tpu_custom_call" | custom-call | tf_op jit(solution)/shard_map/pallas_call | solution.py:903
  260.6 146.1 %shard_map.226 = (s16[8,112,896]{2,1,0:T(8,128)(2,1)}, f32[16,7680]{1,0:T(8,128)}, f32[16,768]{1,0:T(8,128)}) custom-call(s32[9]{0:T(128)} %owners.5, bf16[4,192,256]{2,1,0:T(8,128)(2,1)} %bitcast.29, bf16[4,192,256]{2,1,0:T(8,128)(2,1)} %bitcast.30, bf16[4,192,256]{2,1,0:T(8,128)(2,1)} %bitcast.31, bf16[4,192,256]{2,1,0:T(8,128)(2,1)} %bitcast.32, ...), custom_call_target="tpu_custom_call" | custom-call | tf_op jit(solution)/shard_map/pallas_call | solution.py:1287
  406.7 0.0 copy-start.1
  406.7 0.0 copy-start.3
  406.7 0.0 copy-start.4
  406.7 10.0 %shard_map.227 = (f32[192,3072]{1,0:T(8,128)}, f32[192,3072]{1,0:T(8,128)}, f32[192,3072]{1,0:T(8,128)}, f32[16,7632]{1,0:T(8,128)}, f32[16,7632]{1,0:T(8,128)},...) custom-call(s32[24]{0:T(128)} %get-tuple-element.74.kind, s32[24]{0:T(128)} %get-tuple-element.75.unit, ...), custom_call_target="tpu_custom_call" | custom-call | bytes 16515072 | tf_op jit(solution)/shard_map/pallas_call | solution.py:1379
  416.8 0.0 copy-done.1
  416.8 0.0 copy-done.3
  416.8 0.0 copy-done.4
  416.8 0.7 multiply_subtract_fusion
  (3 shorter events, 0.0 us)
Async XLA Ops:
  125.4 3.3 copy-start.5
  128.7 51.9 %copy-start = (bf16[128,7632]{0,1:T(8,128)(2,1)}, bf16[128,7632]{0,1:T(8,128)(2,1)S(1)}, u32[]{:S(2)}) copy-start(bf16[128,7632]{0,1:T(8,128)(2,1)S(1)} %copy.27) | copy-start | bytes 5861380
  128.7 4.5 %copy-start.2 = (f32[7680]{0:T(1024)S(1)}, f32[7680]{0:T(1024)}, u32[]{:S(2)}) copy-start(f32[7680]{0:T(1024)} %param.25) | copy-start | bytes 92164
  406.7 10.1 %copy-start.1 = (f32[16,768]{1,0:T(8,128)S(1)}, f32[16,768]{1,0:T(8,128)}, u32[]{:S(2)}) copy-start(f32[16,768]{1,0:T(8,128)} %get-tuple-element.128.sums) | copy-start | bytes 147460
  406.7 10.1 %copy-start.3 = (f32[1920]{0:T(1024)S(1)}, f32[1920]{0:T(1024)}, u32[]{:S(2)}) copy-start(f32[1920]{0:T(1024)} %param.26) | copy-start | bytes 23044
  406.7 10.1 %copy-start.4 = (f32[1920]{0:T(1024)S(1)}, f32[1920]{0:T(1024)}, u32[]{:S(2)}) copy-start(f32[1920]{0:T(1024)} %param.27) | copy-start | bytes 23044

commit v6 on v5

--- a/solution.py
+++ b/solution.py
@@ -290,16 +290,18 @@
             store[at] = copy
         return copy
 
-    def start_class(c):
+    def own_slab(c):
         keeps[c] = pltpu.make_async_copy(homes[c], spot(c, z), local.at[c])
         keeps[c].start()
+        note(remote(homes[c], spot(c, z), (y_send, y_recv), (c, 0), (d ^ 1, v)), side, (c, 0))
+
+    def start_class(c):
         for k in (2, 1, 3):
             note(
                 remote(homes[c], spot(c, z), (z_send, z_recv), (c, k - 1), (d ^ (2 * k), v)),
                 line,
                 (c, k),
             )
-        note(remote(homes[c], spot(c, z), (y_send, y_recv), (c, 0), (d ^ 1, v)), side, (c, 0))
 
     def relay(c, then=()):
         for k in (2, 1, 3):
@@ -314,15 +316,15 @@
         note(remote(source, target, (x_send, x_recv), (c, k), (d, far)), chip, (c, k))
         landing[c].append(note(remote(source, target, (n_send, n_recv), (c, k), (d, near))))
 
-    def to_chip(c):
-        for k in (0, 2, 1, 3):
+    def to_chip(c, slabs=(2, 1, 3)):
+        for k in slabs:
             side[c, k].wait_recv()
             if k == 0:
                 keeps[c].wait()
             if c < 3:
                 slab = fulls[c].at[z ^ k, own_rows, :]
                 chip_slab(c, k, slab, slab)
-        if c == 3:
+        if c == 3 and slabs[-1] == 3:
             keep = pltpu.make_async_copy(attn.at[3], out.at[own_rows, :], local.at[5])
             keep.start()
             chip_slab(c, 0, attn.at[3], out.at[own_rows, :])
@@ -384,6 +386,10 @@
             store(fulls[c], (up_to, down_to, small_to)[c], c)
 
     start_class(0)
+    for c in range(5):
+        own_slab(c)
+    for c in range(3):
+        to_chip(c, (0,))
     relay(0, (1,))
     to_chip(0)
     relay(1, (2, 3))
@@ -391,7 +397,7 @@
     relay(2)
     relay(3, (4,))
     to_chip(2)
-    to_chip(3)
+    to_chip(3, (0, 2, 1, 3))
     store(attn, attn_to, 4)
     to_last(0)
     relay(4)
@@ -399,7 +405,7 @@
     to_last(1)
     to_last(2)
     to_last(3)
-    to_chip(4)
+    to_chip(4, (0, 2, 1, 3))
     store(table, table_to, 5)
     finish(1)
     finish(2)
@@ -472,7 +478,7 @@
     found, clean, inputs, hidden, normed_all, q, k, k_t, values, log_total, mixed, middle, normed_two,
     up_proj, active, hidden_two, final_norm, predicted, pred_all,
     noise, small, attn, out_w, up_w, down_w, found_in, values_t, mixed_out, mixed_in, seen,
-    w_sem, s_sem, e_send, e_recv, n_send, n_recv, m_send, m_recv, p_send, p_recv,
+    w_sem, s_sem, e_send, e_recv, n_send, n_recv, m_send, m_recv, p_send, p_recv, tables,
 ):
     v = lax.axis_index("vocab")
     partners = neighbours()
@@ -488,6 +494,8 @@
             copy = pltpu.make_async_copy(src.at[j], dst.at[j], w_sem.at[2 * j + i])
             copy.start()
             loads.append(copy)
+    for copy in tables:
+        copy.start()
     for b in range(4):
         found[b] = jnp.where(
             valid[256 * b : 256 * b + 256, :] > 0.0, looked[b].astype(f32), 0.0
@@ -598,60 +606,6 @@
         copy.wait_send()
 
 
-def forward(*operands):
-    dma, vmem = pltpu.SemaphoreType.DMA, pltpu.VMEM
-    n = 256
-
-    def shape(kind, *dims):
-        return jax.ShapeDtypeStruct(dims, kind)
-
-    return pl.pallas_call(
-        forward_kernel,
-        out_shape=[
-            shape(bf16, 4, n, EMBED_WIDTH),
-            shape(f32, n, EMBED_WIDTH),
-            shape(bf16, n, 2 * EMBED_WIDTH),
-            shape(f32, n, D),
-            shape(bf16, 4, n, D),
-            shape(bf16, 3, 4 * n, HDIM),
-            shape(bf16, 3, 4 * n, HDIM),
-            shape(bf16, QUARTER, 4 * n),
-            shape(bf16, 3, 4 * n, HDIM),
-            shape(f32, 16, n),
-            shape(bf16, n, D),
-            shape(f32, n, D),
-            shape(bf16, n, D),
-            shape(f32, 4, n, UNIT),
-            shape(bf16, 4, n, UNIT),
-            shape(f32, n, D),
-            shape(bf16, n, D),
-            shape(f32, n, EMBED_WIDTH),
-            shape(bf16, 4, n, EMBED_WIDTH),
-        ],
-        in_specs=[VMEM] * 6 + [ANY] * 6,
-        out_specs=[VMEM] * 19,
-        scratch_shapes=[
-            vmem((n, EMBED_WIDTH), bf16),
-            vmem((4, D, LANES), bf16),
-            vmem((4, QUARTER, UNIT), bf16),
-            vmem((D, UNIT), bf16),
-            vmem((4, D, UNIT), bf16),
-            vmem((4, D, UNIT), bf16),
-            vmem((3, n, EMBED_WIDTH), bf16),
-            vmem((QUARTER, 4 * n), bf16),
-            vmem((3, n, QUARTER), bf16),
-            vmem((4, n, QUARTER), bf16),
-            vmem((4 * n, n), f32),
-            dma((8,)),
-            dma((4,)),
-        ]
-        + [dma((3,))] * 8,
-        compiler_params=pltpu.CompilerParams(
-            collective_id=4, has_side_effects=True, vmem_limit_bytes=60 * 2**20
-        ),
-    )(*operands)
-
-
 STRIP = 768
 
 
@@ -665,7 +619,6 @@
     s_send, s_recv, g_send, g_recv,
 ):
     partners = neighbours()
-    greet(partners)
     rows = table_t.shape[0]
     full, rest = rows // STRIP, rows % STRIP
     mixes = []
@@ -737,30 +690,6 @@
         copy.wait_send()
 
 
-def head(pred_all, table, table_t, weight, found):
-    dma, vmem = pltpu.SemaphoreType.DMA, pltpu.VMEM
-    return pl.pallas_call(
-        head_kernel,
-        out_shape=[
-            jax.ShapeDtypeStruct((256, EMBED_WIDTH), f32),
-            jax.ShapeDtypeStruct((8, 256), f32),
-        ],
-        in_specs=[VMEM] * 5,
-        out_specs=[VMEM] * 2,
-        scratch_shapes=[
-            vmem((4, EMBED_WIDTH, 256), f32),
-            vmem((4, 8, 256), f32),
-            vmem((3, 4, 8, 256), f32),
-            vmem((4, 256, EMBED_WIDTH), bf16),
-            vmem((3, 256, EMBED_WIDTH), bf16),
-        ]
-        + [dma((3,))] * 4,
-        compiler_params=pltpu.CompilerParams(
-            collective_id=5, has_side_effects=True, vmem_limit_bytes=60 * 2**20
-        ),
-    )(pred_all, table, table_t, weight, found)
-
-
 def gelu_slope(u):
     inner = math.sqrt(2.0 / math.pi)
     bent = jnp.tanh(inner * (u + 0.044715 * (u * u * u)))
@@ -772,21 +701,13 @@
 def backward_kernel(
     grad_pred, clean, predicted, twice, levels, head_stats, hidden, middle, hidden_two,
     normed_two, final_norm, up_proj, q, k, k_t, values, log_total, keep,
-    small, attn, out_w, up_hbm, down_hbm, vecs,
+    small, attn, out_w, up_w, down_w, vecs,
     grad_pred_low, down_left, up_left, out_left, small_left, final_left, qkv_left, grad_up, grad_clean, sums,
-    up_w, down_w, carried, folded, mix_out, mix_in, grad_k, grad_v, n_out, n_in, f_out, f_in, seen,
-    w_sem, m_send, m_recv, n_send, n_recv, c_send, c_recv,
+    carried, folded, mix_out, mix_in, grad_k, grad_v, n_out, n_in, f_out, f_in, seen,
+    m_send, m_recv, n_send, n_recv, c_send, c_recv,
 ):
     v = lax.axis_index("vocab")
     partners = neighbours()
-    loads = []
-    for j in range(4):
-        for i, (src, dst) in enumerate(((down_hbm, down_w), (up_hbm, up_w))):
-            copy = pltpu.make_async_copy(src.at[j], dst.at[j], w_sem.at[2 * j + i])
-            copy.start()
-            loads.append(copy)
-    seen[...] = jnp.broadcast_to(keep[...], seen.shape)
-    greet(partners)
 
     def turned(value):
         return value.astype(f32).T.astype(bf16)
@@ -815,8 +736,6 @@
     up_left[...] = turned(normed_two[...])
     final_left[...] = turned(final_norm[...])
     for j in range(4):
-        loads[2 * j].wait()
-        loads[2 * j + 1].wait()
         slope = matmul_nn(low, down_w[j]) * gelu_slope(up_proj[j])
         grad_up[j] = slope.astype(bf16)
         sums[4 + j : 5 + j, :] = jnp.sum(grad_up[j].astype(f32), 0, keepdims=True)
@@ -893,16 +812,66 @@
         copy.wait_send()
 
 
-def backward(*operands):
+def step_kernel(
+    looked, valid, levels, places, vecs, keep, weight, twice,
+    noise_hbm, small_hbm, attn_hbm, out_hbm, up_hbm, down_hbm, table_hbm, table_t_hbm,
+    inputs, normed_all, mixed, active, pred_all, lse, grad_pred_low, down_left, up_left, out_left, small_left,
+    final_left, qkv_left, grad_up, grad_clean, sums,
+    found, clean, hidden, q, k, k_t, values, log_total, middle, normed_two, up_proj, hidden_two, final_norm,
+    predicted, grad_pred, noise, small, attn, out_w, up_w, down_w, found_in, values_t, mixed_out, mixed_in, seen,
+    table, table_t, found_t, stats, gathered, outgoing, incoming,
+    carried, folded, mix_out, mix_in, grad_k, grad_v, n_out, n_in, f_out, f_in,
+    w_sem, s_sem, t_sem,
+    e_send, e_recv, n_send, n_recv, m_send, m_recv, p_send, p_recv, h_send, h_recv, g_send, g_recv,
+    i_send, i_recv, j_send, j_recv, c_send, c_recv,
+):
+    tables = [
+        pltpu.make_async_copy(table_hbm, table, t_sem.at[0]),
+        pltpu.make_async_copy(table_t_hbm, table_t, t_sem.at[1]),
+    ]
+    forward_kernel(
+        looked, valid, levels, places, vecs, keep, noise_hbm, small_hbm, attn_hbm, out_hbm, up_hbm, down_hbm,
+        found, clean, inputs, hidden, normed_all, q, k, k_t, values, log_total, mixed, middle, normed_two,
+        up_proj, active, hidden_two, final_norm, predicted, pred_all,
+        noise, small, attn, out_w, up_w, down_w, found_in, values_t, mixed_out, mixed_in, seen,
+        w_sem, s_sem, e_send, e_recv, n_send, n_recv, m_send, m_recv, p_send, p_recv, tables,
+    )
+    for copy in tables:
+        copy.wait()
+    head_kernel(
+        pred_all, table, table_t, weight, found,
+        grad_pred, lse, found_t, stats, gathered, outgoing, incoming,
+        h_send, h_recv, g_send, g_recv,
+    )
+    backward_kernel(
+        grad_pred, clean, predicted, twice, levels, lse, hidden, middle, hidden_two,
+        normed_two, final_norm, up_proj, q, k, k_t, values, log_total, keep,
+        small, attn, out_w, up_w, down_w, vecs,
+        grad_pred_low, down_left, up_left, out_left, small_left, final_left, qkv_left, grad_up, grad_clean, sums,
+        carried, folded, mix_out, mix_in, grad_k, grad_v, n_out, n_in, f_out, f_in, seen,
+        i_send, i_recv, j_send, j_recv, c_send, c_recv,
+    )
+
+
+def step(*operands):
     dma, vmem = pltpu.SemaphoreType.DMA, pltpu.VMEM
     n = 256
+    table, table_t = operands[-2:]
 
     def shape(kind, *dims):
         return jax.ShapeDtypeStruct(dims, kind)
 
     return pl.pallas_call(
-        backward_kernel,
-        out_shape=[shape(bf16, n, EMBED_WIDTH)]
+        step_kernel,
+        out_shape=[
+            shape(bf16, n, 2 * EMBED_WIDTH),
+            shape(bf16, 4, n, D),
+            shape(bf16, n, D),
+            shape(bf16, 4, n, UNIT),
+            shape(bf16, 4, n, EMBED_WIDTH),
+            shape(f32, 8, n),
+            shape(bf16, n, EMBED_WIDTH),
+        ]
         + [shape(bf16, D, n)] * 5
         + [
             shape(bf16, 3, QUARTER, 4 * n),
@@ -910,11 +879,42 @@
             shape(bf16, 4, n, EMBED_WIDTH),
             shape(f32, 16, UNIT),
         ],
-        in_specs=[VMEM] * 21 + [ANY] * 2 + [VMEM],
-        out_specs=[VMEM] * 10,
+        in_specs=[VMEM] * 8 + [ANY] * 8,
+        out_specs=[VMEM] * 16,
         scratch_shapes=[
+            vmem((4, n, EMBED_WIDTH), bf16),
+            vmem((n, EMBED_WIDTH), f32),
+            vmem((n, D), f32),
+            vmem((3, 4 * n, HDIM), bf16),
+            vmem((3, 4 * n, HDIM), bf16),
+            vmem((QUARTER, 4 * n), bf16),
+            vmem((3, 4 * n, HDIM), bf16),
+            vmem((16, n), f32),
+            vmem((n, D), f32),
+            vmem((n, D), bf16),
+            vmem((4, n, UNIT), f32),
+            vmem((n, D), f32),
+            vmem((n, D), bf16),
+            vmem((n, EMBED_WIDTH), f32),
+            vmem((n, EMBED_WIDTH), f32),
+            vmem((n, EMBED_WIDTH), bf16),
+            vmem((4, D, LANES), bf16),
+            vmem((4, QUARTER, UNIT), bf16),
+            vmem((D, UNIT), bf16),
             vmem((4, D, UNIT), bf16),
             vmem((4, D, UNIT), bf16),
+            vmem((3, n, EMBED_WIDTH), bf16),
+            vmem((QUARTER, 4 * n), bf16),
+            vmem((3, n, QUARTER), bf16),
+            vmem((4, n, QUARTER), bf16),
+            vmem((4 * n, n), f32),
+            vmem(table.shape, bf16),
+            vmem(table_t.shape, bf16),
+            vmem((4, EMBED_WIDTH, n), f32),
+            vmem((4, 8, n), f32),
+            vmem((3, 4, 8, n), f32),
+            vmem((4, n, EMBED_WIDTH), bf16),
+            vmem((3, n, EMBED_WIDTH), bf16),
             vmem((n, D), f32),
             vmem((n, D), f32),
             vmem((4, n, QUARTER), bf16),
@@ -925,12 +925,13 @@
             vmem((2, n, D), bf16),
             vmem((n, D), bf16),
             vmem((n, D), bf16),
-            vmem((4 * n, n), f32),
             dma((8,)),
+            dma((4,)),
+            dma((2,)),
         ]
-        + [dma((3,))] * 6,
+        + [dma((3,))] * 18,
         compiler_params=pltpu.CompilerParams(
-            collective_id=6, has_side_effects=True, vmem_limit_bytes=60 * 2**20
+            collective_id=4, has_side_effects=True, vmem_limit_bytes=60 * 2**20
         ),
     )(*operands)
 
@@ -993,16 +994,34 @@
 
 
 def grads_kernel(
-    owners, down_left, up_left, out_left, small_left, final_left, qkv_left,
-    active, grad_up, mixed, inputs, grad_pred, normed, pred_all, grad_clean, table_t, lse, weight, row_of, tile,
+    owners, inputs, grad_pred, pred_all, grad_clean, lse, weight, row_of, tile,
+    out_left_hbm, mixed_hbm, down_left_hbm, active_hbm, qkv_left_hbm, normed_hbm, table_t_hbm, up_left_hbm,
+    grad_up_hbm, small_left_hbm, final_left_hbm,
     summed, table_sum, tile_sum,
+    out_left, mixed, down_left, active, qkv_left, normed, table_t, up_left, grad_up, small_left, final_left,
     home, small_home, outgoing, cs, cr, xs, xr, ys, yr, zs, zr, part, half,
     small_cs, small_cr, small_xs, small_xr, small_ys, small_yr, small_zs, small_zr, small_half,
     table, pred_t, clean_t, ts, tr, tzs, tzr, tile_at, tile_from,
-    c_send, c_recv, x_send, x_recv, y_send, y_recv, z_send, z_recv, t_send, t_recv, a_send, a_recv, local,
+    c_send, c_recv, x_send, x_recv, y_send, y_recv, z_send, z_recv, t_send, t_recv, a_send, a_recv, local, l_sem,
 ):
     z, y, d, v = place()
     far, near = v ^ 2, v ^ 1
+    pairs = (
+        (out_left_hbm, out_left), (mixed_hbm, mixed), (down_left_hbm, down_left), (active_hbm, active),
+        (qkv_left_hbm, qkv_left), (normed_hbm, normed), (table_t_hbm, table_t), (up_left_hbm, up_left),
+        (grad_up_hbm, grad_up), (small_left_hbm, small_left), (final_left_hbm, final_left),
+    )
+    loads = [pltpu.make_async_copy(src, dst, l_sem.at[i]) for i, (src, dst) in enumerate(pairs)]
+    for copy in loads:
+        copy.start()
+    loaded = set()
+
+    def need(*which):
+        for i in which:
+            if i not in loaded:
+                loads[i].wait()
+                loaded.add(i)
+
     greet([(d ^ m, v) for m in TRADE_MASKS] + [(d, far), (d, near)])
     sent = []
 
@@ -1013,6 +1032,7 @@
         return copy
 
     def product(n, who):
+        need(*((0, 1) if n == 0 else (2, 3) if n < 5 else (7, 8)))
         if n == 0:
             return matmul_nn(out_left[who], mixed[...])
         if n < 5:
@@ -1061,6 +1081,7 @@
         put(home.at[group], total)
 
     def small_product(who):
+        need(9, 10)
         return jnp.concatenate(
             [matmul_nn(small_left[who], inputs[...]), matmul_nn(final_left[who], grad_pred[...])], 1
         )
@@ -1113,6 +1134,7 @@
     vocab_rows = table_t.shape[0]
 
     def table_strip(lo, size):
+        need(6)
         total = jnp.zeros((EMBED_WIDTH, size), f32)
         for b in range(4):
             logits = matmul_nt(table_t[lo : lo + size, :], pred_all[b])
@@ -1189,18 +1211,19 @@
         )
 
     def token_products():
+        need(4, 5)
         for u in range(3):
             halves(
                 u,
                 sum(matmul_nn(qkv_left[u, :, 256 * b : 256 * b + 256], normed[b]) for b in range(4)),
             )
 
-    turn_tokens()
-    token_products()
     to_core(0)
     to_core(1)
     to_chip(0)
+    token_products()
     tile_send(0)
+    turn_tokens()
     table_strip(*table_strips[0])
     table_strip(*table_strips[1])
     to_core(2)
@@ -1291,9 +1314,10 @@
             jax.ShapeDtypeStruct((16, table_cols), f32),
             jax.ShapeDtypeStruct((16, UNIT), f32),
         ],
-        in_specs=[SMEM] + [VMEM] * 19,
+        in_specs=[SMEM] + [VMEM] * 8 + [ANY] * 11,
         out_specs=[VMEM] * 3,
-        scratch_shapes=[
+        scratch_shapes=[vmem(value.shape, bf16) for value in operands[9:]]
+        + [
             vmem((3, low, UNIT), I16),
             vmem((low, LANES), I16),
             vmem((8, low, UNIT + LANES), I16),
@@ -1331,7 +1355,7 @@
         + [dma((18,))] * 2
         + [dma((5,))] * 2
         + [dma((7,))] * 2
-        + [dma],
+        + [dma, dma((11,))],
         compiler_params=pltpu.CompilerParams(
             collective_id=2, has_side_effects=True, vmem_limit_bytes=60 * 2**20
         ),
@@ -1427,52 +1451,20 @@
     looked = table_t.at[safe_row[0]].get(mode="promise_in_bounds").reshape(4, tokens, EMBED_WIDTH)
     vecs = vec_params.reshape(10, D)
     (
-        found_rows, clean_emb, inputs, hidden, normed_all, q_h, k_h, k_t, v_h, log_total, mixed_own, middle,
-        normed_two, up_proj, active, hidden_two, final_norm, predicted, pred_all,
-    ) = forward(
-        looked, valid_column, levels, places, vecs, keep_column,
-        noise_draw[0], w_small, w_attn, w_out, w_up, w_down,
-    )
-    grad_pred, head_stats = head(
-        pred_all,
-        table_low,
-        table_t,
-        row_weight,
-        found_rows,
-    )
-    (
-        grad_pred_low, down_left, up_left, out_left, small_left, final_left, qkv_left, grad_up, grad_clean, sums,
-    ) = backward(
-        grad_pred, clean_emb, predicted, twice, levels, head_stats,
-        hidden, middle, hidden_two, normed_two, final_norm, up_proj,
-        q_h, k_h, k_t, v_h, log_total, keep_column,
-        w_small, w_attn, w_out, w_up, w_down, vecs,
+        inputs, normed_all, mixed_own, active, pred_all, head_stats, grad_pred_low, down_left, up_left, out_left,
+        small_left, final_left, qkv_left, grad_up, grad_clean, sums,
+    ) = step(
+        looked, valid_column, levels, places, vecs, keep_column, row_weight, twice,
+        noise_draw[0], w_small, w_attn, w_out, w_up, w_down, table_low, table_t,
     )
 
     def left(value):
         return value.reshape(4, QUARTER, tokens)
 
     summed, table_grad, tile_sum = reduce_grads(
-        owners,
-        left(down_left),
-        left(up_left),
-        left(out_left),
-        left(small_left),
-        left(final_left),
-        qkv_left,
-        active,
-        grad_up,
-        mixed_own,
-        inputs,
-        grad_pred_low,
-        normed_all,
-        pred_all,
-        grad_clean,
-        table_t,
-        head_stats,
-        row_weight,
-        row_of,
-        sums,
+        owners, inputs, grad_pred_low, pred_all, grad_clean, head_stats, row_weight, row_of, sums,
+        left(out_left), mixed_own, left(down_left), active, qkv_left, normed_all, table_t, left(up_left),
+        grad_up, left(small_left), left(final_left),
     )
     (
         new_slots, slot_first_new, slot_second_new, new_table, table_first_new, table_second_new, loss_pair, emb_norm,

time: 422 us -> 399 us (0.945)
  Pallas kernels: 407 us -> 383 us
    pallas_call x3 -> x1, Pallas kernels: 127 us -> 112 us  [step(): pl.pallas_call(step_kernel, out_shape=[shape(bf16, n, 2 * EMBED_WIDTH), s...]
    pallas_call x1, Pallas kernels: 146 us -> 135 us  [reduce_grads(): pl.pallas_call(grads_kernel, out_shape=[jax.ShapeDtypeStruct((8, low, UNI...]
where the time goes in v6:
time: 399 us; the launch traced here: 394 us
  Pallas kernels  383 us (96%)
  local copies, waits for them, and re-layouts  8.37 us (2%)
    pallas_call x1, Pallas kernels, reduce_grads(): pl.pallas_call(grads_kernel, out_shape=[jax.ShapeDtypeStruct((8, low, UNI...  135 us
    pallas_call x1, Pallas kernels, spread(): pl.pallas_call(spread_kernel, out_shape=[shape(4, D, UNIT), shape(4, D, U...  122 us
    pallas_call x1, Pallas kernels, step(): pl.pallas_call(step_kernel, out_shape=[shape(bf16, n, 2 * EMBED_WIDTH), s...  112 us
    pallas_call x1, Pallas kernels, slot_update(): pl.pallas_call(slot_kernel, grid_spec=pltpu.PrefetchScalarGridSpec(num_sc...  10 us

profile of v6, /device:TPU:0, one launch (start us, length us, event | category | flops | bytes accessed | tf_op | source)
XLA Modules:
  0.0 394.0 jit_solution(10398690584249212983)
XLA Ops:
  0.6 4.4 %shard_map.221 = (bf16[8,96,896]{2,1,0:T(8,128)(2,1)}, bf16[16,7632]{1,0:T(8,128)(2,1)}, s32[4,256]{1,0:T(4,128)}, s32[1,1024]{1,0:T(1,128)}, f32[4,256]{1,0:T(4...) custom-call(s32[9]{0:T(128)} %owners.5, ...), custom_call_target="tpu_custom_call" | custom-call | tf_op jit(solution)/shard_map/pallas_call | solution.py:215
  5.7 121.8 %shard_map.222 = (bf16[4,768,768]{2,1,0:T(8,128)(2,1)}, bf16[4,768,768]{2,1,0:T(8,128)(2,1)}, bf16[4,768,128]{2,1,0:T(8,128)(2,1)}, bf16[4,192,768]{2,1,0:T(8,12...) custom-call(s32[9]{0:T(128)} %owners.5, ...), custom_call_target="tpu_custom_call" | custom-call | tf_op jit(solution)/shard_map/pallas_call | solution.py:426
  127.5 0.0 copy-start.5
  127.5 3.2 copy.27
  130.8 0.0 copy-start
  130.8 0.0 copy-start.2
  130.8 0.0 copy-done.5
  130.8 4.5 %gather_fusion = bf16[1024,128]{1,0:T(8,128)(2,1)} fusion(bf16[7632,128]{1,0:T(8,128)(2,1)S(1)} %bitcast.19, s32[1024]{0:T(1024)S(1)} %broadcast_clamp_fusion), kind=kCustom, calls=%fused_computation | custom fusion | bytes 528384 | tf_op jit(solution)/shard_map/gather | solution.py:1451
  135.3 0.0 copy-done.2
  135.3 0.6 reshape.79.vecs
  135.9 0.0 copy-done
  135.9 111.7 %shard_map.223 = (bf16[256,256]{1,0:T(8,128)(2,1)}, bf16[4,256,768]{2,1,0:T(8,128)(2,1)}, bf16[256,768]{1,0:T(8,128)(2,1)}, bf16[4,256,768]{2,1,0:T(8,128)(2,1)}...) custom-call(bf16[4,256,128]{2,1,0:T(8,128)(2,1)} %bitcast.26, ...), custom_call_target="tpu_custom_call" | custom-call | tf_op jit(solution)/shard_map/pallas_call | solution.py:864
  247.7 135.3 %shard_map.224 = (s16[8,112,896]{2,1,0:T(8,128)(2,1)}, f32[16,7680]{1,0:T(8,128)}, f32[16,768]{1,0:T(8,128)}) custom-call(s32[9]{0:T(128)} %owners.5, bf16[256,256]{1,0:T(8,128)(2,1)} %get-tuple-element.79.inputs, bf16[256,128]{1,0:T(8,128)(2,1)} %get-tuple-element.80.grad_pred, bf16[4,256,128]{2,1,0:T(8,128)(2,1)} %get-tuple-element.81.pred_all, ...), custom_call_target="tpu_custom_call" | custom-call | tf_op jit(solution)/shard_map/pallas_call | solution.py:1310
  383.0 0.0 copy-start.1
  383.0 0.0 copy-start.3
  383.0 0.0 copy-start.4
  383.0 10.0 %shard_map.225 = (f32[192,3072]{1,0:T(8,128)}, f32[192,3072]{1,0:T(8,128)}, f32[192,3072]{1,0:T(8,128)}, f32[16,7632]{1,0:T(8,128)}, f32[16,7632]{1,0:T(8,128)},...) custom-call(s32[24]{0:T(128)} %get-tuple-element.59.kind, s32[24]{0:T(128)} %get-tuple-element.60.unit, ...), custom_call_target="tpu_custom_call" | custom-call | bytes 16515072 | tf_op jit(solution)/shard_map/pallas_call | solution.py:1403
  393.0 0.0 copy-done.1
  393.1 0.0 copy-done.3
  393.1 0.0 copy-done.4
  393.1 0.7 multiply_subtract_fusion
  (3 shorter events, 0.0 us)
Async XLA Ops:
  127.5 3.3 copy-start.5
  130.8 5.2 %copy-start = (bf16[128,7632]{0,1:T(8,128)(2,1)}, bf16[128,7632]{0,1:T(8,128)(2,1)S(1)}, u32[]{:S(2)}) copy-start(bf16[128,7632]{0,1:T(8,128)(2,1)S(1)} %copy.27) | copy-start | bytes 5861380
  130.8 4.5 %copy-start.2 = (f32[7680]{0:T(1024)S(1)}, f32[7680]{0:T(1024)}, u32[]{:S(2)}) copy-start(f32[7680]{0:T(1024)} %param.25) | copy-start | bytes 92164
  383.0 10.1 %copy-start.1 = (f32[16,768]{1,0:T(8,128)S(1)}, f32[16,768]{1,0:T(8,128)}, u32[]{:S(2)}) copy-start(f32[16,768]{1,0:T(8,128)} %get-tuple-element.98.sums) | copy-start | bytes 147460
  383.0 10.1 %copy-start.3 = (f32[1920]{0:T(1024)S(1)}, f32[1920]{0:T(1024)}, u32[]{:S(2)}) copy-start(f32[1920]{0:T(1024)} %param.26) | copy-start | bytes 23044
  383.0 10.1 %copy-start.4 = (f32[1920]{0:T(1024)S(1)}, f32[1920]{0:T(1024)}, u32[]{:S(2)}) copy-start(f32[1920]{0:T(1024)} %param.27) | copy-start | bytes 23044

commit v7 on v6

--- a/solution.py
+++ b/solution.py
@@ -337,6 +337,8 @@
             slab = out.at[rows, :] if c == 3 else fulls[c].at[z ^ k, rows, :]
             landing[c].append(note(remote(slab, slab, (f_send, f_recv), (c, k), (d, near))))
 
+    own_slab(4)
+
     def angles(position, width, count):
         lane = lax.broadcasted_iota(jnp.int32, (count, width), 1).astype(f32)
         return position * jnp.exp(-math.log(10000.0) * lane / width)
@@ -386,7 +388,7 @@
             store(fulls[c], (up_to, down_to, small_to)[c], c)
 
     start_class(0)
-    for c in range(5):
+    for c in range(4):
         own_slab(c)
     for c in range(3):
         to_chip(c, (0,))

time: 399 us -> 402 us (level)
  the two profiles are of different devices: /device:TPU:0 before, /device:TPU:10 now
where the time goes in v7:
time: 402 us; the launch traced here: 398 us
  Pallas kernels  387 us (96%)
  local copies, waits for them, and re-layouts  8.37 us (2%)
    pallas_call x1, Pallas kernels, reduce_grads(): pl.pallas_call(grads_kernel, out_shape=[jax.ShapeDtypeStruct((8, low, UNI...  148 us
    pallas_call x1, Pallas kernels, spread(): pl.pallas_call(spread_kernel, out_shape=[shape(4, D, UNIT), shape(4, D, U...  112 us
    pallas_call x1, Pallas kernels, step(): pl.pallas_call(step_kernel, out_shape=[shape(bf16, n, 2 * EMBED_WIDTH), s...  112 us
    pallas_call x1, Pallas kernels, slot_update(): pl.pallas_call(slot_kernel, grid_spec=pltpu.PrefetchScalarGridSpec(num_sc...  10.1 us

profile of v7, /device:TPU:10, one launch (start us, length us, event | category | flops | bytes accessed | tf_op | source)
XLA Modules:
  0.0 397.8 jit_solution(13276804746733617408)
XLA Ops:
  0.6 4.4 %shard_map.221 = (bf16[8,96,896]{2,1,0:T(8,128)(2,1)}, bf16[16,7632]{1,0:T(8,128)(2,1)}, s32[4,256]{1,0:T(4,128)}, s32[1,1024]{1,0:T(1,128)}, f32[4,256]{1,0:T(4...) custom-call(s32[9]{0:T(128)} %owners.5, ...), custom_call_target="tpu_custom_call" | custom-call | tf_op jit(solution)/shard_map/pallas_call | solution.py:215
  5.7 112.4 %shard_map.222 = (bf16[4,768,768]{2,1,0:T(8,128)(2,1)}, bf16[4,768,768]{2,1,0:T(8,128)(2,1)}, bf16[4,768,128]{2,1,0:T(8,128)(2,1)}, bf16[4,192,768]{2,1,0:T(8,12...) custom-call(s32[9]{0:T(128)} %owners.5, ...), custom_call_target="tpu_custom_call" | custom-call | tf_op jit(solution)/shard_map/pallas_call | solution.py:428
  118.2 0.0 copy-start.5
  118.2 3.2 copy.27
  121.4 0.0 copy-start
  121.4 0.0 copy-start.2
  121.5 0.0 copy-done.5
  121.5 4.5 %gather_fusion = bf16[1024,128]{1,0:T(8,128)(2,1)} fusion(bf16[7632,128]{1,0:T(8,128)(2,1)S(1)} %bitcast.19, s32[1024]{0:T(1024)S(1)} %broadcast_clamp_fusion), kind=kCustom, calls=%fused_computation | custom fusion | bytes 528384 | tf_op jit(solution)/shard_map/gather | solution.py:1453
  126.0 0.0 copy-done.2
  126.0 0.6 reshape.79.vecs
  126.6 0.0 copy-done
  126.6 112.0 %shard_map.223 = (bf16[256,256]{1,0:T(8,128)(2,1)}, bf16[4,256,768]{2,1,0:T(8,128)(2,1)}, bf16[256,768]{1,0:T(8,128)(2,1)}, bf16[4,256,768]{2,1,0:T(8,128)(2,1)}...) custom-call(bf16[4,256,128]{2,1,0:T(8,128)(2,1)} %bitcast.26, ...), custom_call_target="tpu_custom_call" | custom-call | tf_op jit(solution)/shard_map/pallas_call | solution.py:866
  238.6 148.1 %shard_map.224 = (s16[8,112,896]{2,1,0:T(8,128)(2,1)}, f32[16,7680]{1,0:T(8,128)}, f32[16,768]{1,0:T(8,128)}) custom-call(s32[9]{0:T(128)} %owners.5, bf16[256,256]{1,0:T(8,128)(2,1)} %get-tuple-element.79.inputs, bf16[256,128]{1,0:T(8,128)(2,1)} %get-tuple-element.80.grad_pred, bf16[4,256,128]{2,1,0:T(8,128)(2,1)} %get-tuple-element.81.pred_all, ...), custom_call_target="tpu_custom_call" | custom-call | tf_op jit(solution)/shard_map/pallas_call | solution.py:1312
  386.8 0.0 copy-start.1
  386.8 0.0 copy-start.3
  386.8 0.0 copy-start.4
  386.8 10.1 %shard_map.225 = (f32[192,3072]{1,0:T(8,128)}, f32[192,3072]{1,0:T(8,128)}, f32[192,3072]{1,0:T(8,128)}, f32[16,7632]{1,0:T(8,128)}, f32[16,7632]{1,0:T(8,128)},...) custom-call(s32[24]{0:T(128)} %get-tuple-element.59.kind, s32[24]{0:T(128)} %get-tuple-element.60.unit, ...), custom_call_target="tpu_custom_call" | custom-call | bytes 16515072 | tf_op jit(solution)/shard_map/pallas_call | solution.py:1405
  396.9 0.0 copy-done.1
  396.9 0.0 copy-done.3
  396.9 0.0 copy-done.4
  396.9 0.7 multiply_subtract_fusion
  (3 shorter events, 0.0 us)
Async XLA Ops:
  118.2 3.3 copy-start.5
  121.4 5.2 %copy-start = (bf16[128,7632]{0,1:T(8,128)(2,1)}, bf16[128,7632]{0,1:T(8,128)(2,1)S(1)}, u32[]{:S(2)}) copy-start(bf16[128,7632]{0,1:T(8,128)(2,1)S(1)} %copy.27) | copy-start | bytes 5861380
  121.4 4.5 %copy-start.2 = (f32[7680]{0:T(1024)S(1)}, f32[7680]{0:T(1024)}, u32[]{:S(2)}) copy-start(f32[7680]{0:T(1024)} %param.25) | copy-start | bytes 92164
  386.8 10.1 %copy-start.1 = (f32[16,768]{1,0:T(8,128)S(1)}, f32[16,768]{1,0:T(8,128)}, u32[]{:S(2)}) copy-start(f32[16,768]{1,0:T(8,128)} %get-tuple-element.98.sums) | copy-start | bytes 147460
  386.8 10.1 %copy-start.3 = (f32[1920]{0:T(1024)S(1)}, f32[1920]{0:T(1024)}, u32[]{:S(2)}) copy-start(f32[1920]{0:T(1024)} %param.26) | copy-start | bytes 23044
  386.8 10.1 %copy-start.4 = (f32[1920]{0:T(1024)S(1)}, f32[1920]{0:T(1024)}, u32[]{:S(2)}) copy-start(f32[1920]{0:T(1024)} %param.27) | copy-start | bytes 23044
